TPU v7x, 32 devices: a whole 2x2x4 slice. The times are simulated.
32 devices in a mesh: box: 32 (over z, y, x, core).
Axes of the slice: x: 2, y: 2, z: 4, core: 2. Of those that a mesh axis runs over, the one named last changes fastest.
Arguments:
- sources: float32 [2048, 32768], P(None, 'box'), may hold values from -6 to 6
- leaf_basis: bfloat16 [64, 512, 256], P('box'), may hold values from -0.25 to 0.25
- stay_blocks: bfloat16 [6, 64, 256, 256], P(None, 'box'), may hold values from -0.25 to 0.25
- cross_blocks: bfloat16 [6, 64, 256, 256], P(None, 'box'), may hold values from -0.25 to 0.25
- out_basis: bfloat16 [64, 256, 512], P('box'), may hold values from -0.375 to 0.375
- near_blocks: bfloat16 [64, 768, 512], P('box'), may hold values from -0.21875 to 0.21875
Outputs:
- targets: float32 [2048, 32768], P(None, 'box')
All inputs are finite; a program needn't handle non-finite values.
Results may differ from a plain program's by a relative error of at most 0.014.
Values may be sent and summed in bfloat16 or wider, within the bound.
No kernel may reach another device: no remote copies, remote signals or barrier semaphores. Data moves between devices by JAX's collectives and lax.ppermute only.
A program may use at most 128 MiB of HBM per device.

v0:
```python
import jax
import jax.numpy as jnp
from jax import lax
from jax.sharding import PartitionSpec as P

B = 512
H = 128


def with_halo(cells, sides, width):
    for axis, dim in sides:
        count = lax.axis_size(axis)
        ends = count - 1
        head = lax.slice_in_dim(cells, 0, width, axis=dim)
        tail = lax.slice_in_dim(cells, cells.shape[dim] - width, cells.shape[dim], axis=dim)
        cells = jnp.concatenate(
            [
                lax.ppermute(tail, axis, [(i, (i + 1) % count) for i in range(ends)]),
                cells,
                lax.ppermute(head, axis, [((i + 1) % count, i) for i in range(ends)]),
            ],
            axis=dim,
        )
    return cells


def from_partner(shard, axis, apart):
    return lax.ppermute(shard, axis, [(i, i ^ 1 << apart) for i in range(lax.axis_size(axis))])


def near_terms(rounded, near_blocks):
    padded = with_halo(rounded, (("box", 1),), H)
    return [
        jnp.dot(
            padded[:, which * B : which * B + B + 2 * H],
            near_blocks[which],
            preferred_element_type=jnp.float32,
        )
        for which in range(2)
    ]


def per_device(sources, leaf_basis, stay_blocks, cross_blocks, out_basis, near_blocks):
    rounded = sources.astype(jnp.bfloat16)
    proxies = [
        jnp.dot(
            rounded[:, which * B : (which + 1) * B],
            leaf_basis[which],
            preferred_element_type=jnp.float32,
        ).astype(jnp.bfloat16)
        for which in range(2)
    ]
    first = jnp.dot(proxies[0], stay_blocks[0, 0], preferred_element_type=jnp.float32) + jnp.dot(
        proxies[1], cross_blocks[0, 1], preferred_element_type=jnp.float32
    )
    second = jnp.dot(proxies[1], stay_blocks[0, 1], preferred_element_type=jnp.float32) + jnp.dot(
        proxies[0], cross_blocks[0, 0], preferred_element_type=jnp.float32
    )
    proxies = [first.astype(jnp.bfloat16), second.astype(jnp.bfloat16)]
    depths = stay_blocks.shape[0]
    for depth_at in range(1, depths):
        other = from_partner(
            (proxies[0], proxies[1], cross_blocks[depth_at, 0], cross_blocks[depth_at, 1]),
            "box",
            depth_at - 1,
        )
        moved = (
            jnp.dot(other[0], other[2], preferred_element_type=jnp.float32),
            jnp.dot(other[1], other[3], preferred_element_type=jnp.float32),
        )
        proxies = [
            (
                jnp.dot(
                    proxies[which], stay_blocks[depth_at, which], preferred_element_type=jnp.float32
                )
                + moved[which]
            ).astype(jnp.bfloat16)
            for which in range(2)
        ]
    near_field = near_terms(rounded, near_blocks)
    columns = [
        jnp.dot(proxies[which], out_basis[which], preferred_element_type=jnp.float32)
        + near_field[which]
        for which in range(2)
    ]
    return jnp.concatenate(columns, axis=1)


def solution(mesh):
    in_specs = (
        P(None, "box"),
        P("box", None, None),
        P(None, "box", None, None),
        P(None, "box", None, None),
        P("box", None, None),
        P("box", None, None),
    )
    out_specs = P(None, "box")
    return jax.shard_map(
        per_device, mesh=mesh, in_specs=in_specs, out_specs=out_specs, check_vma=False
    )
```

profile of v0, /device:TPU:0, one launch (start us, length us, event | category | flops | bytes accessed | tf_op | source)
XLA Modules:
  0.0 292.4 jit_solution(16829210960975007276)
XLA Ops:
  0.0 4.1 %convert_element_type.45 = bf16[2048,1024]{1,0:T(8,128)(2,1)S(1)} convert(f32[2048,1024]{1,0:T(8,128)} %param.6) | non-fusion elementwise | flops 2097152 | bytes 12582912 | tf_op jit(solution)/shard_map/convert_element_type | solution.py:44
  4.1 0.7 convolution_convert_fusion
  4.9 0.7 convolution_convert_fusion.1
  5.6 1.4 copy-done.3
  7.4 1.0 copy-done.4
  8.8 0.5 collective-permute-start.11
  10.4 0.5 collective-permute-start.12
  11.5 0.4 fusion.55
  11.9 1.4 collective-permute-done.12
  13.3 0.4 fusion.13
  13.8 2.9 collective-permute-start.13
  17.2 2.0 collective-permute-start.14
  19.7 0.4 fusion.53
  20.2 45.7 %collective-permute-done.14 = bf16[256,256]{1,0:T(8,128)(2,1)S(1)} collective-permute-done((bf16[256,256]{1,0:T(8,128)(2,1)S(1)}, bf16[256,256]{1,0:T(8,128)(2,1)S(1)}, u32[]{:S(2)}, u32[]{:S(2)}) %collective-permute-start.14) | collective-permute-done | bytes 131104 | tf_op jit(solution)/shard_map/ppermute | solution.py:28
  65.9 0.4 fusion.14
  66.4 2.2 collective-permute-start.15
  69.0 1.6 collective-permute-start.4
  70.5 0.5 collective-permute-start.16
  71.0 1.5 collective-permute-start.5
  73.0 0.4 fusion.51
  73.4 43.9 %collective-permute-done.16 = bf16[256,256]{1,0:T(8,128)(2,1)S(1)} collective-permute-done((bf16[256,256]{1,0:T(8,128)(2,1)S(1)}, bf16[256,256]{1,0:T(8,128)(2,1)S(1)}, u32[]{:S(2)}, u32[]{:S(2)}) %collective-permute-start.16) | collective-permute-done | bytes 131104 | tf_op jit(solution)/shard_map/ppermute | solution.py:28
  117.3 0.4 fusion.15
  117.8 1.6 collective-permute-start.17
  119.8 1.0 collective-permute-start.6
  120.7 2.6 collective-permute-start.9
  123.3 1.1 collective-permute-start.7
  124.4 0.9 collective-permute-start.18
  125.8 0.4 fusion.49
  126.2 45.6 %collective-permute-done.18 = bf16[256,256]{1,0:T(8,128)(2,1)S(1)} collective-permute-done((bf16[256,256]{1,0:T(8,128)(2,1)S(1)}, bf16[256,256]{1,0:T(8,128)(2,1)S(1)}, u32[]{:S(2)}, u32[]{:S(2)}) %collective-permute-start.18) | collective-permute-done | bytes 131104 | tf_op jit(solution)/shard_map/ppermute | solution.py:28
  171.8 2.0 collective-permute-start.20
  173.8 0.4 fusion.16
  174.3 1.0 collective-permute-start.19
  175.2 0.4 fusion.10
  175.7 2.1 collective-permute-start.8
  177.8 1.1 fusion.76
  178.9 2.1 collective-permute-start.10
  181.0 1.8 fusion.34
  183.2 39.4 %collective-permute-done.20 = bf16[256,256]{1,0:T(8,128)(2,1)S(1)} collective-permute-done((bf16[256,256]{1,0:T(8,128)(2,1)S(1)}, bf16[256,256]{1,0:T(8,128)(2,1)S(1)}, u32[]{:S(2)}, u32[]{:S(2)}) %collective-permute-start.20) | collective-permute-done | bytes 131104 | tf_op jit(solution)/shard_map/ppermute | solution.py:28
  222.6 1.5 collective-permute-start.21
  224.0 21.2 %collective-permute-done.19 = bf16[2048,256]{1,0:T(8,128)(2,1)} collective-permute-done((bf16[2048,256]{1,0:T(8,128)(2,1)S(1)}, bf16[2048,256]{1,0:T(8,128)(2,1)}, u32[]{:S(2)}, u32[]{:S(2)}) %collective-permute-start.19) | collective-permute-done | bytes 1048608 | tf_op jit(solution)/shard_map/ppermute | solution.py:28
  245.3 5.0 %fusion.20 = f32[2048,512]{0,1:T(8,128)} fusion(f32[2048,256]{1,0:T(8,128)} %fusion.34, bf16[2048,256]{1,0:T(8,128)(2,1)} %collective-permute-done.19, bf16[256,256]{1,0:T(8,128)(2,1)S(1)} %collective-permute-done.20, bf16[2,256,512]{2,1,0:T(8,128)(2,1)} %param.10), kind=kOutput, calls=%fused_computation.37 | convolution fusion | flops 806354944 | bytes 7733248 | tf_op jit(solution)/shard_map/dot_general | solution.py:82
  250.3 15.3 %collective-permute-done.8 = bf16[2048,256]{1,0:T(8,128)(2,1)} collective-permute-done((bf16[2048,256]{1,0:T(8,128)(2,1)S(1)}, bf16[2048,256]{1,0:T(8,128)(2,1)}, u32[]{:S(2)}, u32[]{:S(2)}) %collective-permute-start.8) | collective-permute-done | bytes 1048608 | tf_op jit(solution)/shard_map/ppermute | solution.py:28
  265.6 4.4 %fusion.21 = f32[2048,512]{0,1:T(8,128)} fusion(f32[2048,256]{1,0:T(8,128)S(1)} %fusion.47, bf16[2048,256]{1,0:T(8,128)(2,1)} %collective-permute-done.8, bf16[256,256]{1,0:T(8,128)(2,1)S(1)} %collective-permute-done.9, bf16[2,256,512]{2,1,0:T(8,128)(2,1)} %param.10), kind=kOutput, calls=%fused_computation.38 | convolution fusion | flops 806354944 | bytes 7733248 | tf_op jit(solution)/shard_map/dot_general | solution.py:82
  270.0 5.4 %fusion.5 = f32[2048,512]{0,1:T(8,128)S(1)} fusion(f32[2048,512]{0,1:T(8,128)} %fusion.20, bf16[2048,128]{1,0:T(8,128)(2,1)} %collective-permute-done.21, bf16[2048,1024]{1,0:T(8,128)(2,1)} %copy-done, bf16[2,768,512]{2,1,0:T(8,128)(2,1)} %param.11), kind=kOutput, calls=%fused_computation.8 | convolution fusion | flops 1617952768 | bytes 13893632 | tf_op jit(solution)/shard_map/dot_general | solution.py:34
  275.4 0.4 copy-done.2
  276.2 3.1 %fusion.4 = f32[2048,512]{0,1:T(8,128)S(1)} fusion(f32[2048,512]{0,1:T(8,128)S(1)} %copy-done.2, bf16[2048,1024]{1,0:T(8,128)(2,1)S(1)} %copy-done.1, bf16[2048,128]{1,0:T(8,128)(2,1)} %collective-permute-done.10, bf16[2,768,512]{2,1,0:T(8,128)(2,1)S(1)} %copy-done.5), kind=kOutput, calls=%fused_computation.7 | convolution fusion | flops 1617952768 | bytes 13893632 | tf_op jit(solution)/shard_map/dot_general | solution.py:34
  279.3 3.9 %pad_maximum_fusion = f32[2048,1024]{0,1:T(8,128)} fusion(f32[2048,512]{0,1:T(8,128)S(1)} %fusion.5, f32[2048,512]{0,1:T(8,128)S(1)} %fusion.4), kind=kLoop, calls=%fused_computation | loop fusion | flops 2097152 | bytes 16777216 | tf_op jit(solution)/shard_map/concatenate | solution.py:86
  283.2 9.2 %copy.7 = f32[2048,1024]{1,0:T(8,128)} copy(f32[2048,1024]{0,1:T(8,128)} %pad_maximum_fusion) | data formatting | bytes 16777216 | tf_op jit(solution)/shard_map/concatenate | solution.py:86
  (43 shorter events, 6.1 us)
Async XLA Ops:
  0.0 4.1 %copy-start.6 = (bf16[2,512,256]{2,1,0:T(8,128)(2,1)S(1)}, bf16[2,512,256]{2,1,0:T(8,128)(2,1)}, u32[]{:S(2)}) copy-start(bf16[2,512,256]{2,1,0:T(8,128)(2,1)} %param.7) | copy-start | bytes 1572868
  4.1 173.6 %copy-start = (bf16[2048,1024]{1,0:T(8,128)(2,1)}, bf16[2048,1024]{1,0:T(8,128)(2,1)S(1)}, u32[]{:S(2)}) copy-start(bf16[2048,1024]{1,0:T(8,128)(2,1)S(1)} %convert_element_type.45) | copy-start | bytes 12582916
  4.8 2.1 copy-start.3
  7.0 1.4 copy-start.4
  8.8 4.5 %collective-permute-start.11 = (bf16[2048,256]{1,0:T(8,128)(2,1)S(1)}, bf16[2048,256]{1,0:T(8,128)(2,1)S(1)}, u32[]{:S(2)}, u32[]{:S(2)}) collective-permute-start(bf16[2048,256]{1,0:T(8,128)(2,1)S(1)} %fusion.12), channel_id=1, source_target_pairs={{0,1},{1,0},{2,3},{3,2},{4,5},{5,4},{6,7},{7,6},{8,9},{9,8},{10,11... | collective-permute-start | bytes 3145736 | tf_op jit(solution)/shard_map/ppermute | solution.py:28
  10.2 6.5 %collective-permute-start = (bf16[2048,256]{1,0:T(8,128)(2,1)S(1)}, bf16[2048,256]{1,0:T(8,128)(2,1)S(1)}, u32[]{:S(2)}, u32[]{:S(2)}) collective-permute-start(bf16[2048,256]{1,0:T(8,128)(2,1)S(1)} %fusion.6), channel_id=1, source_target_pairs={{0,1},{1,0},{2,3},{3,2},{4,5},{5,4},{6,7},{7,6},{8,9},{9,8},{10,11... | collective-permute-start | bytes 3145736 | tf_op jit(solution)/shard_map/ppermute | solution.py:28
  10.4 2.9 collective-permute-start.12
  10.9 5.7 %collective-permute-start.1 = (bf16[256,256]{1,0:T(8,128)(2,1)S(1)}, bf16[256,256]{1,0:T(8,128)(2,1)S(1)}, u32[]{:S(2)}, u32[]{:S(2)}) collective-permute-start(bf16[256,256]{1,0:T(8,128)(2,1)S(1)} %get-tuple-element.14), channel_id=1, source_target_pairs={{0,1},{1,0},{2,3},{3,2},{4,5},{5,4},{6,7},{7,6},{8,9},{9,8},{10,11... | collective-permute-start | bytes 393224 | tf_op jit(solution)/shard_map/ppermute | solution.py:28
  13.8 52.1 %collective-permute-start.13 = (bf16[2048,256]{1,0:T(8,128)(2,1)S(1)}, bf16[2048,256]{1,0:T(8,128)(2,1)S(1)}, u32[]{:S(2)}, u32[]{:S(2)}) collective-permute-start(bf16[2048,256]{1,0:T(8,128)(2,1)S(1)} %fusion.13), channel_id=1, source_target_pairs={{0,2},{1,3},{2,0},{3,1},{4,6},{5,7},{6,4},{7,5},{8,10},{9,11},{10,... | collective-permute-start | bytes 3145736 | tf_op jit(solution)/shard_map/ppermute | solution.py:28
  17.1 51.4 %collective-permute-start.2 = (bf16[2048,256]{1,0:T(8,128)(2,1)S(1)}, bf16[2048,256]{1,0:T(8,128)(2,1)S(1)}, u32[]{:S(2)}, u32[]{:S(2)}) collective-permute-start(bf16[2048,256]{1,0:T(8,128)(2,1)S(1)} %fusion.7), channel_id=1, source_target_pairs={{0,2},{1,3},{2,0},{3,1},{4,6},{5,7},{6,4},{7,5},{8,10},{9,11},{10,... | collective-permute-start | bytes 3145736 | tf_op jit(solution)/shard_map/ppermute | solution.py:28
  17.2 48.7 %collective-permute-start.14 = (bf16[256,256]{1,0:T(8,128)(2,1)S(1)}, bf16[256,256]{1,0:T(8,128)(2,1)S(1)}, u32[]{:S(2)}, u32[]{:S(2)}) collective-permute-start(bf16[256,256]{1,0:T(8,128)(2,1)S(1)} %get-tuple-element.9), channel_id=1, source_target_pairs={{0,2},{1,3},{2,0},{3,1},{4,6},{5,7},{6,4},{7,5},{8,10},{9,11},{10,... | collective-permute-start | bytes 393224 | tf_op jit(solution)/shard_map/ppermute | solution.py:28
  19.2 49.3 %collective-permute-start.3 = (bf16[256,256]{1,0:T(8,128)(2,1)S(1)}, bf16[256,256]{1,0:T(8,128)(2,1)S(1)}, u32[]{:S(2)}, u32[]{:S(2)}) collective-permute-start(bf16[256,256]{1,0:T(8,128)(2,1)S(1)} %get-tuple-element.13), channel_id=1, source_target_pairs={{0,2},{1,3},{2,0},{3,1},{4,6},{5,7},{6,4},{7,5},{8,10},{9,11},{10,... | collective-permute-start | bytes 393224 | tf_op jit(solution)/shard_map/ppermute | solution.py:28
  66.4 51.0 %collective-permute-start.15 = (bf16[2048,256]{1,0:T(8,128)(2,1)S(1)}, bf16[2048,256]{1,0:T(8,128)(2,1)S(1)}, u32[]{:S(2)}, u32[]{:S(2)}) collective-permute-start(bf16[2048,256]{1,0:T(8,128)(2,1)S(1)} %fusion.14), channel_id=1, source_target_pairs={{0,4},{1,5},{2,6},{3,7},{4,0},{5,1},{6,2},{7,3},{8,12},{9,13},{10,... | collective-permute-start | bytes 3145736 | tf_op jit(solution)/shard_map/ppermute | solution.py:28
  69.0 50.4 %collective-permute-start.4 = (bf16[2048,256]{1,0:T(8,128)(2,1)S(1)}, bf16[2048,256]{1,0:T(8,128)(2,1)S(1)}, u32[]{:S(2)}, u32[]{:S(2)}) collective-permute-start(bf16[2048,256]{1,0:T(8,128)(2,1)S(1)} %fusion.8), channel_id=1, source_target_pairs={{0,4},{1,5},{2,6},{3,7},{4,0},{5,1},{6,2},{7,3},{8,12},{9,13},{10,... | collective-permute-start | bytes 3145736 | tf_op jit(solution)/shard_map/ppermute | solution.py:28
  70.5 46.8 %collective-permute-start.16 = (bf16[256,256]{1,0:T(8,128)(2,1)S(1)}, bf16[256,256]{1,0:T(8,128)(2,1)S(1)}, u32[]{:S(2)}, u32[]{:S(2)}) collective-permute-start(bf16[256,256]{1,0:T(8,128)(2,1)S(1)} %get-tuple-element.8), channel_id=1, source_target_pairs={{0,4},{1,5},{2,6},{3,7},{4,0},{5,1},{6,2},{7,3},{8,12},{9,13},{10,... | collective-permute-start | bytes 393224 | tf_op jit(solution)/shard_map/ppermute | solution.py:28
  71.0 48.3 %collective-permute-start.5 = (bf16[256,256]{1,0:T(8,128)(2,1)S(1)}, bf16[256,256]{1,0:T(8,128)(2,1)S(1)}, u32[]{:S(2)}, u32[]{:S(2)}) collective-permute-start(bf16[256,256]{1,0:T(8,128)(2,1)S(1)} %get-tuple-element.12), channel_id=1, source_target_pairs={{0,4},{1,5},{2,6},{3,7},{4,0},{5,1},{6,2},{7,3},{8,12},{9,13},{10,... | collective-permute-start | bytes 393224 | tf_op jit(solution)/shard_map/ppermute | solution.py:28
  117.8 56.1 %collective-permute-start.17 = (bf16[2048,256]{1,0:T(8,128)(2,1)S(1)}, bf16[2048,256]{1,0:T(8,128)(2,1)S(1)}, u32[]{:S(2)}, u32[]{:S(2)}) collective-permute-start(bf16[2048,256]{1,0:T(8,128)(2,1)S(1)} %fusion.15), channel_id=1, source_target_pairs={{0,8},{1,9},{2,10},{3,11},{4,12},{5,13},{6,14},{7,15},{8,0},{9,1},... | collective-permute-start | bytes 3145736 | tf_op jit(solution)/shard_map/ppermute | solution.py:28
  119.8 55.5 %collective-permute-start.6 = (bf16[2048,256]{1,0:T(8,128)(2,1)S(1)}, bf16[2048,256]{1,0:T(8,128)(2,1)S(1)}, u32[]{:S(2)}, u32[]{:S(2)}) collective-permute-start(bf16[2048,256]{1,0:T(8,128)(2,1)S(1)} %fusion.9), channel_id=1, source_target_pairs={{0,8},{1,9},{2,10},{3,11},{4,12},{5,13},{6,14},{7,15},{8,0},{9,1},... | collective-permute-start | bytes 3145736 | tf_op jit(solution)/shard_map/ppermute | solution.py:28
  120.7 129.6 %collective-permute-start.9 = (bf16[256,256]{1,0:T(8,128)(2,1)S(1)}, bf16[256,256]{1,0:T(8,128)(2,1)S(1)}, u32[]{:S(2)}, u32[]{:S(2)}) collective-permute-start(bf16[256,256]{1,0:T(8,128)(2,1)S(1)} %get-tuple-element.7), channel_id=1, source_target_pairs={{0,16},{1,17},{2,18},{3,19},{4,20},{5,21},{6,22},{7,23},{8,24},{9,... | collective-permute-start | bytes 393224 | tf_op jit(solution)/shard_map/ppermute | solution.py:28
  123.3 51.9 %collective-permute-start.7 = (bf16[256,256]{1,0:T(8,128)(2,1)S(1)}, bf16[256,256]{1,0:T(8,128)(2,1)S(1)}, u32[]{:S(2)}, u32[]{:S(2)}) collective-permute-start(bf16[256,256]{1,0:T(8,128)(2,1)S(1)} %get-tuple-element.11), channel_id=1, source_target_pairs={{0,8},{1,9},{2,10},{3,11},{4,12},{5,13},{6,14},{7,15},{8,0},{9,1},... | collective-permute-start | bytes 393224 | tf_op jit(solution)/shard_map/ppermute | solution.py:28
  124.4 47.4 %collective-permute-start.18 = (bf16[256,256]{1,0:T(8,128)(2,1)S(1)}, bf16[256,256]{1,0:T(8,128)(2,1)S(1)}, u32[]{:S(2)}, u32[]{:S(2)}) collective-permute-start(bf16[256,256]{1,0:T(8,128)(2,1)S(1)} %get-tuple-element.16), channel_id=1, source_target_pairs={{0,8},{1,9},{2,10},{3,11},{4,12},{5,13},{6,14},{7,15},{8,0},{9,1},... | collective-permute-start | bytes 393224 | tf_op jit(solution)/shard_map/ppermute | solution.py:28
  171.8 50.8 %collective-permute-start.20 = (bf16[256,256]{1,0:T(8,128)(2,1)S(1)}, bf16[256,256]{1,0:T(8,128)(2,1)S(1)}, u32[]{:S(2)}, u32[]{:S(2)}) collective-permute-start(bf16[256,256]{1,0:T(8,128)(2,1)S(1)} %get-tuple-element.15), channel_id=1, source_target_pairs={{0,16},{1,17},{2,18},{3,19},{4,20},{5,21},{6,22},{7,23},{8,24},{9,... | collective-permute-start | bytes 393224 | tf_op jit(solution)/shard_map/ppermute | solution.py:28
  174.3 71.0 %collective-permute-start.19 = (bf16[2048,256]{1,0:T(8,128)(2,1)S(1)}, bf16[2048,256]{1,0:T(8,128)(2,1)}, u32[]{:S(2)}, u32[]{:S(2)}) collective-permute-start(bf16[2048,256]{1,0:T(8,128)(2,1)S(1)} %fusion.16), channel_id=1, source_target_pairs={{0,16},{1,17},{2,18},{3,19},{4,20},{5,21},{6,22},{7,23},{8,24},{9,... | collective-permute-start | bytes 3145736 | tf_op jit(solution)/shard_map/ppermute | solution.py:28
  175.7 89.9 %collective-permute-start.8 = (bf16[2048,256]{1,0:T(8,128)(2,1)S(1)}, bf16[2048,256]{1,0:T(8,128)(2,1)}, u32[]{:S(2)}, u32[]{:S(2)}) collective-permute-start(bf16[2048,256]{1,0:T(8,128)(2,1)S(1)} %fusion.10), channel_id=1, source_target_pairs={{0,16},{1,17},{2,18},{3,19},{4,20},{5,21},{6,22},{7,23},{8,24},{9,... | collective-permute-start | bytes 3145736 | tf_op jit(solution)/shard_map/ppermute | solution.py:28
  178.9 96.5 %collective-permute-start.10 = (bf16[2048,128]{1,0:T(8,128)(2,1)}, bf16[2048,128]{1,0:T(8,128)(2,1)}, u32[]{:S(2)}, u32[]{:S(2)}) collective-permute-start(bf16[2048,128]{1,0:T(8,128)(2,1)} %get-tuple-element.5), channel_id=1, source_target_pairs={{0,1},{1,2},{2,3},{3,4},{4,5},{5,6},{6,7},{7,8},{8,9},{9,10},{10,1... | collective-permute-start | bytes 1572872 | tf_op jit(solution)/shard_map/ppermute | solution.py:18
  222.6 47.4 %collective-permute-start.21 = (bf16[2048,128]{1,0:T(8,128)(2,1)}, bf16[2048,128]{1,0:T(8,128)(2,1)}, u32[]{:S(2)}, u32[]{:S(2)}) collective-permute-start(bf16[2048,128]{1,0:T(8,128)(2,1)} %get-tuple-element.6), channel_id=1, source_target_pairs={{1,0},{2,1},{3,2},{4,3},{5,4},{6,5},{7,6},{8,7},{9,8},{10,9},{11,1... | collective-permute-start | bytes 1572872 | tf_op jit(solution)/shard_map/ppermute | solution.py:20
  270.0 5.4 %copy-start.1 = (bf16[2048,1024]{1,0:T(8,128)(2,1)S(1)}, bf16[2048,1024]{1,0:T(8,128)(2,1)}, u32[]{:S(2)}) copy-start(bf16[2048,1024]{1,0:T(8,128)(2,1)} %copy-done) | copy-start | bytes 12582916
  270.0 5.8 %copy-start.2 = (f32[2048,512]{0,1:T(8,128)S(1)}, f32[2048,512]{0,1:T(8,128)}, u32[]{:S(2)}) copy-start(f32[2048,512]{0,1:T(8,128)} %fusion.21) | copy-start | bytes 12582916
  270.0 6.2 %copy-start.5 = (bf16[2,768,512]{2,1,0:T(8,128)(2,1)S(1)}, bf16[2,768,512]{2,1,0:T(8,128)(2,1)}, u32[]{:S(2)}) copy-start(bf16[2,768,512]{2,1,0:T(8,128)(2,1)} %param.11) | copy-start | bytes 4718596
where the time goes:
time: 293 us; the launch traced here: 292 us
  waiting for transfers between devices  213 us (73%)
  matrix products  30.2 us (10%)
  starting transfers between devices  27.8 us (9%)
  local copies, waits for them, and re-layouts  13.7 us (5%)
  other arithmetic  7.95 us (3%)
    ppermute x20, waiting for transfers between devices, from_partner(): lax.ppermute(shard, axis, [(i, i ^ 1 << apart) for i in range(lax.axis_si...  213 us
    ppermute x20, starting transfers between devices, from_partner(): lax.ppermute(shard, axis, [(i, i ^ 1 << apart) for i in range(lax.axis_si...  24.3 us
    dot_general x2, matrix products, per_device(): jnp.dot(proxies[which], out_basis[which], preferred_element_type=jnp.floa...  9.46 us
    concatenate x1, local copies, waits for them, and re-layouts, per_device(): return jnp.concatenate(columns, axis=1)  9.24 us
    dot_general x2, matrix products, near_terms(): jnp.dot(padded[:, which * B:which * B + B + 2 * H], near_blocks[which], p...  8.45 us
  transfers between devices with their start and end apart: 22, of which 7 were waited for; matrix products, arithmetic and copies ran while one was open for 9% of the time, Pallas kernels for 0%

commit v1 on v0

v1 whole, which is shorter than its diff:
```python
import functools

import jax
import jax.numpy as jnp
from jax import lax
from jax.experimental import pallas as pl
from jax.experimental.pallas import tpu as pltpu
from jax.sharding import PartitionSpec as P

BF16 = jnp.bfloat16
F32 = jnp.float32
FIRST = (23,22,22,21,20,20)
MIDDLE = FIRST
LAST = FIRST


def dot(a, b):
    return jnp.dot(a, b, preferred_element_type=F32)


def cut(rows, shares):
    ends = [rows * sum(shares[: at + 1]) // sum(shares) // 16 * 16 for at in range(len(shares))]
    ends[-1] = rows
    starts = [0] + ends[:-1]
    return [(start, end - start) for start, end in zip(starts, ends)]


def inside(piece, pieces):
    return [q for q in pieces if piece[0] <= q[0] and q[0] + q[1] <= piece[0] + piece[1]]


RIMS = (-1, (0, 0))
IN_FLIGHT = 5


RIMS = (-1, (0, 0))
TAKE = (-2, (0, 0))


def order_of(cuts, rows):
    levels = len(cuts)
    pieces = cuts[1]
    order = []
    for t in range(len(pieces) + levels - 1):
        for level in [levels - 2, levels - 1] + list(range(levels - 3, -1, -1)):
            if 0 <= t - level < len(pieces):
                order.append((level, pieces[t - level]))
        if t == 1:
            order.append(RIMS)
        if t == 2:
            order.append(TAKE)
    return order, 0


def copies(pairs, sems):
    return [pltpu.make_async_copy(src, dst, sems.at[at]) for at, (src, dst) in enumerate(pairs)]


def blocks_of(size):
    step = 128
    return [(at, min(step, size - at)) for at in range(0, size, step)]


def leaf_rows(src, leaf, stay, cross, held, sent, rows):
    points, rank = leaf.shape[1:]
    grown = [
        dot(src[rows, b * points : (b + 1) * points].astype(BF16), leaf[b]).astype(BF16) for b in range(2)
    ]
    for b in range(2):
        cols = slice(b * rank, (b + 1) * rank)
        mixed = (dot(grown[b], stay[0, b]) + dot(grown[1 - b], cross[0, 1 - b])).astype(BF16)
        held[:, cols] = mixed
        sent[:, cols] = dot(mixed, cross[1, b]).astype(BF16)


def first_leaf_step(size, src, leaf, stay, cross, prev, held, sent, token, rows, leaf_in, stay_in, cross_in, sems):
    moves = copies(
        [
            (src.at[pl.ds(0, size)], rows),
            (leaf, leaf_in),
            (stay.at[pl.ds(0, 1)], stay_in),
            (cross.at[pl.ds(0, 2)], cross_in),
        ],
        sems,
    )
    for move in moves:
        move.start()
    for move in moves:
        move.wait()
    leaf_rows(rows, leaf_in, stay_in, cross_in, held, sent, slice(None))
    token[...] = jnp.zeros_like(token)


def leaf_step(start, size, src, leaf, stay, cross, prev, *outs):
    held, sent, token = outs[-3:]
    leaf_rows(src, leaf, stay, cross, held, sent, slice(start, start + size))
    token[...] = jnp.zeros_like(token)


def level_step(level, bounds, extra, held_in, moved, stay, cross, prev, *outs):
    outs = outs[extra:]
    rank = stay.shape[-1]
    count = len(bounds)
    for at, (start, size) in enumerate(bounds):
        held, sent = outs[at], outs[count + at]
        for b in range(2):
            cols = slice(b * rank, (b + 1) * rank)
            mixed = dot(held_in[start : start + size, cols], stay[level, b])
            mixed = (mixed + moved[start : start + size, cols].astype(F32)).astype(BF16)
            held[:, cols] = mixed
            sent[:, cols] = dot(mixed, cross[level + 1, b]).astype(BF16)
    token = outs[-1]
    token[...] = jnp.zeros_like(token)


def last_step(level, start, size, held, moved, stay, out_basis, near, src, rim_a, rim_b, prev, *refs):
    out, token, window, result, sems = refs[-5:]
    rank, points = out_basis.shape[1:]
    rim = rim_a.shape[1]
    blocks = blocks_of(size)
    odd = lax.rem(lax.axis_index("box"), 2) == 1
    leaves = copies([(result.at[pl.ds(at, n)], out.at[pl.ds(start + at, n)]) for at, n in blocks], sems)
    for leave, (at, n) in zip(leaves, blocks):
        part, whole = slice(at, at + n), slice(start + at, start + at + n)
        window[part, :rim] = jnp.where(odd, rim_a[whole], rim_b[whole])
        window[part, rim : rim + 2 * points] = src[whole].astype(BF16)
        window[part, rim + 2 * points :] = jnp.where(odd, rim_b[whole], rim_a[whole])
        for b in range(2):
            cols = slice(b * rank, (b + 1) * rank)
            mixed = (dot(held[part, cols], stay[level, b]) + moved[part, cols].astype(F32)).astype(BF16)
            result[part, b * points : (b + 1) * points] = dot(mixed, out_basis[b]) + dot(
                window[part, b * points : (b + 1) * points + 2 * rim], near[b]
            )
        leave.start()
    for leave in leaves:
        leave.wait()
    token[...] = jnp.zeros_like(token)


def rim_step(src, prev, to_a, to_b, token):
    rim = to_a.shape[1]
    odd = lax.rem(lax.axis_index("box"), 2) == 1
    head, tail = src[:, :rim].astype(BF16), src[:, src.shape[1] - rim :].astype(BF16)
    to_a[...] = jnp.where(odd, head, tail)
    to_b[...] = jnp.where(odd, tail, head)
    token[...] = jnp.zeros_like(token)


ANY = pl.BlockSpec(memory_space=pl.ANY)
VMEM = pl.BlockSpec(memory_space=pltpu.VMEM)
TOKEN = jax.ShapeDtypeStruct((8, 128), F32)
SOME = pl.CostEstimate(flops=6*10**8, bytes_accessed=1, transcendentals=0)
LITTLE = pl.CostEstimate(flops=10**7, bytes_accessed=1, transcendentals=0)


def call(body, operands, in_specs, out_shape, out_specs, scratch, name, mib, aliases=None):
    return pl.pallas_call(
        body,
        in_specs=in_specs,
        out_specs=out_specs,
        out_shape=out_shape,
        scratch_shapes=scratch,
        input_output_aliases=aliases or {},
        compiler_params=pltpu.CompilerParams(vmem_limit_bytes=mib * 1024 * 1024),
        cost_estimate=LITTLE if name in ("last", "near") else SOME,
        name=name,
    )(*operands)


def per_device(sources, leaf_basis, stay_blocks, cross_blocks, out_basis, near_blocks):
    rows, points = sources.shape
    levels, _, rank, _ = stay_blocks.shape
    devices = lax.axis_size("box")
    rim = (near_blocks.shape[1] - near_blocks.shape[2]) // 2
    cuts = [None, cut(rows, FIRST)] + [cut(rows, MIDDLE)] * (levels - 3) + [cut(rows, LAST)]
    order, _ = order_of(cuts, rows)
    pair = lambda size: jax.ShapeDtypeStruct((size, 2 * rank), BF16)
    sems = lambda count: pltpu.SemaphoreType.DMA((count,))
    in_hbm = lambda array: pltpu.with_memory_space_constraint(array, pltpu.HBM)

    token = jnp.zeros(TOKEN.shape, TOKEN.dtype)
    out, rims, taken = None, None, False
    held, moved = {}, {}
    for level, piece in order:
        start, size = piece
        sent = {}
        if level == -2:
            taken = True
            continue
        extra = [*rims] if taken else []
        taken = False
        if level == -1:
            to_a, to_b, token = call(
                rim_step, (sources, token), [VMEM, ANY],
                [jax.ShapeDtypeStruct((rows, rim), BF16)] * 2 + [TOKEN],
                [VMEM] * 3, [], "rims", 8,
            )
            rims = (
                lax.ppermute(to_a, "box", [(i, i ^ 1) for i in range(devices)]),
                lax.ppermute(to_b, "box", [(i, (i - 1 ^ 1) + 1) for i in range(1, devices - 1)]),
            )
        elif level == 0 and start == 0:
            held[1, piece], sent[piece], token = call(
                functools.partial(first_leaf_step, size),
                (*map(in_hbm, (sources, leaf_basis, stay_blocks, cross_blocks)), token),
                [ANY] * 5,
                [pair(size), pair(size), TOKEN],
                [VMEM, VMEM, VMEM],
                [pltpu.VMEM((size, points), F32), pltpu.VMEM(leaf_basis.shape, BF16),
                 pltpu.VMEM((1,) + stay_blocks.shape[1:], BF16), pltpu.VMEM((2,) + cross_blocks.shape[1:], BF16),
                 sems(4)],
                "leaf", 16,
            )
        elif level == 0:
            held[1, piece], sent[piece], token = call(
                functools.partial(leaf_step, start, size),
                (sources, leaf_basis, stay_blocks, cross_blocks, token, *extra),
                [VMEM, VMEM, VMEM, VMEM, ANY] + [ANY] * len(extra),
                [pair(size), pair(size), TOKEN],
                [VMEM, VMEM, VMEM],
                [],
                "leaf", 16,
            )
        elif level < levels - 1:
            children = inside(piece, cuts[level + 1])
            results = call(
                functools.partial(level_step, level, [(q[0] - start, q[1]) for q in children], len(extra)),
                (held.pop((level, piece)), moved.pop((level, piece)), stay_blocks, cross_blocks, token, *extra),
                [VMEM, VMEM, VMEM, VMEM, ANY] + [ANY] * len(extra),
                [pair(q[1]) for q in children] * 2 + [TOKEN],
                [VMEM] * (2 * len(children) + 1),
                [], "near" if level == levels - 2 else "level", 16,
            )
            token = results[-1]
            for which, q in enumerate(children):
                held[level + 1, q] = results[which]
                sent[q] = results[len(children) + which]
        else:
            operands = [held.pop((level, piece)), moved.pop((level, piece)), stay_blocks, out_basis, near_blocks,
                        sources, *rims, token]
            in_specs = [VMEM] * 8 + [ANY]
            aliases = {}
            if out is not None:
                operands.append(out)
                in_specs.append(ANY)
                aliases = {9: 0}
            out, token = call(
                functools.partial(last_step, level, start, size),
                operands, in_specs,
                [jax.ShapeDtypeStruct((rows, points), F32), TOKEN],
                [pl.BlockSpec(memory_space=pltpu.HBM), VMEM],
                [pltpu.VMEM((size, points + 2 * rim), BF16), pltpu.VMEM((size, points), F32),
                 sems(len(blocks_of(size)))],
                "last", 16, aliases,
            )
        for q, array in sent.items():
            moved[level + 1, q] = lax.ppermute(array, "box", [(i, i ^ 1 << level) for i in range(devices)])
    return out


def solution(mesh):
    in_specs = (
        P(None, "box"),
        P("box", None, None),
        P(None, "box", None, None),
        P(None, "box", None, None),
        P("box", None, None),
        P("box", None, None),
    )
    out_specs = P(None, "box")
    return jax.shard_map(
        per_device, mesh=mesh, in_specs=in_specs, out_specs=out_specs, check_vma=False
    )
```

time: 293 us -> 167 us (0.57)
  waiting for transfers between devices: 213 us -> 85.1 us
  Pallas kernels: 0 us -> 30.8 us
  matrix products: 30.2 us -> 0 us
  starting transfers between devices: 27.8 us -> 49.9 us
  local copies, waits for them, and re-layouts: 13.7 us -> 0.03 us
  other arithmetic: 7.95 us -> 0 us
    ppermute x22 -> x32, waiting for transfers between devices: 213 us -> 85.1 us  [the longest x30 85.1 us: per_device(): lax.ppermute(array, 'box', [(i, i ^ 1 << level) for i in range(devices)])]
    pallas_call x0 -> x37, Pallas kernels: none -> 30.8 us  [call(): pl.pallas_call(body, in_specs=in_specs, out_specs=out_specs, out_shape=ou...]
    dot_general x28 -> x0, matrix products: 30.2 us -> none  [the longest x2 9.46 us: per_device(): jnp.dot(proxies[which], out_basis[which], preferred_element_type=jnp.floa...]
    ppermute x22 -> x32, starting transfers between devices: 27.8 us -> 49.9 us  [the longest x30 48.5 us: per_device(): lax.ppermute(array, 'box', [(i, i ^ 1 << level) for i in range(devices)])]
    concatenate x1 -> x0, local copies, waits for them, and re-layouts: 9.24 us -> none  [per_device(): return jnp.concatenate(columns, axis=1)]
    convert_element_type x1 -> x0, other arithmetic: 4.09 us -> none  [per_device(): rounded = sources.astype(jnp.bfloat16)]
    concatenate x1 -> x0, other arithmetic: 3.86 us -> none  [per_device(): return jnp.concatenate(columns, axis=1)]
    unnamed x14 -> x12, local copies, waits for them, and re-layouts: 3.26 us -> 0.03 us
  transfers between devices with their start and end apart: 22 -> 32, of which waited for: 7 -> 14; matrix products, arithmetic and copies ran while one was open for 9% -> 0% of each run, Pallas kernels for 0% -> 15%
where the time goes in v1:
time: 167 us; the launch traced here: 166 us
  waiting for transfers between devices  85.1 us (51%)
  starting transfers between devices  49.9 us (30%)
  Pallas kernels  30.8 us (18%)
    ppermute x30, waiting for transfers between devices, per_device(): lax.ppermute(array, 'box', [(i, i ^ 1 << level) for i in range(devices)])  85.1 us
    ppermute x30, starting transfers between devices, per_device(): lax.ppermute(array, 'box', [(i, i ^ 1 << level) for i in range(devices)])  48.5 us
    pallas_call x37, Pallas kernels, call(): pl.pallas_call(body, in_specs=in_specs, out_specs=out_specs, out_shape=ou...  30.8 us
  transfers between devices with their start and end apart: 32, of which 14 were waited for; matrix products, arithmetic and copies ran while one was open for 0% of the time, Pallas kernels for 15%

profile of v1, /device:TPU:0, one launch (start us, length us, event | category | flops | bytes accessed | tf_op | source)
XLA Modules:
  0.0 166.4 jit_solution(1242770670818733315)
XLA Ops:
  0.0 2.9 %leaf.12 = (bf16[368,512]{1,0:T(8,128)(2,1)S(1)}, bf16[368,512]{1,0:T(8,128)(2,1)S(1)}, f32[8,128]{1,0:T(8,128)S(1)}) custom-call(f32[2048,1024]{1,0:T(8,128)} %src.25, bf16[2,512,256]{2,1,0:T(8,128)(2,1)} %leaf.23, bf16[6,2,256,256]{3,2,1,0:T(8,128)(2,1)} %stay.71, bf16[6,2,256,256]{3,2,1,0:T(8,128)(2,1)} %cross.59, f32[8,128]{1,0:T(8,128)S(1)} %broadcast_in_dim.3.prev), custom_call_target="tpu_custom_call" | custom-call | flops 600000000 | bytes 1 | tf_op jit(solution)/shard_map/leaf/pallas_call | solution.py:157
  3.0 0.5 collective-permute-start
  3.5 1.3 collective-permute-done.moved
  4.8 0.5 level.18
  5.3 2.9 %collective-permute-start.2 = (bf16[368,512]{1,0:T(8,128)(2,1)S(1)}, bf16[368,512]{1,0:T(8,128)(2,1)S(1)}, u32[]{:S(2)}, u32[]{:S(2)}) collective-permute-start(bf16[368,512]{1,0:T(8,128)(2,1)S(1)} %get-tuple-element.116), channel_id=1, source_target_pairs={{0,2},{1,3},{2,0},{3,1},{4,6},{5,7},{6,4},{7,5},{8,10},{9,11},{10,... | collective-permute-start | bytes 1130504 | tf_op jit(solution)/shard_map/ppermute | solution.py:257
  8.2 1.0 leaf.14
  9.5 0.6 collective-permute-start.6
  10.1 0.9 collective-permute-start.7
  11.0 12.0 %collective-permute-done.2.moved = bf16[368,512]{1,0:T(8,128)(2,1)S(1)} collective-permute-done((bf16[368,512]{1,0:T(8,128)(2,1)S(1)}, bf16[368,512]{1,0:T(8,128)(2,1)S(1)}, u32[]{:S(2)}, u32[]{:S(2)}) %collective-permute-start.2) | collective-permute-done | bytes 376864 | tf_op jit(solution)/shard_map/ppermute | solution.py:257
  23.0 0.5 level.19
  24.0 2.5 %collective-permute-start.4 = (bf16[352,512]{1,0:T(8,128)(2,1)S(1)}, bf16[352,512]{1,0:T(8,128)(2,1)S(1)}, u32[]{:S(2)}, u32[]{:S(2)}) collective-permute-start(bf16[352,512]{1,0:T(8,128)(2,1)S(1)} %get-tuple-element.124), channel_id=1, source_target_pairs={{0,2},{1,3},{2,0},{3,1},{4,6},{5,7},{6,4},{7,5},{8,10},{9,11},{10,... | collective-permute-start | bytes 1081352 | tf_op jit(solution)/shard_map/ppermute | solution.py:257
  26.5 1.0 leaf.16
  27.6 5.1 %collective-permute-done.5.moved = bf16[368,512]{1,0:T(8,128)(2,1)S(1)} collective-permute-done((bf16[368,512]{1,0:T(8,128)(2,1)S(1)}, bf16[368,512]{1,0:T(8,128)(2,1)S(1)}, u32[]{:S(2)}, u32[]{:S(2)}) %collective-permute-start.5) | collective-permute-done | bytes 376864 | tf_op jit(solution)/shard_map/ppermute | solution.py:257
  33.2 2.8 %collective-permute-start.11 = (bf16[368,512]{1,0:T(8,128)(2,1)S(1)}, bf16[368,512]{1,0:T(8,128)(2,1)S(1)}, u32[]{:S(2)}, u32[]{:S(2)}) collective-permute-start(bf16[368,512]{1,0:T(8,128)(2,1)S(1)} %get-tuple-element.140), channel_id=1, source_target_pairs={{0,8},{1,9},{2,10},{3,11},{4,12},{5,13},{6,14},{7,15},{8,0},{9,1},... | collective-permute-start | bytes 1130504 | tf_op jit(solution)/shard_map/ppermute | solution.py:257
  36.7 2.3 %collective-permute-start.10 = (bf16[352,512]{1,0:T(8,128)(2,1)S(1)}, bf16[352,512]{1,0:T(8,128)(2,1)S(1)}, u32[]{:S(2)}, u32[]{:S(2)}) collective-permute-start(bf16[352,512]{1,0:T(8,128)(2,1)S(1)} %get-tuple-element.138), channel_id=1, source_target_pairs={{0,4},{1,5},{2,6},{3,7},{4,0},{5,1},{6,2},{7,3},{8,12},{9,13},{10,... | collective-permute-start | bytes 1081352 | tf_op jit(solution)/shard_map/ppermute | solution.py:257
  39.4 1.4 collective-permute-start.9
  40.8 1.0 leaf.18
  41.9 2.2 %collective-permute-done.11.moved = bf16[368,512]{1,0:T(8,128)(2,1)S(1)} collective-permute-done((bf16[368,512]{1,0:T(8,128)(2,1)S(1)}, bf16[368,512]{1,0:T(8,128)(2,1)S(1)}, u32[]{:S(2)}, u32[]{:S(2)}) %collective-permute-start.11) | collective-permute-done | bytes 376864 | tf_op jit(solution)/shard_map/ppermute | solution.py:257
  44.1 0.5 near.12
  44.6 2.1 %collective-permute-done.10.moved = bf16[352,512]{1,0:T(8,128)(2,1)S(1)} collective-permute-done((bf16[352,512]{1,0:T(8,128)(2,1)S(1)}, bf16[352,512]{1,0:T(8,128)(2,1)S(1)}, u32[]{:S(2)}, u32[]{:S(2)}) %collective-permute-start.10) | collective-permute-done | bytes 360480 | tf_op jit(solution)/shard_map/ppermute | solution.py:257
  47.2 1.6 collective-permute-start.16
  48.8 2.6 %collective-permute-start.15 = (bf16[368,512]{1,0:T(8,128)(2,1)S(1)}, bf16[368,512]{1,0:T(8,128)(2,1)S(1)}, u32[]{:S(2)}, u32[]{:S(2)}) collective-permute-start(bf16[368,512]{1,0:T(8,128)(2,1)S(1)} %get-tuple-element.153), channel_id=1, source_target_pairs={{0,16},{1,17},{2,18},{3,19},{4,20},{5,21},{6,22},{7,23},{8,24},{9,... | collective-permute-start | bytes 1130504 | tf_op jit(solution)/shard_map/ppermute | solution.py:257
  51.8 0.7 collective-permute-start.14
  52.9 2.5 %collective-permute-start.13 = (bf16[336,512]{1,0:T(8,128)(2,1)S(1)}, bf16[336,512]{1,0:T(8,128)(2,1)S(1)}, u32[]{:S(2)}, u32[]{:S(2)}) collective-permute-start(bf16[336,512]{1,0:T(8,128)(2,1)S(1)} %get-tuple-element.149), channel_id=1, source_target_pairs={{0,2},{1,3},{2,0},{3,1},{4,6},{5,7},{6,4},{7,5},{8,10},{9,11},{10,... | collective-permute-start | bytes 1032200 | tf_op jit(solution)/shard_map/ppermute | solution.py:257
  55.4 1.0 leaf.20
  56.5 7.2 %collective-permute-done.16.moved = bf16[352,512]{1,0:T(8,128)(2,1)S(1)} collective-permute-done((bf16[352,512]{1,0:T(8,128)(2,1)S(1)}, bf16[352,512]{1,0:T(8,128)(2,1)S(1)}, u32[]{:S(2)}, u32[]{:S(2)}) %collective-permute-start.16) | collective-permute-done | bytes 360480 | tf_op jit(solution)/shard_map/ppermute | solution.py:257
  64.6 9.0 %collective-permute-done.15.moved = bf16[368,512]{1,0:T(8,128)(2,1)S(1)} collective-permute-done((bf16[368,512]{1,0:T(8,128)(2,1)S(1)}, bf16[368,512]{1,0:T(8,128)(2,1)S(1)}, u32[]{:S(2)}, u32[]{:S(2)}) %collective-permute-start.15) | collective-permute-done | bytes 376864 | tf_op jit(solution)/shard_map/ppermute | solution.py:257
  73.5 1.9 %last.6 = (f32[2048,1024]{1,0:T(8,128)}, f32[8,128]{1,0:T(8,128)S(1)}) custom-call(bf16[368,512]{1,0:T(8,128)(2,1)S(1)} %get-tuple-element.152.held, bf16[368,512]{1,0:T(8,128)(2,1)S(1)} %collective-permute-done.15.moved, bf16[6,2,256,256]{3,2,1,0:T(8,128)(2,1)S(1)} %copy-done, bf16[2,256,512]{2,1,0:T(8,128)(2,1)S(1)} %copy-done.5, ...), custom_call_target="tpu_custom_call" | custom-call | flops 10000000 | bytes 1 | tf_op jit(solution)/shard_map/last/pallas_call | solution.py:157
  75.9 1.3 collective-permute-start.21
  77.7 2.7 %collective-permute-start.19 = (bf16[336,512]{1,0:T(8,128)(2,1)S(1)}, bf16[336,512]{1,0:T(8,128)(2,1)S(1)}, u32[]{:S(2)}, u32[]{:S(2)}) collective-permute-start(bf16[336,512]{1,0:T(8,128)(2,1)S(1)} %get-tuple-element.167), channel_id=1, source_target_pairs={{0,4},{1,5},{2,6},{3,7},{4,0},{5,1},{6,2},{7,3},{8,12},{9,13},{10,... | collective-permute-start | bytes 1032200 | tf_op jit(solution)/shard_map/ppermute | solution.py:257
  81.2 1.0 leaf.22
  82.2 3.6 %collective-permute-done.21.moved = bf16[352,512]{1,0:T(8,128)(2,1)S(1)} collective-permute-done((bf16[352,512]{1,0:T(8,128)(2,1)S(1)}, bf16[352,512]{1,0:T(8,128)(2,1)S(1)}, u32[]{:S(2)}, u32[]{:S(2)}) %collective-permute-start.21) | collective-permute-done | bytes 360480 | tf_op jit(solution)/shard_map/ppermute | solution.py:257
  86.3 1.9 %last.7 = (f32[2048,1024]{1,0:T(8,128)}, f32[8,128]{1,0:T(8,128)S(1)}) custom-call(bf16[352,512]{1,0:T(8,128)(2,1)S(1)} %get-tuple-element.168.held, bf16[352,512]{1,0:T(8,128)(2,1)S(1)} %collective-permute-done.20.moved, bf16[6,2,256,256]{3,2,1,0:T(8,128)(2,1)S(1)} %copy-done, bf16[2,256,512]{2,1,0:T(8,128)(2,1)S(1)} %copy-done.5, ...), custom_call_target="tpu_custom_call", output_to_operand_aliasing={{0}: (9, {})} | custom-call | flops 10000000 | bytes 1 | tf_op jit(solution)/shard_map/last/pallas_call | solution.py:157
  88.8 3.0 %collective-permute-start.24 = (bf16[352,512]{1,0:T(8,128)(2,1)S(1)}, bf16[352,512]{1,0:T(8,128)(2,1)S(1)}, u32[]{:S(2)}, u32[]{:S(2)}) collective-permute-start(bf16[352,512]{1,0:T(8,128)(2,1)S(1)} %get-tuple-element.183), channel_id=1, source_target_pairs={{0,16},{1,17},{2,18},{3,19},{4,20},{5,21},{6,22},{7,23},{8,24},{9,... | collective-permute-start | bytes 1081352 | tf_op jit(solution)/shard_map/ppermute | solution.py:257
  92.3 2.1 %collective-permute-start.23 = (bf16[320,512]{1,0:T(8,128)(2,1)S(1)}, bf16[320,512]{1,0:T(8,128)(2,1)S(1)}, u32[]{:S(2)}, u32[]{:S(2)}) collective-permute-start(bf16[320,512]{1,0:T(8,128)(2,1)S(1)} %get-tuple-element.181), channel_id=1, source_target_pairs={{0,4},{1,5},{2,6},{3,7},{4,0},{5,1},{6,2},{7,3},{8,12},{9,13},{10,... | collective-permute-start | bytes 983048 | tf_op jit(solution)/shard_map/ppermute | solution.py:257
  94.8 1.3 collective-permute-start.22
  96.1 7.3 %collective-permute-done.25.moved = bf16[336,512]{1,0:T(8,128)(2,1)S(1)} collective-permute-done((bf16[336,512]{1,0:T(8,128)(2,1)S(1)}, bf16[336,512]{1,0:T(8,128)(2,1)S(1)}, u32[]{:S(2)}, u32[]{:S(2)}) %collective-permute-start.25) | collective-permute-done | bytes 344096 | tf_op jit(solution)/shard_map/ppermute | solution.py:257
  103.9 1.9 %last.8 = (f32[2048,1024]{1,0:T(8,128)}, f32[8,128]{1,0:T(8,128)S(1)}) custom-call(bf16[352,512]{1,0:T(8,128)(2,1)S(1)} %get-tuple-element.182.held, bf16[352,512]{1,0:T(8,128)(2,1)S(1)} %collective-permute-done.24.moved, bf16[6,2,256,256]{3,2,1,0:T(8,128)(2,1)S(1)} %copy-done, bf16[2,256,512]{2,1,0:T(8,128)(2,1)S(1)} %copy-done.5, ...), custom_call_target="tpu_custom_call", output_to_operand_aliasing={{0}: (9, {})} | custom-call | flops 10000000 | bytes 1 | tf_op jit(solution)/shard_map/last/pallas_call | solution.py:157
  106.3 11.6 %collective-permute-start.28 = (bf16[320,512]{1,0:T(8,128)(2,1)S(1)}, bf16[320,512]{1,0:T(8,128)(2,1)S(1)}, u32[]{:S(2)}, u32[]{:S(2)}) collective-permute-start(bf16[320,512]{1,0:T(8,128)(2,1)S(1)} %get-tuple-element.196), channel_id=1, source_target_pairs={{0,8},{1,9},{2,10},{3,11},{4,12},{5,13},{6,14},{7,15},{8,0},{9,1},... | collective-permute-start | bytes 983048 | tf_op jit(solution)/shard_map/ppermute | solution.py:257
  118.3 1.7 collective-permute-start.26
  120.0 8.3 %collective-permute-done.28.moved = bf16[320,512]{1,0:T(8,128)(2,1)S(1)} collective-permute-done((bf16[320,512]{1,0:T(8,128)(2,1)S(1)}, bf16[320,512]{1,0:T(8,128)(2,1)S(1)}, u32[]{:S(2)}, u32[]{:S(2)}) %collective-permute-start.28) | collective-permute-done | bytes 327712 | tf_op jit(solution)/shard_map/ppermute | solution.py:257
  128.7 1.9 %last.9 = (f32[2048,1024]{1,0:T(8,128)}, f32[8,128]{1,0:T(8,128)S(1)}) custom-call(bf16[336,512]{1,0:T(8,128)(2,1)S(1)} %get-tuple-element.193.held, bf16[336,512]{1,0:T(8,128)(2,1)S(1)} %collective-permute-done.27.moved, bf16[6,2,256,256]{3,2,1,0:T(8,128)(2,1)S(1)} %copy-done, bf16[2,256,512]{2,1,0:T(8,128)(2,1)S(1)} %copy-done.5, ...), custom_call_target="tpu_custom_call", output_to_operand_aliasing={{0}: (9, {})} | custom-call | flops 10000000 | bytes 1 | tf_op jit(solution)/shard_map/last/pallas_call | solution.py:157
  131.2 3.6 %collective-permute-start.31 = (bf16[320,512]{1,0:T(8,128)(2,1)S(1)}, bf16[320,512]{1,0:T(8,128)(2,1)S(1)}, u32[]{:S(2)}, u32[]{:S(2)}) collective-permute-start(bf16[320,512]{1,0:T(8,128)(2,1)S(1)} %get-tuple-element.207), channel_id=1, source_target_pairs={{0,16},{1,17},{2,18},{3,19},{4,20},{5,21},{6,22},{7,23},{8,24},{9,... | collective-permute-start | bytes 983048 | tf_op jit(solution)/shard_map/ppermute | solution.py:257
  134.7 12.9 %collective-permute-done.29.moved = bf16[320,512]{1,0:T(8,128)(2,1)S(1)} collective-permute-done((bf16[320,512]{1,0:T(8,128)(2,1)S(1)}, bf16[320,512]{1,0:T(8,128)(2,1)S(1)}, u32[]{:S(2)}, u32[]{:S(2)}) %collective-permute-start.29) | collective-permute-done | bytes 327712 | tf_op jit(solution)/shard_map/ppermute | solution.py:257
  148.1 1.3 collective-permute-done.31.moved
  149.4 1.9 %last.10 = (f32[2048,1024]{1,0:T(8,128)}, f32[8,128]{1,0:T(8,128)S(1)}) custom-call(bf16[320,512]{1,0:T(8,128)(2,1)S(1)} %get-tuple-element.206.held, bf16[320,512]{1,0:T(8,128)(2,1)S(1)} %collective-permute-done.31.moved, bf16[6,2,256,256]{3,2,1,0:T(8,128)(2,1)S(1)} %copy-done, bf16[2,256,512]{2,1,0:T(8,128)(2,1)S(1)} %copy-done.5, ...), custom_call_target="tpu_custom_call", output_to_operand_aliasing={{0}: (9, {})} | custom-call | flops 10000000 | bytes 1 | tf_op jit(solution)/shard_map/last/pallas_call | solution.py:157
  151.3 12.5 %collective-permute-done.30.moved = bf16[320,512]{1,0:T(8,128)(2,1)S(1)} collective-permute-done((bf16[320,512]{1,0:T(8,128)(2,1)S(1)}, bf16[320,512]{1,0:T(8,128)(2,1)S(1)}, u32[]{:S(2)}, u32[]{:S(2)}) %collective-permute-start.30) | collective-permute-done | bytes 327712 | tf_op jit(solution)/shard_map/ppermute | solution.py:257
  163.8 2.5 %last.11 = (f32[2048,1024]{1,0:T(8,128)}, f32[8,128]{1,0:T(8,128)}) custom-call(bf16[320,512]{1,0:T(8,128)(2,1)S(1)} %get-tuple-element.204.held, bf16[320,512]{1,0:T(8,128)(2,1)S(1)} %collective-permute-done.30.moved, bf16[6,2,256,256]{3,2,1,0:T(8,128)(2,1)S(1)} %copy-done, bf16[2,256,512]{2,1,0:T(8,128)(2,1)S(1)} %copy-done.5, ...), custom_call_target="tpu_custom_call", output_to_operand_aliasing={{0}: (9, {})} | custom-call | flops 10000000 | bytes 1 | tf_op jit(solution)/shard_map/last/pallas_call | solution.py:157
  (66 shorter events, 11.4 us)
Async XLA Ops:
  0.0 4.8 %copy-start = (bf16[6,2,256,256]{3,2,1,0:T(8,128)(2,1)S(1)}, bf16[6,2,256,256]{3,2,1,0:T(8,128)(2,1)}, u32[]{:S(2)}) copy-start(bf16[6,2,256,256]{3,2,1,0:T(8,128)(2,1)} %stay.71) | copy-start | bytes 4718596
  0.0 4.8 %copy-start.2 = (bf16[6,2,256,256]{3,2,1,0:T(8,128)(2,1)S(1)}, bf16[6,2,256,256]{3,2,1,0:T(8,128)(2,1)}, u32[]{:S(2)}) copy-start(bf16[6,2,256,256]{3,2,1,0:T(8,128)(2,1)} %cross.59) | copy-start | bytes 4718596
  0.0 8.2 %copy-start.1 = (f32[2048,1024]{1,0:T(8,128)S(1)}, f32[2048,1024]{1,0:T(8,128)}, u32[]{:S(2)}) copy-start(f32[2048,1024]{1,0:T(8,128)} %src.25) | copy-start | bytes 25165828
  0.0 8.2 %copy-start.4 = (bf16[2,512,256]{2,1,0:T(8,128)(2,1)S(1)}, bf16[2,512,256]{2,1,0:T(8,128)(2,1)}, u32[]{:S(2)}) copy-start(bf16[2,512,256]{2,1,0:T(8,128)(2,1)} %leaf.23) | copy-start | bytes 1572868
  3.0 1.9 %collective-permute-start = (bf16[368,512]{1,0:T(8,128)(2,1)S(1)}, bf16[368,512]{1,0:T(8,128)(2,1)S(1)}, u32[]{:S(2)}, u32[]{:S(2)}) collective-permute-start(bf16[368,512]{1,0:T(8,128)(2,1)S(1)} %get-tuple-element.110), channel_id=1, source_target_pairs={{0,1},{1,0},{2,3},{3,2},{4,5},{5,4},{6,7},{7,6},{8,9},{9,8},{10,11... | collective-permute-start | bytes 1130504 | tf_op jit(solution)/shard_map/ppermute | solution.py:257
  5.3 17.7 %collective-permute-start.2 = (bf16[368,512]{1,0:T(8,128)(2,1)S(1)}, bf16[368,512]{1,0:T(8,128)(2,1)S(1)}, u32[]{:S(2)}, u32[]{:S(2)}) collective-permute-start(bf16[368,512]{1,0:T(8,128)(2,1)S(1)} %get-tuple-element.116), channel_id=1, source_target_pairs={{0,2},{1,3},{2,0},{3,1},{4,6},{5,7},{6,4},{7,5},{8,10},{9,11},{10,... | collective-permute-start | bytes 1130504 | tf_op jit(solution)/shard_map/ppermute | solution.py:257
  9.2 14.3 %collective-permute-start.1 = (bf16[352,512]{1,0:T(8,128)(2,1)S(1)}, bf16[352,512]{1,0:T(8,128)(2,1)S(1)}, u32[]{:S(2)}, u32[]{:S(2)}) collective-permute-start(bf16[352,512]{1,0:T(8,128)(2,1)S(1)} %get-tuple-element.114), channel_id=1, source_target_pairs={{0,1},{1,0},{2,3},{3,2},{4,5},{5,4},{6,7},{7,6},{8,9},{9,8},{10,11... | collective-permute-start | bytes 1081352 | tf_op jit(solution)/shard_map/ppermute | solution.py:257
  9.5 18.1 %collective-permute-start.6 = (bf16[2048,128]{1,0:T(8,128)(2,1)S(1)}, bf16[2048,128]{1,0:T(8,128)(2,1)S(1)}, u32[]{:S(2)}, u32[]{:S(2)}) collective-permute-start(bf16[2048,128]{1,0:T(8,128)(2,1)S(1)} %get-tuple-element.128), channel_id=1, source_target_pairs={{0,1},{1,0},{2,3},{3,2},{4,5},{5,4},{6,7},{7,6},{8,9},{9,8},{10,11... | collective-permute-start | bytes 1572872 | tf_op jit(solution)/shard_map/ppermute | solution.py:199
  10.1 17.5 %collective-permute-start.7 = (bf16[2048,128]{1,0:T(8,128)(2,1)S(1)}, bf16[2048,128]{1,0:T(8,128)(2,1)S(1)}, u32[]{:S(2)}, u32[]{:S(2)}) collective-permute-start(bf16[2048,128]{1,0:T(8,128)(2,1)S(1)} %get-tuple-element.129), channel_id=1, source_target_pairs={{1,2},{2,1},{3,4},{4,3},{5,6},{6,5},{7,8},{8,7},{9,10},{10,9},{11,... | collective-permute-start | bytes 1572872 | tf_op jit(solution)/shard_map/ppermute | solution.py:200
  23.4 9.3 %collective-permute-start.5 = (bf16[368,512]{1,0:T(8,128)(2,1)S(1)}, bf16[368,512]{1,0:T(8,128)(2,1)S(1)}, u32[]{:S(2)}, u32[]{:S(2)}) collective-permute-start(bf16[368,512]{1,0:T(8,128)(2,1)S(1)} %get-tuple-element.126), channel_id=1, source_target_pairs={{0,4},{1,5},{2,6},{3,7},{4,0},{5,1},{6,2},{7,3},{8,12},{9,13},{10,... | collective-permute-start | bytes 1130504 | tf_op jit(solution)/shard_map/ppermute | solution.py:257
  24.0 12.3 %collective-permute-start.4 = (bf16[352,512]{1,0:T(8,128)(2,1)S(1)}, bf16[352,512]{1,0:T(8,128)(2,1)S(1)}, u32[]{:S(2)}, u32[]{:S(2)}) collective-permute-start(bf16[352,512]{1,0:T(8,128)(2,1)S(1)} %get-tuple-element.124), channel_id=1, source_target_pairs={{0,2},{1,3},{2,0},{3,1},{4,6},{5,7},{6,4},{7,5},{8,10},{9,11},{10,... | collective-permute-start | bytes 1081352 | tf_op jit(solution)/shard_map/ppermute | solution.py:257
  27.5 11.5 %collective-permute-start.3 = (bf16[352,512]{1,0:T(8,128)(2,1)S(1)}, bf16[352,512]{1,0:T(8,128)(2,1)S(1)}, u32[]{:S(2)}, u32[]{:S(2)}) collective-permute-start(bf16[352,512]{1,0:T(8,128)(2,1)S(1)} %get-tuple-element.122), channel_id=1, source_target_pairs={{0,1},{1,0},{2,3},{3,2},{4,5},{5,4},{6,7},{7,6},{8,9},{9,8},{10,11... | collective-permute-start | bytes 1081352 | tf_op jit(solution)/shard_map/ppermute | solution.py:257
  33.2 10.9 %collective-permute-start.11 = (bf16[368,512]{1,0:T(8,128)(2,1)S(1)}, bf16[368,512]{1,0:T(8,128)(2,1)S(1)}, u32[]{:S(2)}, u32[]{:S(2)}) collective-permute-start(bf16[368,512]{1,0:T(8,128)(2,1)S(1)} %get-tuple-element.140), channel_id=1, source_target_pairs={{0,8},{1,9},{2,10},{3,11},{4,12},{5,13},{6,14},{7,15},{8,0},{9,1},... | collective-permute-start | bytes 1130504 | tf_op jit(solution)/shard_map/ppermute | solution.py:257
  36.7 10.0 %collective-permute-start.10 = (bf16[352,512]{1,0:T(8,128)(2,1)S(1)}, bf16[352,512]{1,0:T(8,128)(2,1)S(1)}, u32[]{:S(2)}, u32[]{:S(2)}) collective-permute-start(bf16[352,512]{1,0:T(8,128)(2,1)S(1)} %get-tuple-element.138), channel_id=1, source_target_pairs={{0,4},{1,5},{2,6},{3,7},{4,0},{5,1},{6,2},{7,3},{8,12},{9,13},{10,... | collective-permute-start | bytes 1081352 | tf_op jit(solution)/shard_map/ppermute | solution.py:257
  39.4 11.9 %collective-permute-start.9 = (bf16[352,512]{1,0:T(8,128)(2,1)S(1)}, bf16[352,512]{1,0:T(8,128)(2,1)S(1)}, u32[]{:S(2)}, u32[]{:S(2)}) collective-permute-start(bf16[352,512]{1,0:T(8,128)(2,1)S(1)} %get-tuple-element.136), channel_id=1, source_target_pairs={{0,2},{1,3},{2,0},{3,1},{4,6},{5,7},{6,4},{7,5},{8,10},{9,11},{10,... | collective-permute-start | bytes 1081352 | tf_op jit(solution)/shard_map/ppermute | solution.py:257
  41.8 10.7 %collective-permute-start.8 = (bf16[336,512]{1,0:T(8,128)(2,1)S(1)}, bf16[336,512]{1,0:T(8,128)(2,1)S(1)}, u32[]{:S(2)}, u32[]{:S(2)}) collective-permute-start(bf16[336,512]{1,0:T(8,128)(2,1)S(1)} %get-tuple-element.134), channel_id=1, source_target_pairs={{0,1},{1,0},{2,3},{3,2},{4,5},{5,4},{6,7},{7,6},{8,9},{9,8},{10,11... | collective-permute-start | bytes 1032200 | tf_op jit(solution)/shard_map/ppermute | solution.py:257
  47.2 16.5 %collective-permute-start.16 = (bf16[352,512]{1,0:T(8,128)(2,1)S(1)}, bf16[352,512]{1,0:T(8,128)(2,1)S(1)}, u32[]{:S(2)}, u32[]{:S(2)}) collective-permute-start(bf16[352,512]{1,0:T(8,128)(2,1)S(1)} %get-tuple-element.155), channel_id=1, source_target_pairs={{0,8},{1,9},{2,10},{3,11},{4,12},{5,13},{6,14},{7,15},{8,0},{9,1},... | collective-permute-start | bytes 1081352 | tf_op jit(solution)/shard_map/ppermute | solution.py:257
  48.8 24.8 %collective-permute-start.15 = (bf16[368,512]{1,0:T(8,128)(2,1)S(1)}, bf16[368,512]{1,0:T(8,128)(2,1)S(1)}, u32[]{:S(2)}, u32[]{:S(2)}) collective-permute-start(bf16[368,512]{1,0:T(8,128)(2,1)S(1)} %get-tuple-element.153), channel_id=1, source_target_pairs={{0,16},{1,17},{2,18},{3,19},{4,20},{5,21},{6,22},{7,23},{8,24},{9,... | collective-permute-start | bytes 1130504 | tf_op jit(solution)/shard_map/ppermute | solution.py:257
  51.8 23.7 %collective-permute-start.14 = (bf16[352,512]{1,0:T(8,128)(2,1)S(1)}, bf16[352,512]{1,0:T(8,128)(2,1)S(1)}, u32[]{:S(2)}, u32[]{:S(2)}) collective-permute-start(bf16[352,512]{1,0:T(8,128)(2,1)S(1)} %get-tuple-element.151), channel_id=1, source_target_pairs={{0,4},{1,5},{2,6},{3,7},{4,0},{5,1},{6,2},{7,3},{8,12},{9,13},{10,... | collective-permute-start | bytes 1081352 | tf_op jit(solution)/shard_map/ppermute | solution.py:257
  52.9 20.6 %copy-start.3 = (bf16[2,768,512]{2,1,0:T(8,128)(2,1)S(1)}, bf16[2,768,512]{2,1,0:T(8,128)(2,1)}, u32[]{:S(2)}) copy-start(bf16[2,768,512]{2,1,0:T(8,128)(2,1)} %near.23) | copy-start | bytes 4718596
  52.9 20.6 %copy-start.5 = (bf16[2,256,512]{2,1,0:T(8,128)(2,1)S(1)}, bf16[2,256,512]{2,1,0:T(8,128)(2,1)}, u32[]{:S(2)}) copy-start(bf16[2,256,512]{2,1,0:T(8,128)(2,1)} %out_basis.11) | copy-start | bytes 1572868
  52.9 24.3 %collective-permute-start.13 = (bf16[336,512]{1,0:T(8,128)(2,1)S(1)}, bf16[336,512]{1,0:T(8,128)(2,1)S(1)}, u32[]{:S(2)}, u32[]{:S(2)}) collective-permute-start(bf16[336,512]{1,0:T(8,128)(2,1)S(1)} %get-tuple-element.149), channel_id=1, source_target_pairs={{0,2},{1,3},{2,0},{3,1},{4,6},{5,7},{6,4},{7,5},{8,10},{9,11},{10,... | collective-permute-start | bytes 1032200 | tf_op jit(solution)/shard_map/ppermute | solution.py:257
  56.4 24.0 %collective-permute-start.12 = (bf16[320,512]{1,0:T(8,128)(2,1)S(1)}, bf16[320,512]{1,0:T(8,128)(2,1)S(1)}, u32[]{:S(2)}, u32[]{:S(2)}) collective-permute-start(bf16[320,512]{1,0:T(8,128)(2,1)S(1)} %get-tuple-element.147), channel_id=1, source_target_pairs={{0,1},{1,0},{2,3},{3,2},{4,5},{5,4},{6,7},{7,6},{8,9},{9,8},{10,11... | collective-permute-start | bytes 983048 | tf_op jit(solution)/shard_map/ppermute | solution.py:257
  64.1 22.2 %collective-permute-start.20 = (bf16[352,512]{1,0:T(8,128)(2,1)S(1)}, bf16[352,512]{1,0:T(8,128)(2,1)S(1)}, u32[]{:S(2)}, u32[]{:S(2)}) collective-permute-start(bf16[352,512]{1,0:T(8,128)(2,1)S(1)} %get-tuple-element.169), channel_id=1, source_target_pairs={{0,16},{1,17},{2,18},{3,19},{4,20},{5,21},{6,22},{7,23},{8,24},{9,... | collective-permute-start | bytes 1081352 | tf_op jit(solution)/shard_map/ppermute | solution.py:257
  75.9 9.9 %collective-permute-start.21 = (bf16[352,512]{1,0:T(8,128)(2,1)S(1)}, bf16[352,512]{1,0:T(8,128)(2,1)S(1)}, u32[]{:S(2)}, u32[]{:S(2)}) collective-permute-start(bf16[352,512]{1,0:T(8,128)(2,1)S(1)} %get-tuple-element.171), channel_id=1, source_target_pairs={{0,8},{1,9},{2,10},{3,11},{4,12},{5,13},{6,14},{7,15},{8,0},{9,1},... | collective-permute-start | bytes 1081352 | tf_op jit(solution)/shard_map/ppermute | solution.py:257
  77.7 10.6 %collective-permute-start.19 = (bf16[336,512]{1,0:T(8,128)(2,1)S(1)}, bf16[336,512]{1,0:T(8,128)(2,1)S(1)}, u32[]{:S(2)}, u32[]{:S(2)}) collective-permute-start(bf16[336,512]{1,0:T(8,128)(2,1)S(1)} %get-tuple-element.167), channel_id=1, source_target_pairs={{0,4},{1,5},{2,6},{3,7},{4,0},{5,1},{6,2},{7,3},{8,12},{9,13},{10,... | collective-permute-start | bytes 1032200 | tf_op jit(solution)/shard_map/ppermute | solution.py:257
  80.8 11.0 %collective-permute-start.18 = (bf16[320,512]{1,0:T(8,128)(2,1)S(1)}, bf16[320,512]{1,0:T(8,128)(2,1)S(1)}, u32[]{:S(2)}, u32[]{:S(2)}) collective-permute-start(bf16[320,512]{1,0:T(8,128)(2,1)S(1)} %get-tuple-element.165), channel_id=1, source_target_pairs={{0,2},{1,3},{2,0},{3,1},{4,6},{5,7},{6,4},{7,5},{8,10},{9,11},{10,... | collective-permute-start | bytes 983048 | tf_op jit(solution)/shard_map/ppermute | solution.py:257
  82.2 12.2 %collective-permute-start.17 = (bf16[320,512]{1,0:T(8,128)(2,1)S(1)}, bf16[320,512]{1,0:T(8,128)(2,1)S(1)}, u32[]{:S(2)}, u32[]{:S(2)}) collective-permute-start(bf16[320,512]{1,0:T(8,128)(2,1)S(1)} %get-tuple-element.163), channel_id=1, source_target_pairs={{0,1},{1,0},{2,3},{3,2},{4,5},{5,4},{6,7},{7,6},{8,9},{9,8},{10,11... | collective-permute-start | bytes 983048 | tf_op jit(solution)/shard_map/ppermute | solution.py:257
  88.7 14.6 %collective-permute-start.25 = (bf16[336,512]{1,0:T(8,128)(2,1)S(1)}, bf16[336,512]{1,0:T(8,128)(2,1)S(1)}, u32[]{:S(2)}, u32[]{:S(2)}) collective-permute-start(bf16[336,512]{1,0:T(8,128)(2,1)S(1)} %get-tuple-element.185), channel_id=1, source_target_pairs={{0,8},{1,9},{2,10},{3,11},{4,12},{5,13},{6,14},{7,15},{8,0},{9,1},... | collective-permute-start | bytes 1032200 | tf_op jit(solution)/shard_map/ppermute | solution.py:257
  88.8 15.1 %collective-permute-start.24 = (bf16[352,512]{1,0:T(8,128)(2,1)S(1)}, bf16[352,512]{1,0:T(8,128)(2,1)S(1)}, u32[]{:S(2)}, u32[]{:S(2)}) collective-permute-start(bf16[352,512]{1,0:T(8,128)(2,1)S(1)} %get-tuple-element.183), channel_id=1, source_target_pairs={{0,16},{1,17},{2,18},{3,19},{4,20},{5,21},{6,22},{7,23},{8,24},{9,... | collective-permute-start | bytes 1081352 | tf_op jit(solution)/shard_map/ppermute | solution.py:257
  92.3 13.5 %collective-permute-start.23 = (bf16[320,512]{1,0:T(8,128)(2,1)S(1)}, bf16[320,512]{1,0:T(8,128)(2,1)S(1)}, u32[]{:S(2)}, u32[]{:S(2)}) collective-permute-start(bf16[320,512]{1,0:T(8,128)(2,1)S(1)} %get-tuple-element.181), channel_id=1, source_target_pairs={{0,4},{1,5},{2,6},{3,7},{4,0},{5,1},{6,2},{7,3},{8,12},{9,13},{10,... | collective-permute-start | bytes 983048 | tf_op jit(solution)/shard_map/ppermute | solution.py:257
  94.8 23.1 %collective-permute-start.22 = (bf16[320,512]{1,0:T(8,128)(2,1)S(1)}, bf16[320,512]{1,0:T(8,128)(2,1)S(1)}, u32[]{:S(2)}, u32[]{:S(2)}) collective-permute-start(bf16[320,512]{1,0:T(8,128)(2,1)S(1)} %get-tuple-element.179), channel_id=1, source_target_pairs={{0,2},{1,3},{2,0},{3,1},{4,6},{5,7},{6,4},{7,5},{8,10},{9,11},{10,... | collective-permute-start | bytes 983048 | tf_op jit(solution)/shard_map/ppermute | solution.py:257
  103.8 24.9 %collective-permute-start.27 = (bf16[336,512]{1,0:T(8,128)(2,1)S(1)}, bf16[336,512]{1,0:T(8,128)(2,1)S(1)}, u32[]{:S(2)}, u32[]{:S(2)}) collective-permute-start(bf16[336,512]{1,0:T(8,128)(2,1)S(1)} %get-tuple-element.194), channel_id=1, source_target_pairs={{0,16},{1,17},{2,18},{3,19},{4,20},{5,21},{6,22},{7,23},{8,24},{9,... | collective-permute-start | bytes 1032200 | tf_op jit(solution)/shard_map/ppermute | solution.py:257
  106.3 22.0 %collective-permute-start.28 = (bf16[320,512]{1,0:T(8,128)(2,1)S(1)}, bf16[320,512]{1,0:T(8,128)(2,1)S(1)}, u32[]{:S(2)}, u32[]{:S(2)}) collective-permute-start(bf16[320,512]{1,0:T(8,128)(2,1)S(1)} %get-tuple-element.196), channel_id=1, source_target_pairs={{0,8},{1,9},{2,10},{3,11},{4,12},{5,13},{6,14},{7,15},{8,0},{9,1},... | collective-permute-start | bytes 983048 | tf_op jit(solution)/shard_map/ppermute | solution.py:257
  118.3 12.3 %collective-permute-start.26 = (bf16[320,512]{1,0:T(8,128)(2,1)S(1)}, bf16[320,512]{1,0:T(8,128)(2,1)S(1)}, u32[]{:S(2)}, u32[]{:S(2)}) collective-permute-start(bf16[320,512]{1,0:T(8,128)(2,1)S(1)} %get-tuple-element.192), channel_id=1, source_target_pairs={{0,4},{1,5},{2,6},{3,7},{4,0},{5,1},{6,2},{7,3},{8,12},{9,13},{10,... | collective-permute-start | bytes 983048 | tf_op jit(solution)/shard_map/ppermute | solution.py:257
  131.1 16.5 %collective-permute-start.29 = (bf16[320,512]{1,0:T(8,128)(2,1)S(1)}, bf16[320,512]{1,0:T(8,128)(2,1)S(1)}, u32[]{:S(2)}, u32[]{:S(2)}) collective-permute-start(bf16[320,512]{1,0:T(8,128)(2,1)S(1)} %get-tuple-element.202), channel_id=1, source_target_pairs={{0,8},{1,9},{2,10},{3,11},{4,12},{5,13},{6,14},{7,15},{8,0},{9,1},... | collective-permute-start | bytes 983048 | tf_op jit(solution)/shard_map/ppermute | solution.py:257
  131.2 18.2 %collective-permute-start.31 = (bf16[320,512]{1,0:T(8,128)(2,1)S(1)}, bf16[320,512]{1,0:T(8,128)(2,1)S(1)}, u32[]{:S(2)}, u32[]{:S(2)}) collective-permute-start(bf16[320,512]{1,0:T(8,128)(2,1)S(1)} %get-tuple-element.207), channel_id=1, source_target_pairs={{0,16},{1,17},{2,18},{3,19},{4,20},{5,21},{6,22},{7,23},{8,24},{9,... | collective-permute-start | bytes 983048 | tf_op jit(solution)/shard_map/ppermute | solution.py:257
  148.0 15.8 %collective-permute-start.30 = (bf16[320,512]{1,0:T(8,128)(2,1)S(1)}, bf16[320,512]{1,0:T(8,128)(2,1)S(1)}, u32[]{:S(2)}, u32[]{:S(2)}) collective-permute-start(bf16[320,512]{1,0:T(8,128)(2,1)S(1)} %get-tuple-element.205), channel_id=1, source_target_pairs={{0,16},{1,17},{2,18},{3,19},{4,20},{5,21},{6,22},{7,23},{8,24},{9,... | collective-permute-start | bytes 983048 | tf_op jit(solution)/shard_map/ppermute | solution.py:257

commit v2 on v1

v2 whole, which is shorter than its diff:
```python
import functools

import jax
import jax.numpy as jnp
from jax import lax
from jax.experimental import pallas as pl
from jax.experimental.pallas import tpu as pltpu
from jax.sharding import PartitionSpec as P

BF16 = jnp.bfloat16
F32 = jnp.float32
SHARES = (12, 17, 20, 22, 23, 20, 14)


def dot(a, b):
    return jnp.dot(a, b, preferred_element_type=F32)


def cut(rows, shares):
    ends = [rows * sum(shares[: at + 1]) // sum(shares) // 16 * 16 for at in range(len(shares))]
    ends[-1] = rows
    starts = [0] + ends[:-1]
    return [(start, end - start) for start, end in zip(starts, ends)]


def order_of(pieces, inward):
    count = len(pieces)
    order = [("leaf", pieces[0]), ("level", pieces[0], 1), ("leaf", pieces[1]), ("swap rims",)]
    for turn in range(2, count + inward + 2):
        new, old = turn - inward, turn - inward - 2
        if turn == inward:
            order.append(("take",))
        if new >= 0 and new != 1:
            order.append(("turn", pieces[new] if new < count else None, pieces[old] if old >= 0 else None))
        for level in range(inward - 1, 0, -1):
            if turn == inward + 1 and level == 1:
                order.append(("take",))
            if 0 <= turn - level < count:
                order.append(("level", pieces[turn - level], level))
        if turn == inward:
            order += [("pass rims",), ("turn", pieces[1], None), ("relay", pieces[new])]
        if turn == inward + 1:
            order.append(("relay", pieces[new]))
        if turn < count:
            order.append(("leaf", pieces[turn]))
        if inward + 1 < turn and new < count:
            order.append(("relay", pieces[new]))
        if old >= 0:
            order.append(("last", pieces[old]))
    return order


def copies(pairs, sems):
    return [pltpu.make_async_copy(src, dst, sems.at[at]) for at, (src, dst) in enumerate(pairs)]


def blocks_of(size):
    step = 128
    return [(at, min(step, size - at)) for at in range(0, size, step)]


def leaf_rows(src, leaf, stay, cross, held, sent, rows):
    points, rank = leaf.shape[1:]
    grown = [
        dot(src[rows, b * points : (b + 1) * points].astype(BF16), leaf[b]).astype(BF16) for b in range(2)
    ]
    for b in range(2):
        cols = slice(b * rank, (b + 1) * rank)
        mixed = (dot(grown[b], stay[0, b]) + dot(grown[1 - b], cross[0, 1 - b])).astype(BF16)
        held[:, cols] = mixed
        sent[:, cols] = dot(mixed, cross[1, b]).astype(BF16)


def first_leaf_step(size, level, src, leaf, stay, cross, prev, held, sent, packed, token, rows, leaf_in, stay_in, cross_in, sems):
    moves = copies(
        [
            *[(src.at[pl.ds(at, n)], rows.at[pl.ds(at, n)]) for at, n in blocks_of(size)],
            (leaf.at[0], leaf_in.at[0]),
            (leaf.at[1], leaf_in.at[1]),
            (stay.at[pl.ds(0, 1)], stay_in),
            (cross.at[pl.ds(0, 2)], cross_in),
            (cross.at[pl.ds(level, 2)], packed.at[pl.ds(0, 2)]),
            (stay.at[pl.ds(level, 2)], packed.at[pl.ds(2, 2)]),
        ],
        sems,
    )
    for move in moves:
        move.start()
    for move in moves[:-2]:
        move.wait()
    leaf_rows(rows, leaf_in, stay_in, cross_in, held, sent, slice(None))
    for move in moves[-2:]:
        move.wait()
    token[...] = jnp.zeros_like(token)


def leaf_step(start, size, src, leaf, stay, cross, prev, *outs):
    held, sent, token = outs[-3:]
    leaf_rows(src, leaf, stay, cross, held, sent, slice(start, start + size))
    token[...] = jnp.zeros_like(token)


def mix(held, moved, block):
    return (dot(held, block) + moved.astype(F32)).astype(BF16)


def level_step(level, held_in, moved, stay, cross, prev, held, sent, token):
    rank = stay.shape[-1]
    for b in range(2):
        cols = slice(b * rank, (b + 1) * rank)
        mixed = mix(held_in[:, cols], moved[:, cols], stay[level, b])
        held[:, cols] = mixed
        sent[:, cols] = dot(mixed, cross[level + 1, b]).astype(BF16)
    token[...] = jnp.zeros_like(token)


def relay_step(level, own, other, stay, cross, theirs_in, prev, own_out, other_out, sent, token):
    rank = stay.shape[-1]
    width = 2 * rank
    size = own.shape[0]
    for b in range(2):
        cols = slice(b * rank, (b + 1) * rank)
        mine, theirs = own[:, cols], other[:size, cols]
        theirs_mixed = (dot(theirs, theirs_in[2, b]) + dot(mine, cross[level, b])).astype(BF16)
        sent[:, cols] = dot(theirs_mixed, theirs_in[1, b]).astype(BF16)
        other_out[:, cols] = theirs_mixed
        mine_mixed = (dot(mine, stay[level, b]) + dot(theirs, theirs_in[0, b])).astype(BF16)
        sent[:, width + b * rank : width + (b + 1) * rank] = dot(mine_mixed, cross[level + 1, b]).astype(BF16)
        own_out[:, cols] = mine_mixed
    token[...] = jnp.zeros_like(token)


def inward_step(level, held_in, moved, stay, prev, held, token):
    rank = stay.shape[-1]
    for b in range(2):
        cols = slice(b * rank, (b + 1) * rank)
        held[:, cols] = mix(held_in[:, cols], moved[:, cols], stay[level, b])
    token[...] = jnp.zeros_like(token)


def turn_step(quarter, level, new, old, *refs):
    refs = list(refs)
    if new:
        held_in, moved = refs.pop(0), refs.pop(0)
    if old:
        own, other, across, theirs_in = (refs.pop(0) for _ in range(4))
    stay, prev = refs.pop(0), refs.pop(0)
    token = refs.pop()
    rank = stay.shape[-1]
    width = 2 * rank
    me = lax.axis_index("box")
    inner = jnp.logical_and(me >= quarter, me < 3 * quarter)
    sent = refs.pop()
    for b in range(2):
        cols = slice(b * rank, (b + 1) * rank)
        shifted = slice(width + b * rank, width + (b + 1) * rank)
        if new:
            going_in = mix(held_in[:, cols], moved[:, cols], stay[level - 2, b])
            refs[0][:, cols] = going_in
        if old:
            refs[-1][:, cols] = mix(own[:, cols], across[:, cols], stay[level, b])
            going_out = mix(other[:, cols], across[:, shifted], theirs_in[3, b])
        if new and old:
            both = min(new, old)
            sent[:both, cols] = jnp.where(inner, going_out[:both], going_in[:both])
            if new > both:
                sent[both:, cols] = going_in[both:]
            if old > both:
                sent[both:, cols] = going_out[both:]
        elif old:
            sent[:, cols] = going_out
    token[...] = jnp.zeros_like(token)


def last_step(quarter, start, size, own, back, out_basis, near, src, rim_a, rim_b, prev, *refs):
    out, token, window, result, sems = refs[-5:]
    rank, points = out_basis.shape[1:]
    rim = rim_a.shape[1]
    blocks = blocks_of(size)
    me = lax.axis_index("box")
    odd = lax.rem(me, 2) == 1
    inner = jnp.logical_and(me >= quarter, me < 3 * quarter)
    leaves = copies([(result.at[pl.ds(at, n)], out.at[pl.ds(start + at, n)]) for at, n in blocks], sems)
    for leave, (at, n) in zip(leaves, blocks):
        part, whole = slice(at, at + n), slice(start + at, start + at + n)
        before, after = jnp.where(odd, rim_a[whole], rim_b[whole]), jnp.where(odd, rim_b[whole], rim_a[whole])
        window[part, :rim] = before
        window[part, rim : rim + 2 * points] = src[whole].astype(BF16)
        window[part, rim + 2 * points :] = after
        for b in range(2):
            cols = slice(b * rank, (b + 1) * rank)
            mixed = jnp.where(inner, own[part, cols], back[part, cols])
            result[part, b * points : (b + 1) * points] = dot(mixed, out_basis[b]) + dot(
                window[part, b * points : (b + 1) * points + 2 * rim], near[b]
            )
        leave.start()
    for leave in leaves:
        leave.wait()
    token[...] = jnp.zeros_like(token)


def rim_step(swap, src, prev, to, token):
    rim = to.shape[1]
    odd = lax.rem(lax.axis_index("box"), 2) == int(swap)
    head, tail = src[:, :rim].astype(BF16), src[:, src.shape[1] - rim :].astype(BF16)
    to[...] = jnp.where(odd, head, tail)
    token[...] = jnp.zeros_like(token)


def take_step(*refs):
    token = refs[-1]
    token[...] = jnp.zeros_like(token)


ANY = pl.BlockSpec(memory_space=pl.ANY)
VMEM = pl.BlockSpec(memory_space=pltpu.VMEM)
TOKEN = jax.ShapeDtypeStruct((8, 128), F32)
SOME = pl.CostEstimate(flops=3 * 10**9, bytes_accessed=1, transcendentals=0)
LITTLE = pl.CostEstimate(flops=10**7, bytes_accessed=1, transcendentals=0)


LIGHT = ("last", "relay")


def call(body, operands, in_specs, out_shape, out_specs, scratch, name, mib, aliases=None):
    return pl.pallas_call(
        body,
        in_specs=in_specs,
        out_specs=out_specs,
        out_shape=out_shape,
        scratch_shapes=scratch,
        input_output_aliases=aliases or {},
        compiler_params=pltpu.CompilerParams(vmem_limit_bytes=mib * 1024 * 1024),
        cost_estimate=LITTLE if name in LIGHT else SOME,
        name=name,
    )(*operands)


def per_device(sources, leaf_basis, stay_blocks, cross_blocks, out_basis, near_blocks):
    rows, points = sources.shape
    levels, _, rank, _ = stay_blocks.shape
    devices = lax.axis_size("box")
    quarter = devices // 4
    inward = levels - 3
    rim = (near_blocks.shape[1] - near_blocks.shape[2]) // 2
    pieces = cut(rows, SHARES)
    array = lambda *shape: jax.ShapeDtypeStruct(shape, BF16)
    sems = lambda count: pltpu.SemaphoreType.DMA((count,))
    in_hbm = lambda operand: pltpu.with_memory_space_constraint(operand, pltpu.HBM)
    apart = lambda gap: [(i, i ^ gap) for i in range(devices)]
    across = [
        (i, i ^ 3 * quarter if quarter <= i < 3 * quarter else i ^ 1) for i in range(devices)
    ]
    next_over = [(i, (i - 1 ^ 1) + 1) for i in range(1, devices - 1)]
    send = lambda operand, pairs: lax.ppermute(operand, "box", pairs)
    small = tuple(stay_blocks.shape[1:])

    token = jnp.zeros(TOKEN.shape, TOKEN.dtype)
    out, rim_a, rim_b, waiting, theirs = (None,) * 5
    held, moved, kept, across_in, swapped = {}, {}, {}, {}, {}
    for step, *rest in order_of(pieces, inward):
        piece = rest[0] if rest else None
        start, size = piece or (0, rows)
        pair = array(size, 2 * rank)
        if step == "leaf" and start == 0:
            held[1, piece], sent, packed, token = call(
                functools.partial(first_leaf_step, size, levels - 2),
                (*map(in_hbm, (sources, leaf_basis, stay_blocks, cross_blocks)), token),
                [ANY] * 5, [pair, pair, array(4, *small), TOKEN], [VMEM] * 4,
                [pltpu.VMEM((size, points), F32), pltpu.VMEM(leaf_basis.shape, BF16),
                 pltpu.VMEM((1,) + small, BF16), pltpu.VMEM((2,) + small, BF16), sems(6 + len(blocks_of(size)))],
                "leaf", 16,
            )
            moved[1, piece] = send(sent, apart(1))
            theirs = send(packed, apart(quarter))
        elif step == "leaf":
            held[1, piece], sent, token = call(
                functools.partial(leaf_step, start, size),
                (sources, leaf_basis, stay_blocks, cross_blocks, token),
                [VMEM] * 4 + [ANY], [pair, pair, TOKEN], [VMEM] * 3, [], "leaf", 16,
            )
            moved[1, piece] = send(sent, apart(1))
        elif step == "level":
            level = rest[1]
            held[level + 1, piece], sent, token = call(
                functools.partial(level_step, level),
                (held.pop((level, piece)), moved.pop((level, piece)), stay_blocks, cross_blocks, token),
                [VMEM] * 4 + [ANY], [pair, pair, TOKEN], [VMEM] * 3, [], "level", 16,
            )
            moved[level + 1, piece] = send(sent, apart(1 << level))
        elif step == "turn":
            old = rest[1]
            operands, results = (), []
            if piece:
                operands += held.pop((inward, piece)), moved.pop((inward, piece))
                results.append(pair)
            if old:
                operands += (*kept.pop(old), across_in.pop(old), theirs)
                results.append(array(old[1], 2 * rank))
            if old or not piece:
                results.append(array(max(size if piece else 0, old[1]), 2 * rank))
            *results, token = call(
                functools.partial(turn_step, quarter, levels - 1, size if piece else 0, old[1] if old else 0)
                if old else functools.partial(inward_step, levels - 3),
                (*operands, stay_blocks, token),
                [VMEM] * (len(operands) + 1) + [ANY], results + [TOKEN], [VMEM] * (len(results) + 1), [], "turn", 16,
            )
            message = send(results[-1], apart(quarter))
            if piece:
                swapped[piece] = results[0], message
            if old:
                kept[old] = results[-2], message
        elif step == "relay":
            own, arrived = swapped.pop(piece)
            own, other, sent, token = call(
                functools.partial(relay_step, levels - 2),
                (own, arrived, stay_blocks, cross_blocks, theirs, token),
                [VMEM] * 5 + [ANY], [pair, pair, array(size, 4 * rank), TOKEN], [VMEM] * 4, [], "relay", 16,
            )
            kept[piece] = own, other
            across_in[piece] = send(sent, across)
        elif step == "last":
            operands = [*kept.pop(piece), out_basis, near_blocks, sources, rim_a, rim_b, token]
            in_specs = [VMEM] * 7 + [ANY]
            aliases = {}
            if out is not None:
                operands.append(out)
                in_specs.append(ANY)
                aliases = {8: 0}
            out, token = call(
                functools.partial(last_step, quarter, start, size),
                operands, in_specs,
                [jax.ShapeDtypeStruct((rows, points), F32), TOKEN],
                [pl.BlockSpec(memory_space=pltpu.HBM), VMEM],
                [pltpu.VMEM((size, points + 2 * rim), BF16), pltpu.VMEM((size, points), F32),
                 sems(len(blocks_of(size)))],
                "last", 16, aliases,
            )
        elif step == "take":
            (token,) = call(take_step, (waiting, token), [ANY] * 2, [TOKEN], [VMEM], [], "take", 8)
        else:
            swap = step == "swap rims"
            to, token = call(
                functools.partial(rim_step, swap), (sources, token), [VMEM, ANY], [array(rows, rim), TOKEN],
                [VMEM] * 2, [], "rims", 8,
            )
            waiting = send(to, apart(1) if swap else next_over)
            rim_a, rim_b = (waiting, None) if swap else (rim_a, waiting)
    return out


def solution(mesh):
    in_specs = (
        P(None, "box"),
        P("box", None, None),
        P(None, "box", None, None),
        P(None, "box", None, None),
        P("box", None, None),
        P("box", None, None),
    )
    out_specs = P(None, "box")
    return jax.shard_map(
        per_device, mesh=mesh, in_specs=in_specs, out_specs=out_specs, check_vma=False
    )
```

time: 167 us -> 145 us (0.87)
  waiting for transfers between devices: 85.1 us -> 51 us
  Pallas kernels: 30.8 us -> 39.3 us
  starting transfers between devices: 49.9 us -> 53.6 us
    ppermute x32 -> x40, waiting for transfers between devices: 85.1 us -> 51 us  [per_device(): send = lambda operand, pairs: lax.ppermute(operand, 'box', pairs)]
    pallas_call x37 -> x48, Pallas kernels: 30.8 us -> 39.3 us  [call(): pl.pallas_call(body, in_specs=in_specs, out_specs=out_specs, out_shape=ou...]
    ppermute x32 -> x40, starting transfers between devices: 49.9 us -> 53.6 us  [per_device(): send = lambda operand, pairs: lax.ppermute(operand, 'box', pairs)]
  transfers between devices with their start and end apart: 32 -> 40, of which waited for: 14 -> 14; matrix products, arithmetic and copies ran while one was open for 0% -> 0% of each run, Pallas kernels for 15% -> 24%
where the time goes in v2:
time: 145 us
  starting transfers between devices  53.6 us (37%)
  waiting for transfers between devices  51 us (35%)
  Pallas kernels  39.3 us (27%)
    ppermute x40, starting transfers between devices, per_device(): send = lambda operand, pairs: lax.ppermute(operand, 'box', pairs)  53.6 us
    ppermute x40, waiting for transfers between devices, per_device(): send = lambda operand, pairs: lax.ppermute(operand, 'box', pairs)  51 us
    pallas_call x48, Pallas kernels, call(): pl.pallas_call(body, in_specs=in_specs, out_specs=out_specs, out_shape=ou...  39.3 us
  transfers between devices with their start and end apart: 40, of which 14 were waited for; matrix products, arithmetic and copies ran while one was open for 0% of the time, Pallas kernels for 24%

profile of v2, /device:TPU:0, one launch (start us, length us, event | category | flops | bytes accessed | tf_op | source)
XLA Modules:
  0.0 144.7 jit_solution(15081393062492922800)
XLA Ops:
  0.0 2.5 %leaf.14 = (bf16[192,512]{1,0:T(8,128)(2,1)S(1)}, bf16[192,512]{1,0:T(8,128)(2,1)S(1)}, bf16[4,2,256,256]{3,2,1,0:T(8,128)(2,1)S(1)}, f32[8,128]{1,0:T(8,128)S(1)}) custom-call(f32[2048,1024]{1,0:T(8,128)} %src.31, bf16[2,512,256]{2,1,0:T(8,128)(2,1)} %leaf.27, bf16[6,2,256,256]{3,2,1,0:T(8,128)(2,1)} %refs_4_.3, bf16[6,2,256,256]{3,2,1,0:T(8,128)(2,1)} %cross.55, ...), custom_call_target="tpu_custom_call" | custom-call | flops 3000000000 | bytes 1 | tf_op jit(solution)/shard_map/leaf/pallas_call | solution.py:226
  3.1 2.6 %collective-permute-start.9 = (bf16[4,2,256,256]{3,2,1,0:T(8,128)(2,1)S(1)}, bf16[4,2,256,256]{3,2,1,0:T(8,128)(2,1)S(1)}, u32[]{:S(2)}, u32[]{:S(2)}) collective-permute-start(bf16[4,2,256,256]{3,2,1,0:T(8,128)(2,1)S(1)} %get-tuple-element.171), channel_id=1, source_target_pairs={{0,8},{1,9},{2,10},{3,11},{4,12},{5,13},{6,14},{7,15},{8,0},{9,1},... | collective-permute-start | bytes 3145736 | tf_op jit(solution)/shard_map/ppermute | solution.py:255
  6.1 1.6 %collective-permute-start.2 = (bf16[192,512]{1,0:T(8,128)(2,1)S(1)}, bf16[192,512]{1,0:T(8,128)(2,1)S(1)}, u32[]{:S(2)}, u32[]{:S(2)}) collective-permute-start(bf16[192,512]{1,0:T(8,128)(2,1)S(1)} %get-tuple-element.151), channel_id=1, source_target_pairs={{0,2},{1,3},{2,0},{3,1},{4,6},{5,7},{6,4},{7,5},{8,10},{9,11},{10,... | collective-permute-start | bytes 589832 | tf_op jit(solution)/shard_map/ppermute | solution.py:255
  9.4 3.8 %collective-permute-done.2.moved = bf16[192,512]{1,0:T(8,128)(2,1)S(1)} collective-permute-done((bf16[192,512]{1,0:T(8,128)(2,1)S(1)}, bf16[192,512]{1,0:T(8,128)(2,1)S(1)}, u32[]{:S(2)}, u32[]{:S(2)}) %collective-permute-start.2) | collective-permute-done | bytes 196640 | tf_op jit(solution)/shard_map/ppermute | solution.py:255
  13.5 1.6 %collective-permute-start.4 = (bf16[192,512]{1,0:T(8,128)(2,1)S(1)}, bf16[192,512]{1,0:T(8,128)(2,1)S(1)}, u32[]{:S(2)}, u32[]{:S(2)}) collective-permute-start(bf16[192,512]{1,0:T(8,128)(2,1)S(1)} %get-tuple-element.158), channel_id=1, source_target_pairs={{0,4},{1,5},{2,6},{3,7},{4,0},{5,1},{6,2},{7,3},{8,12},{9,13},{10,... | collective-permute-start | bytes 589832 | tf_op jit(solution)/shard_map/ppermute | solution.py:255
  15.5 1.6 %collective-permute-start.3 = (bf16[272,512]{1,0:T(8,128)(2,1)S(1)}, bf16[272,512]{1,0:T(8,128)(2,1)S(1)}, u32[]{:S(2)}, u32[]{:S(2)}) collective-permute-start(bf16[272,512]{1,0:T(8,128)(2,1)S(1)} %get-tuple-element.156), channel_id=1, source_target_pairs={{0,2},{1,3},{2,0},{3,1},{4,6},{5,7},{6,4},{7,5},{8,10},{9,11},{10,... | collective-permute-start | bytes 835592 | tf_op jit(solution)/shard_map/ppermute | solution.py:255
  18.2 1.6 %collective-permute-done.4.moved = bf16[192,512]{1,0:T(8,128)(2,1)S(1)} collective-permute-done((bf16[192,512]{1,0:T(8,128)(2,1)S(1)}, bf16[192,512]{1,0:T(8,128)(2,1)S(1)}, u32[]{:S(2)}, u32[]{:S(2)}) %collective-permute-start.4) | collective-permute-done | bytes 196640 | tf_op jit(solution)/shard_map/ppermute | solution.py:255
  20.0 1.4 collective-permute-start.10
  21.3 1.9 %collective-permute-done.3.moved = bf16[272,512]{1,0:T(8,128)(2,1)S(1)} collective-permute-done((bf16[272,512]{1,0:T(8,128)(2,1)S(1)}, bf16[272,512]{1,0:T(8,128)(2,1)S(1)}, u32[]{:S(2)}, u32[]{:S(2)}) %collective-permute-start.3) | collective-permute-done | bytes 278560 | tf_op jit(solution)/shard_map/ppermute | solution.py:255
  24.7 1.6 %collective-permute-start.13 = (bf16[320,512]{1,0:T(8,128)(2,1)S(1)}, bf16[320,512]{1,0:T(8,128)(2,1)S(1)}, u32[]{:S(2)}, u32[]{:S(2)}) collective-permute-start(bf16[320,512]{1,0:T(8,128)(2,1)S(1)} %get-tuple-element.179), channel_id=1, source_target_pairs={{0,2},{1,3},{2,0},{3,1},{4,6},{5,7},{6,4},{7,5},{8,10},{9,11},{10,... | collective-permute-start | bytes 983048 | tf_op jit(solution)/shard_map/ppermute | solution.py:255
  27.3 3.2 %collective-permute-done.6.moved = bf16[272,512]{1,0:T(8,128)(2,1)S(1)} collective-permute-done((bf16[272,512]{1,0:T(8,128)(2,1)S(1)}, bf16[272,512]{1,0:T(8,128)(2,1)S(1)}, u32[]{:S(2)}, u32[]{:S(2)}) %collective-permute-start.6) | collective-permute-done | bytes 278560 | tf_op jit(solution)/shard_map/ppermute | solution.py:255
  30.6 1.3 collective-permute-start.8
  32.0 2.0 %collective-permute-done.10.other = bf16[192,512]{1,0:T(8,128)(2,1)S(1)} collective-permute-done((bf16[192,512]{1,0:T(8,128)(2,1)S(1)}, bf16[192,512]{1,0:T(8,128)(2,1)S(1)}, u32[]{:S(2)}, u32[]{:S(2)}) %collective-permute-start.10) | collective-permute-done | bytes 196640 | tf_op jit(solution)/shard_map/ppermute | solution.py:255
  34.0 1.0 relay.7
  37.1 2.0 %collective-permute-start.16 = (bf16[320,512]{1,0:T(8,128)(2,1)S(1)}, bf16[320,512]{1,0:T(8,128)(2,1)S(1)}, u32[]{:S(2)}, u32[]{:S(2)}) collective-permute-start(bf16[320,512]{1,0:T(8,128)(2,1)S(1)} %get-tuple-element.189), channel_id=1, source_target_pairs={{0,4},{1,5},{2,6},{3,7},{4,0},{5,1},{6,2},{7,3},{8,12},{9,13},{10,... | collective-permute-start | bytes 983048 | tf_op jit(solution)/shard_map/ppermute | solution.py:255
  39.5 5.9 %collective-permute-start.15 = (bf16[352,512]{1,0:T(8,128)(2,1)S(1)}, bf16[352,512]{1,0:T(8,128)(2,1)S(1)}, u32[]{:S(2)}, u32[]{:S(2)}) collective-permute-start(bf16[352,512]{1,0:T(8,128)(2,1)S(1)} %get-tuple-element.187), channel_id=1, source_target_pairs={{0,2},{1,3},{2,0},{3,1},{4,6},{5,7},{6,4},{7,5},{8,10},{9,11},{10,... | collective-permute-start | bytes 1081352 | tf_op jit(solution)/shard_map/ppermute | solution.py:255
  45.5 1.2 relay.8
  48.9 4.3 %collective-permute-start.22 = (bf16[320,512]{1,0:T(8,128)(2,1)S(1)}, bf16[320,512]{1,0:T(8,128)(2,1)S(1)}, u32[]{:S(2)}, u32[]{:S(2)}) collective-permute-start(bf16[320,512]{1,0:T(8,128)(2,1)S(1)} %get-tuple-element.207), channel_id=1, source_target_pairs={{0,8},{1,9},{2,10},{3,11},{4,12},{5,13},{6,14},{7,15},{8,0},{9,1},... | collective-permute-start | bytes 983048 | tf_op jit(solution)/shard_map/ppermute | solution.py:255
  53.2 1.4 collective-permute-done.15.moved
  55.5 2.2 %collective-permute-start.19 = (bf16[368,512]{1,0:T(8,128)(2,1)S(1)}, bf16[368,512]{1,0:T(8,128)(2,1)S(1)}, u32[]{:S(2)}, u32[]{:S(2)}) collective-permute-start(bf16[368,512]{1,0:T(8,128)(2,1)S(1)} %get-tuple-element.200), channel_id=1, source_target_pairs={{0,2},{1,3},{2,0},{3,1},{4,6},{5,7},{6,4},{7,5},{8,10},{9,11},{10,... | collective-permute-start | bytes 1130504 | tf_op jit(solution)/shard_map/ppermute | solution.py:255
  58.8 2.0 %collective-permute-done.22.other.back = bf16[320,512]{1,0:T(8,128)(2,1)S(1)} collective-permute-done((bf16[320,512]{1,0:T(8,128)(2,1)S(1)}, bf16[320,512]{1,0:T(8,128)(2,1)S(1)}, u32[]{:S(2)}, u32[]{:S(2)}) %collective-permute-start.22) | collective-permute-done | bytes 327712 | tf_op jit(solution)/shard_map/ppermute | solution.py:255
  60.8 1.3 relay.9
  62.2 1.5 %last.7 = (f32[2048,1024]{1,0:T(8,128)}, f32[8,128]{1,0:T(8,128)S(1)}) custom-call(bf16[192,512]{1,0:T(8,128)(2,1)S(1)} %get-tuple-element.206.own, bf16[320,512]{1,0:T(8,128)(2,1)S(1)} %collective-permute-done.22.other.back, bf16[2,256,512]{2,1,0:T(8,128)(2,1)S(1)} %copy-done.4, bf16[2,768,512]{2,1,0:T(8,128)(2,1)S(1)} %copy-done.2, ...), custom_call_target="tpu_custom_call" | custom-call | flops 10000000 | bytes 1 | tf_op jit(solution)/shard_map/last/pallas_call | solution.py:226
  63.8 1.9 %collective-permute-done.20.refs_1_ = bf16[352,512]{1,0:T(8,128)(2,1)S(1)} collective-permute-done((bf16[352,512]{1,0:T(8,128)(2,1)S(1)}, bf16[352,512]{1,0:T(8,128)(2,1)S(1)}, u32[]{:S(2)}, u32[]{:S(2)}) %collective-permute-start.20) | collective-permute-done | bytes 360480 | tf_op jit(solution)/shard_map/ppermute | solution.py:255
  67.3 1.6 %collective-permute-start.25 = (bf16[368,512]{1,0:T(8,128)(2,1)S(1)}, bf16[368,512]{1,0:T(8,128)(2,1)S(1)}, u32[]{:S(2)}, u32[]{:S(2)}) collective-permute-start(bf16[368,512]{1,0:T(8,128)(2,1)S(1)} %get-tuple-element.220), channel_id=1, source_target_pairs={{0,4},{1,5},{2,6},{3,7},{4,0},{5,1},{6,2},{7,3},{8,12},{9,13},{10,... | collective-permute-start | bytes 1130504 | tf_op jit(solution)/shard_map/ppermute | solution.py:255
  69.4 1.8 %collective-permute-start.24 = (bf16[320,512]{1,0:T(8,128)(2,1)S(1)}, bf16[320,512]{1,0:T(8,128)(2,1)S(1)}, u32[]{:S(2)}, u32[]{:S(2)}) collective-permute-start(bf16[320,512]{1,0:T(8,128)(2,1)S(1)} %get-tuple-element.218), channel_id=1, source_target_pairs={{0,2},{1,3},{2,0},{3,1},{4,6},{5,7},{6,4},{7,5},{8,10},{9,11},{10,... | collective-permute-start | bytes 983048 | tf_op jit(solution)/shard_map/ppermute | solution.py:255
  72.1 3.9 %collective-permute-done.27.other.back = bf16[352,512]{1,0:T(8,128)(2,1)S(1)} collective-permute-done((bf16[352,512]{1,0:T(8,128)(2,1)S(1)}, bf16[352,512]{1,0:T(8,128)(2,1)S(1)}, u32[]{:S(2)}, u32[]{:S(2)}) %collective-permute-start.27) | collective-permute-done | bytes 360480 | tf_op jit(solution)/shard_map/ppermute | solution.py:255
  76.0 1.4 relay.10
  77.4 1.7 %last.8 = (f32[2048,1024]{1,0:T(8,128)}, f32[8,128]{1,0:T(8,128)S(1)}) custom-call(bf16[272,512]{1,0:T(8,128)(2,1)S(1)} %get-tuple-element.224.own, bf16[352,512]{1,0:T(8,128)(2,1)S(1)} %collective-permute-done.27.other.back, bf16[2,256,512]{2,1,0:T(8,128)(2,1)S(1)} %copy-done.4, ...), custom_call_target="tpu_custom_call", output_to_operand_aliasing={{0}: (8, {})} | custom-call | flops 10000000 | bytes 1 | tf_op jit(solution)/shard_map/last/pallas_call | solution.py:226
  79.6 3.2 %collective-permute-start.31 = (bf16[368,512]{1,0:T(8,128)(2,1)S(1)}, bf16[368,512]{1,0:T(8,128)(2,1)S(1)}, u32[]{:S(2)}, u32[]{:S(2)}) collective-permute-start(bf16[368,512]{1,0:T(8,128)(2,1)S(1)} %get-tuple-element.241), channel_id=1, source_target_pairs={{0,8},{1,9},{2,10},{3,11},{4,12},{5,13},{6,14},{7,15},{8,0},{9,1},... | collective-permute-start | bytes 1130504 | tf_op jit(solution)/shard_map/ppermute | solution.py:255
  83.9 2.2 %collective-permute-start.28 = (bf16[224,512]{1,0:T(8,128)(2,1)S(1)}, bf16[224,512]{1,0:T(8,128)(2,1)S(1)}, u32[]{:S(2)}, u32[]{:S(2)}) collective-permute-start(bf16[224,512]{1,0:T(8,128)(2,1)S(1)} %get-tuple-element.234), channel_id=1, source_target_pairs={{0,2},{1,3},{2,0},{3,1},{4,6},{5,7},{6,4},{7,5},{8,10},{9,11},{10,... | collective-permute-start | bytes 688136 | tf_op jit(solution)/shard_map/ppermute | solution.py:255
  86.1 4.7 %collective-permute-done.31.other.back = bf16[368,512]{1,0:T(8,128)(2,1)S(1)} collective-permute-done((bf16[368,512]{1,0:T(8,128)(2,1)S(1)}, bf16[368,512]{1,0:T(8,128)(2,1)S(1)}, u32[]{:S(2)}, u32[]{:S(2)}) %collective-permute-start.31) | collective-permute-done | bytes 376864 | tf_op jit(solution)/shard_map/ppermute | solution.py:255
  90.8 1.4 relay.11
  92.3 1.8 %last.9 = (f32[2048,1024]{1,0:T(8,128)}, f32[8,128]{1,0:T(8,128)S(1)}) custom-call(bf16[320,512]{1,0:T(8,128)(2,1)S(1)} %get-tuple-element.240.own, bf16[368,512]{1,0:T(8,128)(2,1)S(1)} %collective-permute-done.31.other.back, bf16[2,256,512]{2,1,0:T(8,128)(2,1)S(1)} %copy-done.4, ...), custom_call_target="tpu_custom_call", output_to_operand_aliasing={{0}: (8, {})} | custom-call | flops 10000000 | bytes 1 | tf_op jit(solution)/shard_map/last/pallas_call | solution.py:226
  94.7 2.9 %collective-permute-start.34 = (bf16[352,512]{1,0:T(8,128)(2,1)S(1)}, bf16[352,512]{1,0:T(8,128)(2,1)S(1)}, u32[]{:S(2)}, u32[]{:S(2)}) collective-permute-start(bf16[352,512]{1,0:T(8,128)(2,1)S(1)} %get-tuple-element.254), channel_id=1, source_target_pairs={{0,8},{1,9},{2,10},{3,11},{4,12},{5,13},{6,14},{7,15},{8,0},{9,1},... | collective-permute-start | bytes 1081352 | tf_op jit(solution)/shard_map/ppermute | solution.py:255
  98.0 1.4 collective-permute-start.32
  99.4 6.1 %collective-permute-done.34.other.back = bf16[352,512]{1,0:T(8,128)(2,1)S(1)} collective-permute-done((bf16[352,512]{1,0:T(8,128)(2,1)S(1)}, bf16[352,512]{1,0:T(8,128)(2,1)S(1)}, u32[]{:S(2)}, u32[]{:S(2)}) %collective-permute-start.34) | collective-permute-done | bytes 360480 | tf_op jit(solution)/shard_map/ppermute | solution.py:255
  105.5 1.3 relay.12
  106.9 1.9 %last.10 = (f32[2048,1024]{1,0:T(8,128)}, f32[8,128]{1,0:T(8,128)S(1)}) custom-call(bf16[352,512]{1,0:T(8,128)(2,1)S(1)} %get-tuple-element.253.own, bf16[352,512]{1,0:T(8,128)(2,1)S(1)} %collective-permute-done.34.other.back, bf16[2,256,512]{2,1,0:T(8,128)(2,1)S(1)} %copy-done.4, ...), custom_call_target="tpu_custom_call", output_to_operand_aliasing={{0}: (8, {})} | custom-call | flops 10000000 | bytes 1 | tf_op jit(solution)/shard_map/last/pallas_call | solution.py:226
  109.3 4.4 %collective-permute-start.35 = (bf16[368,512]{1,0:T(8,128)(2,1)S(1)}, bf16[368,512]{1,0:T(8,128)(2,1)S(1)}, u32[]{:S(2)}, u32[]{:S(2)}) collective-permute-start(bf16[368,512]{1,0:T(8,128)(2,1)S(1)} %get-tuple-element.261), channel_id=1, source_target_pairs={{0,8},{1,9},{2,10},{3,11},{4,12},{5,13},{6,14},{7,15},{8,0},{9,1},... | collective-permute-start | bytes 1130504 | tf_op jit(solution)/shard_map/ppermute | solution.py:255
  113.7 6.8 %collective-permute-done.35.other.back = bf16[368,512]{1,0:T(8,128)(2,1)S(1)} collective-permute-done((bf16[368,512]{1,0:T(8,128)(2,1)S(1)}, bf16[368,512]{1,0:T(8,128)(2,1)S(1)}, u32[]{:S(2)}, u32[]{:S(2)}) %collective-permute-start.35) | collective-permute-done | bytes 376864 | tf_op jit(solution)/shard_map/ppermute | solution.py:255
  120.5 1.1 relay.13
  121.7 1.9 %last.11 = (f32[2048,1024]{1,0:T(8,128)}, f32[8,128]{1,0:T(8,128)S(1)}) custom-call(bf16[368,512]{1,0:T(8,128)(2,1)S(1)} %get-tuple-element.269.own, bf16[368,512]{1,0:T(8,128)(2,1)S(1)} %collective-permute-done.35.other.back, bf16[2,256,512]{2,1,0:T(8,128)(2,1)S(1)} %copy-done.4, ...), custom_call_target="tpu_custom_call", output_to_operand_aliasing={{0}: (8, {})} | custom-call | flops 10000000 | bytes 1 | tf_op jit(solution)/shard_map/last/pallas_call | solution.py:226
  123.9 3.8 %collective-permute-start.38 = (bf16[320,512]{1,0:T(8,128)(2,1)S(1)}, bf16[320,512]{1,0:T(8,128)(2,1)S(1)}, u32[]{:S(2)}, u32[]{:S(2)}) collective-permute-start(bf16[320,512]{1,0:T(8,128)(2,1)S(1)} %get-tuple-element.274), channel_id=1, source_target_pairs={{0,8},{1,9},{2,10},{3,11},{4,12},{5,13},{6,14},{7,15},{8,0},{9,1},... | collective-permute-start | bytes 983048 | tf_op jit(solution)/shard_map/ppermute | solution.py:255
  127.7 6.4 %collective-permute-done.38.back = bf16[320,512]{1,0:T(8,128)(2,1)S(1)} collective-permute-done((bf16[320,512]{1,0:T(8,128)(2,1)S(1)}, bf16[320,512]{1,0:T(8,128)(2,1)S(1)}, u32[]{:S(2)}, u32[]{:S(2)}) %collective-permute-start.38) | collective-permute-done | bytes 327712 | tf_op jit(solution)/shard_map/ppermute | solution.py:255
  134.1 1.8 %last.12 = (f32[2048,1024]{1,0:T(8,128)}, f32[8,128]{1,0:T(8,128)S(1)}) custom-call(bf16[320,512]{1,0:T(8,128)(2,1)S(1)} %get-tuple-element.273.own, bf16[320,512]{1,0:T(8,128)(2,1)S(1)} %collective-permute-done.38.back, bf16[2,256,512]{2,1,0:T(8,128)(2,1)S(1)} %copy-done.4, bf16[2,768,512]{2,1,0:T(8,128)(2,1)S(1)} %copy-done.2, ...), custom_call_target="tpu_custom_call", output_to_operand_aliasing={{0}: (8, {})} | custom-call | flops 10000000 | bytes 1 | tf_op jit(solution)/shard_map/last/pallas_call | solution.py:226
  137.0 5.4 %collective-permute-done.39.back = bf16[224,512]{1,0:T(8,128)(2,1)S(1)} collective-permute-done((bf16[224,512]{1,0:T(8,128)(2,1)S(1)}, bf16[224,512]{1,0:T(8,128)(2,1)S(1)}, u32[]{:S(2)}, u32[]{:S(2)}) %collective-permute-start.39) | collective-permute-done | bytes 229408 | tf_op jit(solution)/shard_map/ppermute | solution.py:255
  142.3 2.2 %last.13 = (f32[2048,1024]{1,0:T(8,128)}, f32[8,128]{1,0:T(8,128)}) custom-call(bf16[224,512]{1,0:T(8,128)(2,1)S(1)} %get-tuple-element.278.own, bf16[224,512]{1,0:T(8,128)(2,1)S(1)} %collective-permute-done.39.back, bf16[2,256,512]{2,1,0:T(8,128)(2,1)S(1)} %copy-done.4, bf16[2,768,512]{2,1,0:T(8,128)(2,1)S(1)} %copy-done.2, ...), custom_call_target="tpu_custom_call", output_to_operand_aliasing={{0}: (8, {})} | custom-call | flops 10000000 | bytes 1 | tf_op jit(solution)/shard_map/last/pallas_call | solution.py:226
  (96 shorter events, 21.5 us)
Async XLA Ops:
  0.0 5.7 %copy-start.1 = (bf16[6,2,256,256]{3,2,1,0:T(8,128)(2,1)S(1)}, bf16[6,2,256,256]{3,2,1,0:T(8,128)(2,1)}, u32[]{:S(2)}) copy-start(bf16[6,2,256,256]{3,2,1,0:T(8,128)(2,1)} %refs_4_.3) | copy-start | bytes 4718596
  0.0 5.7 %copy-start = (bf16[6,2,256,256]{3,2,1,0:T(8,128)(2,1)S(1)}, bf16[6,2,256,256]{3,2,1,0:T(8,128)(2,1)}, u32[]{:S(2)}) copy-start(bf16[6,2,256,256]{3,2,1,0:T(8,128)(2,1)} %cross.55) | copy-start | bytes 4718596
  0.0 7.7 %slice-start = ((s8[8388608]{0:T(1024)(128)(4,1)}), s8[4194304]{0:T(1024)(128)(4,1)S(1)}, s32[]{:S(2)}) async-start(s8[8388608]{0:T(1024)(128)(4,1)} %bitcast), calls=%async_computation | async-start | bytes 8388608
  0.0 7.7 %slice-start.1 = ((s8[8388608]{0:T(1024)(128)(4,1)}), s8[4194304]{0:T(1024)(128)(4,1)S(1)}, s32[]{:S(2)}) async-start(s8[8388608]{0:T(1024)(128)(4,1)} %bitcast), calls=%async_computation.1 | async-start | bytes 8388608
  2.6 5.1 %copy-start.3 = (bf16[2,512,256]{2,1,0:T(8,128)(2,1)S(1)}, bf16[2,512,256]{2,1,0:T(8,128)(2,1)}, u32[]{:S(2)}) copy-start(bf16[2,512,256]{2,1,0:T(8,128)(2,1)} %leaf.27) | copy-start | bytes 1572868
  2.6 3.2 %collective-permute-start = (bf16[192,512]{1,0:T(8,128)(2,1)S(1)}, bf16[192,512]{1,0:T(8,128)(2,1)S(1)}, u32[]{:S(2)}, u32[]{:S(2)}) collective-permute-start(bf16[192,512]{1,0:T(8,128)(2,1)S(1)} %get-tuple-element.145), channel_id=1, source_target_pairs={{0,1},{1,0},{2,3},{3,2},{4,5},{5,4},{6,7},{7,6},{8,9},{9,8},{10,11... | collective-permute-start | bytes 589832 | tf_op jit(solution)/shard_map/ppermute | solution.py:255
  3.1 30.9 %collective-permute-start.9 = (bf16[4,2,256,256]{3,2,1,0:T(8,128)(2,1)S(1)}, bf16[4,2,256,256]{3,2,1,0:T(8,128)(2,1)S(1)}, u32[]{:S(2)}, u32[]{:S(2)}) collective-permute-start(bf16[4,2,256,256]{3,2,1,0:T(8,128)(2,1)S(1)} %get-tuple-element.171), channel_id=1, source_target_pairs={{0,8},{1,9},{2,10},{3,11},{4,12},{5,13},{6,14},{7,15},{8,0},{9,1},... | collective-permute-start | bytes 3145736 | tf_op jit(solution)/shard_map/ppermute | solution.py:255
  6.1 7.0 %collective-permute-start.2 = (bf16[192,512]{1,0:T(8,128)(2,1)S(1)}, bf16[192,512]{1,0:T(8,128)(2,1)S(1)}, u32[]{:S(2)}, u32[]{:S(2)}) collective-permute-start(bf16[192,512]{1,0:T(8,128)(2,1)S(1)} %get-tuple-element.151), channel_id=1, source_target_pairs={{0,2},{1,3},{2,0},{3,1},{4,6},{5,7},{6,4},{7,5},{8,10},{9,11},{10,... | collective-permute-start | bytes 589832 | tf_op jit(solution)/shard_map/ppermute | solution.py:255
  8.6 6.5 %collective-permute-start.1 = (bf16[272,512]{1,0:T(8,128)(2,1)S(1)}, bf16[272,512]{1,0:T(8,128)(2,1)S(1)}, u32[]{:S(2)}, u32[]{:S(2)}) collective-permute-start(bf16[272,512]{1,0:T(8,128)(2,1)S(1)} %get-tuple-element.149), channel_id=1, source_target_pairs={{0,1},{1,0},{2,3},{3,2},{4,5},{5,4},{6,7},{7,6},{8,9},{9,8},{10,11... | collective-permute-start | bytes 835592 | tf_op jit(solution)/shard_map/ppermute | solution.py:255
  8.8 9.3 %collective-permute-start.5 = (bf16[2048,128]{1,0:T(8,128)(2,1)S(1)}, bf16[2048,128]{1,0:T(8,128)(2,1)S(1)}, u32[]{:S(2)}, u32[]{:S(2)}) collective-permute-start(bf16[2048,128]{1,0:T(8,128)(2,1)S(1)} %get-tuple-element.159), channel_id=1, source_target_pairs={{0,1},{1,0},{2,3},{3,2},{4,5},{5,4},{6,7},{7,6},{8,9},{9,8},{10,11... | collective-permute-start | bytes 1572872 | tf_op jit(solution)/shard_map/ppermute | solution.py:255
  13.5 6.2 %collective-permute-start.4 = (bf16[192,512]{1,0:T(8,128)(2,1)S(1)}, bf16[192,512]{1,0:T(8,128)(2,1)S(1)}, u32[]{:S(2)}, u32[]{:S(2)}) collective-permute-start(bf16[192,512]{1,0:T(8,128)(2,1)S(1)} %get-tuple-element.158), channel_id=1, source_target_pairs={{0,4},{1,5},{2,6},{3,7},{4,0},{5,1},{6,2},{7,3},{8,12},{9,13},{10,... | collective-permute-start | bytes 589832 | tf_op jit(solution)/shard_map/ppermute | solution.py:255
  15.5 7.7 %collective-permute-start.3 = (bf16[272,512]{1,0:T(8,128)(2,1)S(1)}, bf16[272,512]{1,0:T(8,128)(2,1)S(1)}, u32[]{:S(2)}, u32[]{:S(2)}) collective-permute-start(bf16[272,512]{1,0:T(8,128)(2,1)S(1)} %get-tuple-element.156), channel_id=1, source_target_pairs={{0,2},{1,3},{2,0},{3,1},{4,6},{5,7},{6,4},{7,5},{8,10},{9,11},{10,... | collective-permute-start | bytes 835592 | tf_op jit(solution)/shard_map/ppermute | solution.py:255
  18.1 6.1 %collective-permute-start.7 = (bf16[320,512]{1,0:T(8,128)(2,1)S(1)}, bf16[320,512]{1,0:T(8,128)(2,1)S(1)}, u32[]{:S(2)}, u32[]{:S(2)}) collective-permute-start(bf16[320,512]{1,0:T(8,128)(2,1)S(1)} %get-tuple-element.166), channel_id=1, source_target_pairs={{0,1},{1,0},{2,3},{3,2},{4,5},{5,4},{6,7},{7,6},{8,9},{9,8},{10,11... | collective-permute-start | bytes 983048 | tf_op jit(solution)/shard_map/ppermute | solution.py:255
  20.0 14.0 %collective-permute-start.10 = (bf16[192,512]{1,0:T(8,128)(2,1)S(1)}, bf16[192,512]{1,0:T(8,128)(2,1)S(1)}, u32[]{:S(2)}, u32[]{:S(2)}) collective-permute-start(bf16[192,512]{1,0:T(8,128)(2,1)S(1)} %get-tuple-element.172.own), channel_id=1, source_target_pairs={{0,8},{1,9},{2,10},{3,11},{4,12},{5,13},{6,14},{7,15},{8,0},{9,1},... | collective-permute-start | bytes 589832 | tf_op jit(solution)/shard_map/ppermute | solution.py:255
  23.6 6.8 %collective-permute-start.6 = (bf16[272,512]{1,0:T(8,128)(2,1)S(1)}, bf16[272,512]{1,0:T(8,128)(2,1)S(1)}, u32[]{:S(2)}, u32[]{:S(2)}) collective-permute-start(bf16[272,512]{1,0:T(8,128)(2,1)S(1)} %get-tuple-element.164), channel_id=1, source_target_pairs={{0,4},{1,5},{2,6},{3,7},{4,0},{5,1},{6,2},{7,3},{8,12},{9,13},{10,... | collective-permute-start | bytes 835592 | tf_op jit(solution)/shard_map/ppermute | solution.py:255
  24.7 12.0 %collective-permute-start.13 = (bf16[320,512]{1,0:T(8,128)(2,1)S(1)}, bf16[320,512]{1,0:T(8,128)(2,1)S(1)}, u32[]{:S(2)}, u32[]{:S(2)}) collective-permute-start(bf16[320,512]{1,0:T(8,128)(2,1)S(1)} %get-tuple-element.179), channel_id=1, source_target_pairs={{0,2},{1,3},{2,0},{3,1},{4,6},{5,7},{6,4},{7,5},{8,10},{9,11},{10,... | collective-permute-start | bytes 983048 | tf_op jit(solution)/shard_map/ppermute | solution.py:255
  26.4 12.7 %collective-permute-start.12 = (bf16[2048,128]{1,0:T(8,128)(2,1)S(1)}, bf16[2048,128]{1,0:T(8,128)(2,1)S(1)}, u32[]{:S(2)}, u32[]{:S(2)}) collective-permute-start(bf16[2048,128]{1,0:T(8,128)(2,1)S(1)} %get-tuple-element.177), channel_id=1, source_target_pairs={{1,2},{2,1},{3,4},{4,3},{5,6},{6,5},{7,8},{8,7},{9,10},{10,9},{11,... | collective-permute-start | bytes 1572872 | tf_op jit(solution)/shard_map/ppermute | solution.py:255
  30.6 14.8 %collective-permute-start.8 = (bf16[272,512]{1,0:T(8,128)(2,1)S(1)}, bf16[272,512]{1,0:T(8,128)(2,1)S(1)}, u32[]{:S(2)}, u32[]{:S(2)}) collective-permute-start(bf16[272,512]{1,0:T(8,128)(2,1)S(1)} %get-tuple-element.170.own), channel_id=1, source_target_pairs={{0,8},{1,9},{2,10},{3,11},{4,12},{5,13},{6,14},{7,15},{8,0},{9,1},... | collective-permute-start | bytes 835592 | tf_op jit(solution)/shard_map/ppermute | solution.py:255
  35.0 13.4 %collective-permute-start.17 = (bf16[192,1024]{1,0:T(8,128)(2,1)S(1)}, bf16[192,1024]{1,0:T(8,128)(2,1)S(1)}, u32[]{:S(2)}, u32[]{:S(2)}) collective-permute-start(bf16[192,1024]{1,0:T(8,128)(2,1)S(1)} %get-tuple-element.192), channel_id=1, source_target_pairs={{0,1},{1,0},{2,3},{3,2},{4,5},{5,4},{6,7},{7,6},{8,16},{9,17},{10,... | collective-permute-start | bytes 1179656 | tf_op jit(solution)/shard_map/ppermute | solution.py:255
  36.1 3.0 %collective-permute-start.11 = (bf16[352,512]{1,0:T(8,128)(2,1)S(1)}, bf16[352,512]{1,0:T(8,128)(2,1)S(1)}, u32[]{:S(2)}, u32[]{:S(2)}) collective-permute-start(bf16[352,512]{1,0:T(8,128)(2,1)S(1)} %get-tuple-element.176), channel_id=1, source_target_pairs={{0,1},{1,0},{2,3},{3,2},{4,5},{5,4},{6,7},{7,6},{8,9},{9,8},{10,11... | collective-permute-start | bytes 1081352 | tf_op jit(solution)/shard_map/ppermute | solution.py:255
  37.1 11.4 %collective-permute-start.16 = (bf16[320,512]{1,0:T(8,128)(2,1)S(1)}, bf16[320,512]{1,0:T(8,128)(2,1)S(1)}, u32[]{:S(2)}, u32[]{:S(2)}) collective-permute-start(bf16[320,512]{1,0:T(8,128)(2,1)S(1)} %get-tuple-element.189), channel_id=1, source_target_pairs={{0,4},{1,5},{2,6},{3,7},{4,0},{5,1},{6,2},{7,3},{8,12},{9,13},{10,... | collective-permute-start | bytes 983048 | tf_op jit(solution)/shard_map/ppermute | solution.py:255
  39.5 15.0 %collective-permute-start.15 = (bf16[352,512]{1,0:T(8,128)(2,1)S(1)}, bf16[352,512]{1,0:T(8,128)(2,1)S(1)}, u32[]{:S(2)}, u32[]{:S(2)}) collective-permute-start(bf16[352,512]{1,0:T(8,128)(2,1)S(1)} %get-tuple-element.187), channel_id=1, source_target_pairs={{0,2},{1,3},{2,0},{3,1},{4,6},{5,7},{6,4},{7,5},{8,10},{9,11},{10,... | collective-permute-start | bytes 1081352 | tf_op jit(solution)/shard_map/ppermute | solution.py:255
  46.7 17.1 %collective-permute-start.21 = (bf16[272,1024]{1,0:T(8,128)(2,1)S(1)}, bf16[272,1024]{1,0:T(8,128)(2,1)S(1)}, u32[]{:S(2)}, u32[]{:S(2)}) collective-permute-start(bf16[272,1024]{1,0:T(8,128)(2,1)S(1)} %get-tuple-element.205), channel_id=1, source_target_pairs={{0,1},{1,0},{2,3},{3,2},{4,5},{5,4},{6,7},{7,6},{8,16},{9,17},{10,... | collective-permute-start | bytes 1671176 | tf_op jit(solution)/shard_map/ppermute | solution.py:255
  48.4 6.7 %collective-permute-start.14 = (bf16[368,512]{1,0:T(8,128)(2,1)S(1)}, bf16[368,512]{1,0:T(8,128)(2,1)S(1)}, u32[]{:S(2)}, u32[]{:S(2)}) collective-permute-start(bf16[368,512]{1,0:T(8,128)(2,1)S(1)} %get-tuple-element.185), channel_id=1, source_target_pairs={{0,1},{1,0},{2,3},{3,2},{4,5},{5,4},{6,7},{7,6},{8,9},{9,8},{10,11... | collective-permute-start | bytes 1130504 | tf_op jit(solution)/shard_map/ppermute | solution.py:255
  48.9 12.0 %collective-permute-start.22 = (bf16[320,512]{1,0:T(8,128)(2,1)S(1)}, bf16[320,512]{1,0:T(8,128)(2,1)S(1)}, u32[]{:S(2)}, u32[]{:S(2)}) collective-permute-start(bf16[320,512]{1,0:T(8,128)(2,1)S(1)} %get-tuple-element.207), channel_id=1, source_target_pairs={{0,8},{1,9},{2,10},{3,11},{4,12},{5,13},{6,14},{7,15},{8,0},{9,1},... | collective-permute-start | bytes 983048 | tf_op jit(solution)/shard_map/ppermute | solution.py:255
  55.0 10.7 %collective-permute-start.20 = (bf16[352,512]{1,0:T(8,128)(2,1)S(1)}, bf16[352,512]{1,0:T(8,128)(2,1)S(1)}, u32[]{:S(2)}, u32[]{:S(2)}) collective-permute-start(bf16[352,512]{1,0:T(8,128)(2,1)S(1)} %get-tuple-element.202), channel_id=1, source_target_pairs={{0,4},{1,5},{2,6},{3,7},{4,0},{5,1},{6,2},{7,3},{8,12},{9,13},{10,... | collective-permute-start | bytes 1081352 | tf_op jit(solution)/shard_map/ppermute | solution.py:255
  55.5 11.3 %collective-permute-start.19 = (bf16[368,512]{1,0:T(8,128)(2,1)S(1)}, bf16[368,512]{1,0:T(8,128)(2,1)S(1)}, u32[]{:S(2)}, u32[]{:S(2)}) collective-permute-start(bf16[368,512]{1,0:T(8,128)(2,1)S(1)} %get-tuple-element.200), channel_id=1, source_target_pairs={{0,2},{1,3},{2,0},{3,1},{4,6},{5,7},{6,4},{7,5},{8,10},{9,11},{10,... | collective-permute-start | bytes 1130504 | tf_op jit(solution)/shard_map/ppermute | solution.py:255
  57.7 4.5 %copy-start.2 = (bf16[2,768,512]{2,1,0:T(8,128)(2,1)S(1)}, bf16[2,768,512]{2,1,0:T(8,128)(2,1)}, u32[]{:S(2)}) copy-start(bf16[2,768,512]{2,1,0:T(8,128)(2,1)} %near.13) | copy-start | bytes 4718596
  57.7 4.5 %copy-start.4 = (bf16[2,256,512]{2,1,0:T(8,128)(2,1)S(1)}, bf16[2,256,512]{2,1,0:T(8,128)(2,1)}, u32[]{:S(2)}) copy-start(bf16[2,256,512]{2,1,0:T(8,128)(2,1)} %out_basis.13) | copy-start | bytes 1572868
  58.7 10.3 %collective-permute-start.18 = (bf16[320,512]{1,0:T(8,128)(2,1)S(1)}, bf16[320,512]{1,0:T(8,128)(2,1)S(1)}, u32[]{:S(2)}, u32[]{:S(2)}) collective-permute-start(bf16[320,512]{1,0:T(8,128)(2,1)S(1)} %get-tuple-element.198), channel_id=1, source_target_pairs={{0,1},{1,0},{2,3},{3,2},{4,5},{5,4},{6,7},{7,6},{8,9},{9,8},{10,11... | collective-permute-start | bytes 983048 | tf_op jit(solution)/shard_map/ppermute | solution.py:255
  62.1 17.0 %collective-permute-start.26 = (bf16[320,1024]{1,0:T(8,128)(2,1)S(1)}, bf16[320,1024]{1,0:T(8,128)(2,1)S(1)}, u32[]{:S(2)}, u32[]{:S(2)}) collective-permute-start(bf16[320,1024]{1,0:T(8,128)(2,1)S(1)} %get-tuple-element.223), channel_id=1, source_target_pairs={{0,1},{1,0},{2,3},{3,2},{4,5},{5,4},{6,7},{7,6},{8,16},{9,17},{10,... | collective-permute-start | bytes 1966088 | tf_op jit(solution)/shard_map/ppermute | solution.py:255
  66.1 9.9 %collective-permute-start.27 = (bf16[352,512]{1,0:T(8,128)(2,1)S(1)}, bf16[352,512]{1,0:T(8,128)(2,1)S(1)}, u32[]{:S(2)}, u32[]{:S(2)}) collective-permute-start(bf16[352,512]{1,0:T(8,128)(2,1)S(1)} %get-tuple-element.225), channel_id=1, source_target_pairs={{0,8},{1,9},{2,10},{3,11},{4,12},{5,13},{6,14},{7,15},{8,0},{9,1},... | collective-permute-start | bytes 1081352 | tf_op jit(solution)/shard_map/ppermute | solution.py:255
  67.3 11.8 %collective-permute-start.25 = (bf16[368,512]{1,0:T(8,128)(2,1)S(1)}, bf16[368,512]{1,0:T(8,128)(2,1)S(1)}, u32[]{:S(2)}, u32[]{:S(2)}) collective-permute-start(bf16[368,512]{1,0:T(8,128)(2,1)S(1)} %get-tuple-element.220), channel_id=1, source_target_pairs={{0,4},{1,5},{2,6},{3,7},{4,0},{5,1},{6,2},{7,3},{8,12},{9,13},{10,... | collective-permute-start | bytes 1130504 | tf_op jit(solution)/shard_map/ppermute | solution.py:255
  69.4 13.4 %collective-permute-start.24 = (bf16[320,512]{1,0:T(8,128)(2,1)S(1)}, bf16[320,512]{1,0:T(8,128)(2,1)S(1)}, u32[]{:S(2)}, u32[]{:S(2)}) collective-permute-start(bf16[320,512]{1,0:T(8,128)(2,1)S(1)} %get-tuple-element.218), channel_id=1, source_target_pairs={{0,2},{1,3},{2,0},{3,1},{4,6},{5,7},{6,4},{7,5},{8,10},{9,11},{10,... | collective-permute-start | bytes 983048 | tf_op jit(solution)/shard_map/ppermute | solution.py:255
  72.0 11.5 %collective-permute-start.23 = (bf16[224,512]{1,0:T(8,128)(2,1)S(1)}, bf16[224,512]{1,0:T(8,128)(2,1)S(1)}, u32[]{:S(2)}, u32[]{:S(2)}) collective-permute-start(bf16[224,512]{1,0:T(8,128)(2,1)S(1)} %get-tuple-element.216), channel_id=1, source_target_pairs={{0,1},{1,0},{2,3},{3,2},{4,5},{5,4},{6,7},{7,6},{8,9},{9,8},{10,11... | collective-permute-start | bytes 688136 | tf_op jit(solution)/shard_map/ppermute | solution.py:255
  77.4 16.8 %collective-permute-start.30 = (bf16[352,1024]{1,0:T(8,128)(2,1)S(1)}, bf16[352,1024]{1,0:T(8,128)(2,1)S(1)}, u32[]{:S(2)}, u32[]{:S(2)}) collective-permute-start(bf16[352,1024]{1,0:T(8,128)(2,1)S(1)} %get-tuple-element.239), channel_id=1, source_target_pairs={{0,1},{1,0},{2,3},{3,2},{4,5},{5,4},{6,7},{7,6},{8,16},{9,17},{10,... | collective-permute-start | bytes 2162696 | tf_op jit(solution)/shard_map/ppermute | solution.py:255
  79.6 11.2 %collective-permute-start.31 = (bf16[368,512]{1,0:T(8,128)(2,1)S(1)}, bf16[368,512]{1,0:T(8,128)(2,1)S(1)}, u32[]{:S(2)}, u32[]{:S(2)}) collective-permute-start(bf16[368,512]{1,0:T(8,128)(2,1)S(1)} %get-tuple-element.241), channel_id=1, source_target_pairs={{0,8},{1,9},{2,10},{3,11},{4,12},{5,13},{6,14},{7,15},{8,0},{9,1},... | collective-permute-start | bytes 1130504 | tf_op jit(solution)/shard_map/ppermute | solution.py:255
  83.5 10.7 %collective-permute-start.29 = (bf16[320,512]{1,0:T(8,128)(2,1)S(1)}, bf16[320,512]{1,0:T(8,128)(2,1)S(1)}, u32[]{:S(2)}, u32[]{:S(2)}) collective-permute-start(bf16[320,512]{1,0:T(8,128)(2,1)S(1)} %get-tuple-element.236), channel_id=1, source_target_pairs={{0,4},{1,5},{2,6},{3,7},{4,0},{5,1},{6,2},{7,3},{8,12},{9,13},{10,... | collective-permute-start | bytes 983048 | tf_op jit(solution)/shard_map/ppermute | solution.py:255
  83.9 13.7 %collective-permute-start.28 = (bf16[224,512]{1,0:T(8,128)(2,1)S(1)}, bf16[224,512]{1,0:T(8,128)(2,1)S(1)}, u32[]{:S(2)}, u32[]{:S(2)}) collective-permute-start(bf16[224,512]{1,0:T(8,128)(2,1)S(1)} %get-tuple-element.234), channel_id=1, source_target_pairs={{0,2},{1,3},{2,0},{3,1},{4,6},{5,7},{6,4},{7,5},{8,10},{9,11},{10,... | collective-permute-start | bytes 688136 | tf_op jit(solution)/shard_map/ppermute | solution.py:255
  92.2 16.6 %collective-permute-start.33 = (bf16[368,1024]{1,0:T(8,128)(2,1)S(1)}, bf16[368,1024]{1,0:T(8,128)(2,1)S(1)}, u32[]{:S(2)}, u32[]{:S(2)}) collective-permute-start(bf16[368,1024]{1,0:T(8,128)(2,1)S(1)} %get-tuple-element.252), channel_id=1, source_target_pairs={{0,1},{1,0},{2,3},{3,2},{4,5},{5,4},{6,7},{7,6},{8,16},{9,17},{10,... | collective-permute-start | bytes 2261000 | tf_op jit(solution)/shard_map/ppermute | solution.py:255
  94.7 10.9 %collective-permute-start.34 = (bf16[352,512]{1,0:T(8,128)(2,1)S(1)}, bf16[352,512]{1,0:T(8,128)(2,1)S(1)}, u32[]{:S(2)}, u32[]{:S(2)}) collective-permute-start(bf16[352,512]{1,0:T(8,128)(2,1)S(1)} %get-tuple-element.254), channel_id=1, source_target_pairs={{0,8},{1,9},{2,10},{3,11},{4,12},{5,13},{6,14},{7,15},{8,0},{9,1},... | collective-permute-start | bytes 1081352 | tf_op jit(solution)/shard_map/ppermute | solution.py:255
  98.0 10.8 %collective-permute-start.32 = (bf16[224,512]{1,0:T(8,128)(2,1)S(1)}, bf16[224,512]{1,0:T(8,128)(2,1)S(1)}, u32[]{:S(2)}, u32[]{:S(2)}) collective-permute-start(bf16[224,512]{1,0:T(8,128)(2,1)S(1)} %get-tuple-element.249), channel_id=1, source_target_pairs={{0,4},{1,5},{2,6},{3,7},{4,0},{5,1},{6,2},{7,3},{8,12},{9,13},{10,... | collective-permute-start | bytes 688136 | tf_op jit(solution)/shard_map/ppermute | solution.py:255
  106.8 16.7 %collective-permute-start.37 = (bf16[320,1024]{1,0:T(8,128)(2,1)S(1)}, bf16[320,1024]{1,0:T(8,128)(2,1)S(1)}, u32[]{:S(2)}, u32[]{:S(2)}) collective-permute-start(bf16[320,1024]{1,0:T(8,128)(2,1)S(1)} %get-tuple-element.268), channel_id=1, source_target_pairs={{0,1},{1,0},{2,3},{3,2},{4,5},{5,4},{6,7},{7,6},{8,16},{9,17},{10,... | collective-permute-start | bytes 1966088 | tf_op jit(solution)/shard_map/ppermute | solution.py:255
  109.3 11.2 %collective-permute-start.35 = (bf16[368,512]{1,0:T(8,128)(2,1)S(1)}, bf16[368,512]{1,0:T(8,128)(2,1)S(1)}, u32[]{:S(2)}, u32[]{:S(2)}) collective-permute-start(bf16[368,512]{1,0:T(8,128)(2,1)S(1)} %get-tuple-element.261), channel_id=1, source_target_pairs={{0,8},{1,9},{2,10},{3,11},{4,12},{5,13},{6,14},{7,15},{8,0},{9,1},... | collective-permute-start | bytes 1130504 | tf_op jit(solution)/shard_map/ppermute | solution.py:255
  121.6 14.3 %collective-permute-start.36 = (bf16[224,1024]{1,0:T(8,128)(2,1)S(1)}, bf16[224,1024]{1,0:T(8,128)(2,1)S(1)}, u32[]{:S(2)}, u32[]{:S(2)}) collective-permute-start(bf16[224,1024]{1,0:T(8,128)(2,1)S(1)} %get-tuple-element.265), channel_id=1, source_target_pairs={{0,1},{1,0},{2,3},{3,2},{4,5},{5,4},{6,7},{7,6},{8,16},{9,17},{10,... | collective-permute-start | bytes 1376264 | tf_op jit(solution)/shard_map/ppermute | solution.py:255
  123.9 10.2 %collective-permute-start.38 = (bf16[320,512]{1,0:T(8,128)(2,1)S(1)}, bf16[320,512]{1,0:T(8,128)(2,1)S(1)}, u32[]{:S(2)}, u32[]{:S(2)}) collective-permute-start(bf16[320,512]{1,0:T(8,128)(2,1)S(1)} %get-tuple-element.274), channel_id=1, source_target_pairs={{0,8},{1,9},{2,10},{3,11},{4,12},{5,13},{6,14},{7,15},{8,0},{9,1},... | collective-permute-start | bytes 983048 | tf_op jit(solution)/shard_map/ppermute | solution.py:255
  136.2 6.1 %collective-permute-start.39 = (bf16[224,512]{1,0:T(8,128)(2,1)S(1)}, bf16[224,512]{1,0:T(8,128)(2,1)S(1)}, u32[]{:S(2)}, u32[]{:S(2)}) collective-permute-start(bf16[224,512]{1,0:T(8,128)(2,1)S(1)} %get-tuple-element.279), channel_id=1, source_target_pairs={{0,8},{1,9},{2,10},{3,11},{4,12},{5,13},{6,14},{7,15},{8,0},{9,1},... | collective-permute-start | bytes 688136 | tf_op jit(solution)/shard_map/ppermute | solution.py:255

commit v3 on v2

--- a/solution.py
+++ b/solution.py
@@ -9,7 +9,7 @@
 
 BF16 = jnp.bfloat16
 F32 = jnp.float32
-SHARES = (12, 17, 20, 22, 23, 20, 14)
+SHARES = (13, 18, 20, 22, 23, 21, 11)
 
 
 def dot(a, b):
@@ -25,29 +25,38 @@
 
 def order_of(pieces, inward):
     count = len(pieces)
-    order = [("leaf", pieces[0]), ("level", pieces[0], 1), ("leaf", pieces[1]), ("swap rims",)]
+    order = [("leaf", pieces[0]), ("level", pieces[0], 1), ("leaf", pieces[1]), ("rims", "chip")]
+    arrived, landed = [], []
     for turn in range(2, count + inward + 2):
         new, old = turn - inward, turn - inward - 2
         if turn == inward:
-            order.append(("take",))
+            order.append(("take", "chip"))
+        if turn == inward:
+            order.append(("rims", "middle"))
         if new >= 0 and new != 1:
             order.append(("turn", pieces[new] if new < count else None, pieces[old] if old >= 0 else None))
+        if turn > count:
+            order += [("take", "next")] if turn == count + 1 else []
+            order += [("last", piece) for piece in arrived]
+            arrived = []
         for level in range(inward - 1, 0, -1):
             if turn == inward + 1 and level == 1:
-                order.append(("take",))
+                order.append(("take", "middle"))
             if 0 <= turn - level < count:
                 order.append(("level", pieces[turn - level], level))
         if turn == inward:
-            order += [("pass rims",), ("turn", pieces[1], None), ("relay", pieces[new])]
+            order += [("turn", pieces[1], None), ("relay", pieces[new])]
         if turn == inward + 1:
             order.append(("relay", pieces[new]))
         if turn < count:
             order.append(("leaf", pieces[turn]))
+        if turn == count:
+            order.append(("rims", "next"))
         if inward + 1 < turn and new < count:
             order.append(("relay", pieces[new]))
         if old >= 0:
-            order.append(("last", pieces[old]))
-    return order
+            arrived.append(pieces[old])
+    return order + [("last", piece) for piece in arrived]
 
 
 def copies(pairs, sems):
@@ -172,7 +181,7 @@
     token[...] = jnp.zeros_like(token)
 
 
-def last_step(quarter, start, size, own, back, out_basis, near, src, rim_a, rim_b, prev, *refs):
+def last_step(quarter, start, size, own, back, out_basis, near, src, rim_a, rim_m, rim_n, prev, *refs):
     out, token, window, result, sems = refs[-5:]
     rank, points = out_basis.shape[1:]
     rim = rim_a.shape[1]
@@ -180,10 +189,12 @@
     me = lax.axis_index("box")
     odd = lax.rem(me, 2) == 1
     inner = jnp.logical_and(me >= quarter, me < 3 * quarter)
+    halfway = jnp.logical_or(me == 2 * quarter - 1, me == 2 * quarter)
     leaves = copies([(result.at[pl.ds(at, n)], out.at[pl.ds(start + at, n)]) for at, n in blocks], sems)
     for leave, (at, n) in zip(leaves, blocks):
         part, whole = slice(at, at + n), slice(start + at, start + at + n)
-        before, after = jnp.where(odd, rim_a[whole], rim_b[whole]), jnp.where(odd, rim_b[whole], rim_a[whole])
+        rim_b = jnp.where(halfway, rim_m[whole], rim_n[whole])
+        before, after = jnp.where(odd, rim_a[whole], rim_b), jnp.where(odd, rim_b, rim_a[whole])
         window[part, :rim] = before
         window[part, rim : rim + 2 * points] = src[whole].astype(BF16)
         window[part, rim + 2 * points :] = after
@@ -251,16 +262,18 @@
     across = [
         (i, i ^ 3 * quarter if quarter <= i < 3 * quarter else i ^ 1) for i in range(devices)
     ]
+    middle = [(devices // 2 - 1, devices // 2), (devices // 2, devices // 2 - 1)]
     next_over = [(i, (i - 1 ^ 1) + 1) for i in range(1, devices - 1)]
+    next_over = [link for link in next_over if link not in middle]
     send = lambda operand, pairs: lax.ppermute(operand, "box", pairs)
     small = tuple(stay_blocks.shape[1:])
 
     token = jnp.zeros(TOKEN.shape, TOKEN.dtype)
-    out, rim_a, rim_b, waiting, theirs = (None,) * 5
-    held, moved, kept, across_in, swapped = {}, {}, {}, {}, {}
+    out, theirs = None, None
+    held, moved, kept, across_in, swapped, rims = {}, {}, {}, {}, {}, {}
     for step, *rest in order_of(pieces, inward):
         piece = rest[0] if rest else None
-        start, size = piece or (0, rows)
+        start, size = piece if isinstance(piece, tuple) else (0, rows)
         pair = array(size, 2 * rank)
         if step == "leaf" and start == 0:
             held[1, piece], sent, packed, token = call(
@@ -320,13 +333,14 @@
             kept[piece] = own, other
             across_in[piece] = send(sent, across)
         elif step == "last":
-            operands = [*kept.pop(piece), out_basis, near_blocks, sources, rim_a, rim_b, token]
-            in_specs = [VMEM] * 7 + [ANY]
+            operands = [*kept.pop(piece), out_basis, near_blocks, sources, rims["chip"], rims["middle"],
+                        rims["next"], token]
+            in_specs = [VMEM] * 8 + [ANY]
             aliases = {}
             if out is not None:
                 operands.append(out)
                 in_specs.append(ANY)
-                aliases = {8: 0}
+                aliases = {9: 0}
             out, token = call(
                 functools.partial(last_step, quarter, start, size),
                 operands, in_specs,
@@ -337,15 +351,13 @@
                 "last", 16, aliases,
             )
         elif step == "take":
-            (token,) = call(take_step, (waiting, token), [ANY] * 2, [TOKEN], [VMEM], [], "take", 8)
+            (token,) = call(take_step, (rims[piece], token), [ANY] * 2, [TOKEN], [VMEM], [], "take", 8)
         else:
-            swap = step == "swap rims"
             to, token = call(
-                functools.partial(rim_step, swap), (sources, token), [VMEM, ANY], [array(rows, rim), TOKEN],
-                [VMEM] * 2, [], "rims", 8,
-            )
-            waiting = send(to, apart(1) if swap else next_over)
-            rim_a, rim_b = (waiting, None) if swap else (rim_a, waiting)
+                functools.partial(rim_step, piece == "chip"), (sources, token), [VMEM, ANY],
+                [array(rows, rim), TOKEN], [VMEM] * 2, [], "rims", 8,
+            )
+            rims[piece] = send(to, {"chip": apart(1), "middle": middle, "next": next_over}[piece])
     return out
 
 

time: 145 us -> 140 us (0.966)
  waiting for transfers between devices: 51 us -> 41 us
  starting transfers between devices: 53.6 us -> 58.9 us
    ppermute x40 -> x41, waiting for transfers between devices: 51 us -> 41 us  [per_device(): send = lambda operand, pairs: lax.ppermute(operand, 'box', pairs)]
    ppermute x40 -> x41, starting transfers between devices: 53.6 us -> 58.9 us  [per_device(): send = lambda operand, pairs: lax.ppermute(operand, 'box', pairs)]
    pallas_call x48 -> x50, Pallas kernels: 39.3 us -> 39.2 us  [call(): pl.pallas_call(body, in_specs=in_specs, out_specs=out_specs, out_shape=ou...]
  transfers between devices with their start and end apart: 40 -> 41, of which waited for: 14 -> 16; matrix products, arithmetic and copies ran while one was open for 0% -> 0% of each run, Pallas kernels for 24% -> 25%
where the time goes in v3:
time: 140 us
  starting transfers between devices  58.9 us (42%)
  waiting for transfers between devices  41 us (29%)
  Pallas kernels  39.2 us (28%)
    ppermute x41, starting transfers between devices, per_device(): send = lambda operand, pairs: lax.ppermute(operand, 'box', pairs)  58.9 us
    ppermute x41, waiting for transfers between devices, per_device(): send = lambda operand, pairs: lax.ppermute(operand, 'box', pairs)  41 us
    pallas_call x50, Pallas kernels, call(): pl.pallas_call(body, in_specs=in_specs, out_specs=out_specs, out_shape=ou...  39.2 us
  transfers between devices with their start and end apart: 41, of which 16 were waited for; matrix products, arithmetic and copies ran while one was open for 0% of the time, Pallas kernels for 25%

profile of v3, /device:TPU:0, one launch (start us, length us, event | category | flops | bytes accessed | tf_op | source)
XLA Modules:
  0.0 139.8 jit_solution(281015537990062933)
XLA Ops:
  0.0 2.6 %leaf.14 = (bf16[208,512]{1,0:T(8,128)(2,1)S(1)}, bf16[208,512]{1,0:T(8,128)(2,1)S(1)}, bf16[4,2,256,256]{3,2,1,0:T(8,128)(2,1)S(1)}, f32[8,128]{1,0:T(8,128)S(1)}) custom-call(f32[2048,1024]{1,0:T(8,128)} %src.33, bf16[2,512,256]{2,1,0:T(8,128)(2,1)} %leaf.27, bf16[6,2,256,256]{3,2,1,0:T(8,128)(2,1)} %refs_4_.3, bf16[6,2,256,256]{3,2,1,0:T(8,128)(2,1)} %cross.55, ...), custom_call_target="tpu_custom_call" | custom-call | flops 3000000000 | bytes 1 | tf_op jit(solution)/shard_map/leaf/pallas_call | solution.py:237
  3.1 2.7 %collective-permute-start.9 = (bf16[4,2,256,256]{3,2,1,0:T(8,128)(2,1)S(1)}, bf16[4,2,256,256]{3,2,1,0:T(8,128)(2,1)S(1)}, u32[]{:S(2)}, u32[]{:S(2)}) collective-permute-start(bf16[4,2,256,256]{3,2,1,0:T(8,128)(2,1)S(1)} %get-tuple-element.173), channel_id=1, source_target_pairs={{0,8},{1,9},{2,10},{3,11},{4,12},{5,13},{6,14},{7,15},{8,0},{9,1},... | collective-permute-start | bytes 3145736 | tf_op jit(solution)/shard_map/ppermute | solution.py:268
  6.2 1.6 %collective-permute-start.2 = (bf16[208,512]{1,0:T(8,128)(2,1)S(1)}, bf16[208,512]{1,0:T(8,128)(2,1)S(1)}, u32[]{:S(2)}, u32[]{:S(2)}) collective-permute-start(bf16[208,512]{1,0:T(8,128)(2,1)S(1)} %get-tuple-element.153), channel_id=1, source_target_pairs={{0,2},{1,3},{2,0},{3,1},{4,6},{5,7},{6,4},{7,5},{8,10},{9,11},{10,... | collective-permute-start | bytes 638984 | tf_op jit(solution)/shard_map/ppermute | solution.py:268
  9.5 4.1 %collective-permute-done.2.moved = bf16[208,512]{1,0:T(8,128)(2,1)S(1)} collective-permute-done((bf16[208,512]{1,0:T(8,128)(2,1)S(1)}, bf16[208,512]{1,0:T(8,128)(2,1)S(1)}, u32[]{:S(2)}, u32[]{:S(2)}) %collective-permute-start.2) | collective-permute-done | bytes 213024 | tf_op jit(solution)/shard_map/ppermute | solution.py:268
  13.9 1.6 %collective-permute-start.4 = (bf16[208,512]{1,0:T(8,128)(2,1)S(1)}, bf16[208,512]{1,0:T(8,128)(2,1)S(1)}, u32[]{:S(2)}, u32[]{:S(2)}) collective-permute-start(bf16[208,512]{1,0:T(8,128)(2,1)S(1)} %get-tuple-element.160), channel_id=1, source_target_pairs={{0,4},{1,5},{2,6},{3,7},{4,0},{5,1},{6,2},{7,3},{8,12},{9,13},{10,... | collective-permute-start | bytes 638984 | tf_op jit(solution)/shard_map/ppermute | solution.py:268
  16.0 1.6 %collective-permute-start.3 = (bf16[288,512]{1,0:T(8,128)(2,1)S(1)}, bf16[288,512]{1,0:T(8,128)(2,1)S(1)}, u32[]{:S(2)}, u32[]{:S(2)}) collective-permute-start(bf16[288,512]{1,0:T(8,128)(2,1)S(1)} %get-tuple-element.158), channel_id=1, source_target_pairs={{0,2},{1,3},{2,0},{3,1},{4,6},{5,7},{6,4},{7,5},{8,10},{9,11},{10,... | collective-permute-start | bytes 884744 | tf_op jit(solution)/shard_map/ppermute | solution.py:268
  18.7 1.8 %collective-permute-done.4.moved = bf16[208,512]{1,0:T(8,128)(2,1)S(1)} collective-permute-done((bf16[208,512]{1,0:T(8,128)(2,1)S(1)}, bf16[208,512]{1,0:T(8,128)(2,1)S(1)}, u32[]{:S(2)}, u32[]{:S(2)}) %collective-permute-start.4) | collective-permute-done | bytes 213024 | tf_op jit(solution)/shard_map/ppermute | solution.py:268
  20.7 3.3 %collective-permute-done.3.moved = bf16[288,512]{1,0:T(8,128)(2,1)S(1)} collective-permute-done((bf16[288,512]{1,0:T(8,128)(2,1)S(1)}, bf16[288,512]{1,0:T(8,128)(2,1)S(1)}, u32[]{:S(2)}, u32[]{:S(2)}) %collective-permute-start.3) | collective-permute-done | bytes 294944 | tf_op jit(solution)/shard_map/ppermute | solution.py:268
  25.0 1.3 collective-permute-start.10
  27.6 1.6 %collective-permute-start.13 = (bf16[320,512]{1,0:T(8,128)(2,1)S(1)}, bf16[320,512]{1,0:T(8,128)(2,1)S(1)}, u32[]{:S(2)}, u32[]{:S(2)}) collective-permute-start(bf16[320,512]{1,0:T(8,128)(2,1)S(1)} %get-tuple-element.181), channel_id=1, source_target_pairs={{0,2},{1,3},{2,0},{3,1},{4,6},{5,7},{6,4},{7,5},{8,10},{9,11},{10,... | collective-permute-start | bytes 983048 | tf_op jit(solution)/shard_map/ppermute | solution.py:268
  29.2 2.3 %collective-permute-done.6.moved = bf16[288,512]{1,0:T(8,128)(2,1)S(1)} collective-permute-done((bf16[288,512]{1,0:T(8,128)(2,1)S(1)}, bf16[288,512]{1,0:T(8,128)(2,1)S(1)}, u32[]{:S(2)}, u32[]{:S(2)}) %collective-permute-start.6) | collective-permute-done | bytes 294944 | tf_op jit(solution)/shard_map/ppermute | solution.py:268
  31.8 1.4 collective-permute-start.8
  33.1 1.2 collective-permute-done.10.other
  34.4 1.1 relay.7
  37.5 1.5 %collective-permute-start.16 = (bf16[320,512]{1,0:T(8,128)(2,1)S(1)}, bf16[320,512]{1,0:T(8,128)(2,1)S(1)}, u32[]{:S(2)}, u32[]{:S(2)}) collective-permute-start(bf16[320,512]{1,0:T(8,128)(2,1)S(1)} %get-tuple-element.191), channel_id=1, source_target_pairs={{0,4},{1,5},{2,6},{3,7},{4,0},{5,1},{6,2},{7,3},{8,12},{9,13},{10,... | collective-permute-start | bytes 983048 | tf_op jit(solution)/shard_map/ppermute | solution.py:268
  39.5 2.0 %collective-permute-start.15 = (bf16[352,512]{1,0:T(8,128)(2,1)S(1)}, bf16[352,512]{1,0:T(8,128)(2,1)S(1)}, u32[]{:S(2)}, u32[]{:S(2)}) collective-permute-start(bf16[352,512]{1,0:T(8,128)(2,1)S(1)} %get-tuple-element.189), channel_id=1, source_target_pairs={{0,2},{1,3},{2,0},{3,1},{4,6},{5,7},{6,4},{7,5},{8,10},{9,11},{10,... | collective-permute-start | bytes 1081352 | tf_op jit(solution)/shard_map/ppermute | solution.py:268
  41.5 1.2 relay.8
  44.4 2.8 %collective-permute-done.16.refs_1_ = bf16[320,512]{1,0:T(8,128)(2,1)S(1)} collective-permute-done((bf16[320,512]{1,0:T(8,128)(2,1)S(1)}, bf16[320,512]{1,0:T(8,128)(2,1)S(1)}, u32[]{:S(2)}, u32[]{:S(2)}) %collective-permute-start.16) | collective-permute-done | bytes 327712 | tf_op jit(solution)/shard_map/ppermute | solution.py:268
  47.6 3.6 %collective-permute-start.22 = (bf16[320,512]{1,0:T(8,128)(2,1)S(1)}, bf16[320,512]{1,0:T(8,128)(2,1)S(1)}, u32[]{:S(2)}, u32[]{:S(2)}) collective-permute-start(bf16[320,512]{1,0:T(8,128)(2,1)S(1)} %get-tuple-element.209), channel_id=1, source_target_pairs={{0,8},{1,9},{2,10},{3,11},{4,12},{5,13},{6,14},{7,15},{8,0},{9,1},... | collective-permute-start | bytes 983048 | tf_op jit(solution)/shard_map/ppermute | solution.py:268
  51.6 1.6 %collective-permute-start.20 = (bf16[352,512]{1,0:T(8,128)(2,1)S(1)}, bf16[352,512]{1,0:T(8,128)(2,1)S(1)}, u32[]{:S(2)}, u32[]{:S(2)}) collective-permute-start(bf16[352,512]{1,0:T(8,128)(2,1)S(1)} %get-tuple-element.204), channel_id=1, source_target_pairs={{0,4},{1,5},{2,6},{3,7},{4,0},{5,1},{6,2},{7,3},{8,12},{9,13},{10,... | collective-permute-start | bytes 1081352 | tf_op jit(solution)/shard_map/ppermute | solution.py:268
  53.7 1.6 %collective-permute-start.19 = (bf16[368,512]{1,0:T(8,128)(2,1)S(1)}, bf16[368,512]{1,0:T(8,128)(2,1)S(1)}, u32[]{:S(2)}, u32[]{:S(2)}) collective-permute-start(bf16[368,512]{1,0:T(8,128)(2,1)S(1)} %get-tuple-element.202), channel_id=1, source_target_pairs={{0,2},{1,3},{2,0},{3,1},{4,6},{5,7},{6,4},{7,5},{8,10},{9,11},{10,... | collective-permute-start | bytes 1130504 | tf_op jit(solution)/shard_map/ppermute | solution.py:268
  56.3 2.3 %collective-permute-done.22.other.back = bf16[320,512]{1,0:T(8,128)(2,1)S(1)} collective-permute-done((bf16[320,512]{1,0:T(8,128)(2,1)S(1)}, bf16[320,512]{1,0:T(8,128)(2,1)S(1)}, u32[]{:S(2)}, u32[]{:S(2)}) %collective-permute-start.22) | collective-permute-done | bytes 327712 | tf_op jit(solution)/shard_map/ppermute | solution.py:268
  58.6 1.3 relay.9
  60.0 1.3 collective-permute-done.20.refs_1_
  61.7 2.2 %collective-permute-start.27 = (bf16[352,512]{1,0:T(8,128)(2,1)S(1)}, bf16[352,512]{1,0:T(8,128)(2,1)S(1)}, u32[]{:S(2)}, u32[]{:S(2)}) collective-permute-start(bf16[352,512]{1,0:T(8,128)(2,1)S(1)} %get-tuple-element.225), channel_id=1, source_target_pairs={{0,8},{1,9},{2,10},{3,11},{4,12},{5,13},{6,14},{7,15},{8,0},{9,1},... | collective-permute-start | bytes 1081352 | tf_op jit(solution)/shard_map/ppermute | solution.py:268
  67.8 3.6 %collective-permute-done.27.other.back = bf16[352,512]{1,0:T(8,128)(2,1)S(1)} collective-permute-done((bf16[352,512]{1,0:T(8,128)(2,1)S(1)}, bf16[352,512]{1,0:T(8,128)(2,1)S(1)}, u32[]{:S(2)}, u32[]{:S(2)}) %collective-permute-start.27) | collective-permute-done | bytes 360480 | tf_op jit(solution)/shard_map/ppermute | solution.py:268
  71.3 1.4 relay.10
  74.3 1.2 collective-permute-start.31
  75.5 6.6 %collective-permute-start.29 = (bf16[368,512]{1,0:T(8,128)(2,1)S(1)}, bf16[368,512]{1,0:T(8,128)(2,1)S(1)}, u32[]{:S(2)}, u32[]{:S(2)}) collective-permute-start(bf16[368,512]{1,0:T(8,128)(2,1)S(1)} %get-tuple-element.233), channel_id=1, source_target_pairs={{0,8},{1,9},{2,10},{3,11},{4,12},{5,13},{6,14},{7,15},{8,0},{9,1},... | collective-permute-start | bytes 1130504 | tf_op jit(solution)/shard_map/ppermute | solution.py:268
  83.5 2.8 %collective-permute-start.28 = (bf16[176,512]{1,0:T(8,128)(2,1)S(1)}, bf16[176,512]{1,0:T(8,128)(2,1)S(1)}, u32[]{:S(2)}, u32[]{:S(2)}) collective-permute-start(bf16[176,512]{1,0:T(8,128)(2,1)S(1)} %get-tuple-element.231), channel_id=1, source_target_pairs={{0,2},{1,3},{2,0},{3,1},{4,6},{5,7},{6,4},{7,5},{8,10},{9,11},{10,... | collective-permute-start | bytes 540680 | tf_op jit(solution)/shard_map/ppermute | solution.py:268
  86.3 1.4 collective-permute-done.29.other.back
  87.6 1.4 %relay.11 = (bf16[368,512]{1,0:T(8,128)(2,1)S(1)}, bf16[368,512]{1,0:T(8,128)(2,1)S(1)}, bf16[368,1024]{1,0:T(8,128)(2,1)S(1)}, f32[8,128]{1,0:T(8,128)S(1)}) custom-call(bf16[368,512]{1,0:T(8,128)(2,1)S(1)} %get-tuple-element.243.own, bf16[368,512]{1,0:T(8,128)(2,1)S(1)} %collective-permute-done.29.other.back, bf16[6,2,256,256]{3,2,1,0:T(8,128)(2,1)S(1)} %copy-done.1, ...), custom_call_target="tpu_custom_call" | custom-call | flops 10000000 | bytes 1 | tf_op jit(solution)/shard_map/relay/pallas_call | solution.py:237
  89.7 5.2 %collective-permute-start.35 = (bf16[352,512]{1,0:T(8,128)(2,1)S(1)}, bf16[352,512]{1,0:T(8,128)(2,1)S(1)}, u32[]{:S(2)}, u32[]{:S(2)}) collective-permute-start(bf16[352,512]{1,0:T(8,128)(2,1)S(1)} %get-tuple-element.258), channel_id=1, source_target_pairs={{0,8},{1,9},{2,10},{3,11},{4,12},{5,13},{6,14},{7,15},{8,0},{9,1},... | collective-permute-start | bytes 1081352 | tf_op jit(solution)/shard_map/ppermute | solution.py:268
  94.9 1.6 %last.7 = (f32[2048,1024]{1,0:T(8,128)}, f32[8,128]{1,0:T(8,128)S(1)}) custom-call(bf16[208,512]{1,0:T(8,128)(2,1)S(1)} %get-tuple-element.237.own, bf16[320,512]{1,0:T(8,128)(2,1)S(1)} %collective-permute-done.22.other.back, bf16[2,256,512]{2,1,0:T(8,128)(2,1)S(1)} %copy-done.4, bf16[2,768,512]{2,1,0:T(8,128)(2,1)S(1)} %copy-done.2, ...), custom_call_target="tpu_custom_call" | custom-call | flops 10000000 | bytes 1 | tf_op jit(solution)/shard_map/last/pallas_call | solution.py:237
  96.5 1.8 %last.8 = (f32[2048,1024]{1,0:T(8,128)}, f32[8,128]{1,0:T(8,128)S(1)}) custom-call(bf16[288,512]{1,0:T(8,128)(2,1)S(1)} %get-tuple-element.236.own, bf16[352,512]{1,0:T(8,128)(2,1)S(1)} %collective-permute-done.27.other.back, bf16[2,256,512]{2,1,0:T(8,128)(2,1)S(1)} %copy-done.4, ...), custom_call_target="tpu_custom_call", output_to_operand_aliasing={{0}: (9, {})} | custom-call | flops 10000000 | bytes 1 | tf_op jit(solution)/shard_map/last/pallas_call | solution.py:237
  98.2 1.8 %last.9 = (f32[2048,1024]{1,0:T(8,128)}, f32[8,128]{1,0:T(8,128)S(1)}) custom-call(bf16[320,512]{1,0:T(8,128)(2,1)S(1)} %get-tuple-element.232.own, bf16[368,512]{1,0:T(8,128)(2,1)S(1)} %collective-permute-done.29.other.back, bf16[2,256,512]{2,1,0:T(8,128)(2,1)S(1)} %copy-done.4, ...), custom_call_target="tpu_custom_call", output_to_operand_aliasing={{0}: (9, {})} | custom-call | flops 10000000 | bytes 1 | tf_op jit(solution)/shard_map/last/pallas_call | solution.py:237
  100.1 2.3 %collective-permute-done.28.moved = bf16[176,512]{1,0:T(8,128)(2,1)S(1)} collective-permute-done((bf16[176,512]{1,0:T(8,128)(2,1)S(1)}, bf16[176,512]{1,0:T(8,128)(2,1)S(1)}, u32[]{:S(2)}, u32[]{:S(2)}) %collective-permute-start.28) | collective-permute-done | bytes 180256 | tf_op jit(solution)/shard_map/ppermute | solution.py:268
  102.7 2.6 %collective-permute-start.33 = (bf16[176,512]{1,0:T(8,128)(2,1)S(1)}, bf16[176,512]{1,0:T(8,128)(2,1)S(1)}, u32[]{:S(2)}, u32[]{:S(2)}) collective-permute-start(bf16[176,512]{1,0:T(8,128)(2,1)S(1)} %get-tuple-element.253), channel_id=1, source_target_pairs={{0,4},{1,5},{2,6},{3,7},{4,0},{5,1},{6,2},{7,3},{8,12},{9,13},{10,... | collective-permute-start | bytes 540680 | tf_op jit(solution)/shard_map/ppermute | solution.py:268
  105.3 1.3 relay.12
  106.8 2.8 %collective-permute-done.33.refs_1_ = bf16[176,512]{1,0:T(8,128)(2,1)S(1)} collective-permute-done((bf16[176,512]{1,0:T(8,128)(2,1)S(1)}, bf16[176,512]{1,0:T(8,128)(2,1)S(1)}, u32[]{:S(2)}, u32[]{:S(2)}) %collective-permute-start.33) | collective-permute-done | bytes 180256 | tf_op jit(solution)/shard_map/ppermute | solution.py:268
  110.8 1.9 %last.10 = (f32[2048,1024]{1,0:T(8,128)}, f32[8,128]{1,0:T(8,128)S(1)}) custom-call(bf16[352,512]{1,0:T(8,128)(2,1)S(1)} %get-tuple-element.263.own, bf16[352,512]{1,0:T(8,128)(2,1)S(1)} %collective-permute-done.35.other.back, bf16[2,256,512]{2,1,0:T(8,128)(2,1)S(1)} %copy-done.4, ...), custom_call_target="tpu_custom_call", output_to_operand_aliasing={{0}: (9, {})} | custom-call | flops 10000000 | bytes 1 | tf_op jit(solution)/shard_map/last/pallas_call | solution.py:237
  112.7 9.1 %collective-permute-done.36.other.back = bf16[368,512]{1,0:T(8,128)(2,1)S(1)} collective-permute-done((bf16[368,512]{1,0:T(8,128)(2,1)S(1)}, bf16[368,512]{1,0:T(8,128)(2,1)S(1)}, u32[]{:S(2)}, u32[]{:S(2)}) %collective-permute-start.36) | collective-permute-done | bytes 376864 | tf_op jit(solution)/shard_map/ppermute | solution.py:268
  123.2 2.2 %collective-permute-start.40 = (bf16[336,512]{1,0:T(8,128)(2,1)S(1)}, bf16[336,512]{1,0:T(8,128)(2,1)S(1)}, u32[]{:S(2)}, u32[]{:S(2)}) collective-permute-start(bf16[336,512]{1,0:T(8,128)(2,1)S(1)} %get-tuple-element.281), channel_id=1, source_target_pairs={{0,8},{1,9},{2,10},{3,11},{4,12},{5,13},{6,14},{7,15},{8,0},{9,1},... | collective-permute-start | bytes 1032200 | tf_op jit(solution)/shard_map/ppermute | solution.py:268
  125.4 1.9 %last.11 = (f32[2048,1024]{1,0:T(8,128)}, f32[8,128]{1,0:T(8,128)S(1)}) custom-call(bf16[368,512]{1,0:T(8,128)(2,1)S(1)} %get-tuple-element.270.own, bf16[368,512]{1,0:T(8,128)(2,1)S(1)} %collective-permute-done.36.other.back, bf16[2,256,512]{2,1,0:T(8,128)(2,1)S(1)} %copy-done.4, ...), custom_call_target="tpu_custom_call", output_to_operand_aliasing={{0}: (9, {})} | custom-call | flops 10000000 | bytes 1 | tf_op jit(solution)/shard_map/last/pallas_call | solution.py:237
  127.6 6.0 %collective-permute-start.39 = (bf16[176,512]{1,0:T(8,128)(2,1)S(1)}, bf16[176,512]{1,0:T(8,128)(2,1)S(1)}, u32[]{:S(2)}, u32[]{:S(2)}) collective-permute-start(bf16[176,512]{1,0:T(8,128)(2,1)S(1)} %get-tuple-element.279), channel_id=1, source_target_pairs={{0,8},{1,9},{2,10},{3,11},{4,12},{5,13},{6,14},{7,15},{8,0},{9,1},... | collective-permute-start | bytes 540680 | tf_op jit(solution)/shard_map/ppermute | solution.py:268
  134.1 1.9 %last.12 = (f32[2048,1024]{1,0:T(8,128)}, f32[8,128]{1,0:T(8,128)S(1)}) custom-call(bf16[336,512]{1,0:T(8,128)(2,1)S(1)} %get-tuple-element.280.own, bf16[336,512]{1,0:T(8,128)(2,1)S(1)} %collective-permute-done.40.back, bf16[2,256,512]{2,1,0:T(8,128)(2,1)S(1)} %copy-done.4, bf16[2,768,512]{2,1,0:T(8,128)(2,1)S(1)} %copy-done.2, ...), custom_call_target="tpu_custom_call", output_to_operand_aliasing={{0}: (9, {})} | custom-call | flops 10000000 | bytes 1 | tf_op jit(solution)/shard_map/last/pallas_call | solution.py:237
  136.0 1.6 %collective-permute-done.39.back = bf16[176,512]{1,0:T(8,128)(2,1)S(1)} collective-permute-done((bf16[176,512]{1,0:T(8,128)(2,1)S(1)}, bf16[176,512]{1,0:T(8,128)(2,1)S(1)}, u32[]{:S(2)}, u32[]{:S(2)}) %collective-permute-start.39) | collective-permute-done | bytes 180256 | tf_op jit(solution)/shard_map/ppermute | solution.py:268
  137.6 2.1 %last.13 = (f32[2048,1024]{1,0:T(8,128)}, f32[8,128]{1,0:T(8,128)}) custom-call(bf16[176,512]{1,0:T(8,128)(2,1)S(1)} %get-tuple-element.278.own, bf16[176,512]{1,0:T(8,128)(2,1)S(1)} %collective-permute-done.39.back, bf16[2,256,512]{2,1,0:T(8,128)(2,1)S(1)} %copy-done.4, bf16[2,768,512]{2,1,0:T(8,128)(2,1)S(1)} %copy-done.2, ...), custom_call_target="tpu_custom_call", output_to_operand_aliasing={{0}: (9, {})} | custom-call | flops 10000000 | bytes 1 | tf_op jit(solution)/shard_map/last/pallas_call | solution.py:237
  (100 shorter events, 25.5 us)
Async XLA Ops:
  0.0 5.8 %copy-start.1 = (bf16[6,2,256,256]{3,2,1,0:T(8,128)(2,1)S(1)}, bf16[6,2,256,256]{3,2,1,0:T(8,128)(2,1)}, u32[]{:S(2)}) copy-start(bf16[6,2,256,256]{3,2,1,0:T(8,128)(2,1)} %refs_4_.3) | copy-start | bytes 4718596
  0.0 5.8 %copy-start = (bf16[6,2,256,256]{3,2,1,0:T(8,128)(2,1)S(1)}, bf16[6,2,256,256]{3,2,1,0:T(8,128)(2,1)}, u32[]{:S(2)}) copy-start(bf16[6,2,256,256]{3,2,1,0:T(8,128)(2,1)} %cross.55) | copy-start | bytes 4718596
  0.0 7.7 %slice-start = ((s8[8388608]{0:T(1024)(128)(4,1)}), s8[4194304]{0:T(1024)(128)(4,1)S(1)}, s32[]{:S(2)}) async-start(s8[8388608]{0:T(1024)(128)(4,1)} %bitcast), calls=%async_computation | async-start | bytes 8388608
  0.0 7.7 %slice-start.1 = ((s8[8388608]{0:T(1024)(128)(4,1)}), s8[4194304]{0:T(1024)(128)(4,1)S(1)}, s32[]{:S(2)}) async-start(s8[8388608]{0:T(1024)(128)(4,1)} %bitcast), calls=%async_computation.1 | async-start | bytes 8388608
  2.6 5.2 %copy-start.3 = (bf16[2,512,256]{2,1,0:T(8,128)(2,1)S(1)}, bf16[2,512,256]{2,1,0:T(8,128)(2,1)}, u32[]{:S(2)}) copy-start(bf16[2,512,256]{2,1,0:T(8,128)(2,1)} %leaf.27) | copy-start | bytes 1572868
  2.6 3.2 %collective-permute-start = (bf16[208,512]{1,0:T(8,128)(2,1)S(1)}, bf16[208,512]{1,0:T(8,128)(2,1)S(1)}, u32[]{:S(2)}, u32[]{:S(2)}) collective-permute-start(bf16[208,512]{1,0:T(8,128)(2,1)S(1)} %get-tuple-element.147), channel_id=1, source_target_pairs={{0,1},{1,0},{2,3},{3,2},{4,5},{5,4},{6,7},{7,6},{8,9},{9,8},{10,11... | collective-permute-start | bytes 638984 | tf_op jit(solution)/shard_map/ppermute | solution.py:268
  3.1 31.2 %collective-permute-start.9 = (bf16[4,2,256,256]{3,2,1,0:T(8,128)(2,1)S(1)}, bf16[4,2,256,256]{3,2,1,0:T(8,128)(2,1)S(1)}, u32[]{:S(2)}, u32[]{:S(2)}) collective-permute-start(bf16[4,2,256,256]{3,2,1,0:T(8,128)(2,1)S(1)} %get-tuple-element.173), channel_id=1, source_target_pairs={{0,8},{1,9},{2,10},{3,11},{4,12},{5,13},{6,14},{7,15},{8,0},{9,1},... | collective-permute-start | bytes 3145736 | tf_op jit(solution)/shard_map/ppermute | solution.py:268
  6.2 7.4 %collective-permute-start.2 = (bf16[208,512]{1,0:T(8,128)(2,1)S(1)}, bf16[208,512]{1,0:T(8,128)(2,1)S(1)}, u32[]{:S(2)}, u32[]{:S(2)}) collective-permute-start(bf16[208,512]{1,0:T(8,128)(2,1)S(1)} %get-tuple-element.153), channel_id=1, source_target_pairs={{0,2},{1,3},{2,0},{3,1},{4,6},{5,7},{6,4},{7,5},{8,10},{9,11},{10,... | collective-permute-start | bytes 638984 | tf_op jit(solution)/shard_map/ppermute | solution.py:268
  8.7 6.9 %collective-permute-start.1 = (bf16[288,512]{1,0:T(8,128)(2,1)S(1)}, bf16[288,512]{1,0:T(8,128)(2,1)S(1)}, u32[]{:S(2)}, u32[]{:S(2)}) collective-permute-start(bf16[288,512]{1,0:T(8,128)(2,1)S(1)} %get-tuple-element.151), channel_id=1, source_target_pairs={{0,1},{1,0},{2,3},{3,2},{4,5},{5,4},{6,7},{7,6},{8,9},{9,8},{10,11... | collective-permute-start | bytes 884744 | tf_op jit(solution)/shard_map/ppermute | solution.py:268
  8.9 9.7 %collective-permute-start.5 = (bf16[2048,128]{1,0:T(8,128)(2,1)S(1)}, bf16[2048,128]{1,0:T(8,128)(2,1)S(1)}, u32[]{:S(2)}, u32[]{:S(2)}) collective-permute-start(bf16[2048,128]{1,0:T(8,128)(2,1)S(1)} %get-tuple-element.161), channel_id=1, source_target_pairs={{0,1},{1,0},{2,3},{3,2},{4,5},{5,4},{6,7},{7,6},{8,9},{9,8},{10,11... | collective-permute-start | bytes 1572872 | tf_op jit(solution)/shard_map/ppermute | solution.py:268
  13.9 6.6 %collective-permute-start.4 = (bf16[208,512]{1,0:T(8,128)(2,1)S(1)}, bf16[208,512]{1,0:T(8,128)(2,1)S(1)}, u32[]{:S(2)}, u32[]{:S(2)}) collective-permute-start(bf16[208,512]{1,0:T(8,128)(2,1)S(1)} %get-tuple-element.160), channel_id=1, source_target_pairs={{0,4},{1,5},{2,6},{3,7},{4,0},{5,1},{6,2},{7,3},{8,12},{9,13},{10,... | collective-permute-start | bytes 638984 | tf_op jit(solution)/shard_map/ppermute | solution.py:268
  16.0 8.0 %collective-permute-start.3 = (bf16[288,512]{1,0:T(8,128)(2,1)S(1)}, bf16[288,512]{1,0:T(8,128)(2,1)S(1)}, u32[]{:S(2)}, u32[]{:S(2)}) collective-permute-start(bf16[288,512]{1,0:T(8,128)(2,1)S(1)} %get-tuple-element.158), channel_id=1, source_target_pairs={{0,2},{1,3},{2,0},{3,1},{4,6},{5,7},{6,4},{7,5},{8,10},{9,11},{10,... | collective-permute-start | bytes 884744 | tf_op jit(solution)/shard_map/ppermute | solution.py:268
  18.5 8.7 %collective-permute-start.7 = (bf16[320,512]{1,0:T(8,128)(2,1)S(1)}, bf16[320,512]{1,0:T(8,128)(2,1)S(1)}, u32[]{:S(2)}, u32[]{:S(2)}) collective-permute-start(bf16[320,512]{1,0:T(8,128)(2,1)S(1)} %get-tuple-element.169), channel_id=1, source_target_pairs={{0,1},{1,0},{2,3},{3,2},{4,5},{5,4},{6,7},{7,6},{8,9},{9,8},{10,11... | collective-permute-start | bytes 983048 | tf_op jit(solution)/shard_map/ppermute | solution.py:268
  24.4 7.1 %collective-permute-start.6 = (bf16[288,512]{1,0:T(8,128)(2,1)S(1)}, bf16[288,512]{1,0:T(8,128)(2,1)S(1)}, u32[]{:S(2)}, u32[]{:S(2)}) collective-permute-start(bf16[288,512]{1,0:T(8,128)(2,1)S(1)} %get-tuple-element.167), channel_id=1, source_target_pairs={{0,4},{1,5},{2,6},{3,7},{4,0},{5,1},{6,2},{7,3},{8,12},{9,13},{10,... | collective-permute-start | bytes 884744 | tf_op jit(solution)/shard_map/ppermute | solution.py:268
  25.0 9.4 %collective-permute-start.10 = (bf16[208,512]{1,0:T(8,128)(2,1)S(1)}, bf16[208,512]{1,0:T(8,128)(2,1)S(1)}, u32[]{:S(2)}, u32[]{:S(2)}) collective-permute-start(bf16[208,512]{1,0:T(8,128)(2,1)S(1)} %get-tuple-element.174.own), channel_id=1, source_target_pairs={{0,8},{1,9},{2,10},{3,11},{4,12},{5,13},{6,14},{7,15},{8,0},{9,1},... | collective-permute-start | bytes 638984 | tf_op jit(solution)/shard_map/ppermute | solution.py:268
  26.3 12.7 %collective-permute-start.12 = (bf16[2048,128]{1,0:T(8,128)(2,1)S(1)}, bf16[2048,128]{1,0:T(8,128)(2,1)S(1)}, u32[]{:S(2)}, u32[]{:S(2)}) collective-permute-start(bf16[2048,128]{1,0:T(8,128)(2,1)S(1)} %get-tuple-element.179), channel_id=1, source_target_pairs={{15,16},{16,15}} | collective-permute-start | bytes 1572872 | tf_op jit(solution)/shard_map/ppermute | solution.py:268
  27.6 9.4 %collective-permute-start.13 = (bf16[320,512]{1,0:T(8,128)(2,1)S(1)}, bf16[320,512]{1,0:T(8,128)(2,1)S(1)}, u32[]{:S(2)}, u32[]{:S(2)}) collective-permute-start(bf16[320,512]{1,0:T(8,128)(2,1)S(1)} %get-tuple-element.181), channel_id=1, source_target_pairs={{0,2},{1,3},{2,0},{3,1},{4,6},{5,7},{6,4},{7,5},{8,10},{9,11},{10,... | collective-permute-start | bytes 983048 | tf_op jit(solution)/shard_map/ppermute | solution.py:268
  31.8 9.7 %collective-permute-start.8 = (bf16[288,512]{1,0:T(8,128)(2,1)S(1)}, bf16[288,512]{1,0:T(8,128)(2,1)S(1)}, u32[]{:S(2)}, u32[]{:S(2)}) collective-permute-start(bf16[288,512]{1,0:T(8,128)(2,1)S(1)} %get-tuple-element.172.own), channel_id=1, source_target_pairs={{0,8},{1,9},{2,10},{3,11},{4,12},{5,13},{6,14},{7,15},{8,0},{9,1},... | collective-permute-start | bytes 884744 | tf_op jit(solution)/shard_map/ppermute | solution.py:268
  35.4 11.8 %collective-permute-start.17 = (bf16[208,1024]{1,0:T(8,128)(2,1)S(1)}, bf16[208,1024]{1,0:T(8,128)(2,1)S(1)}, u32[]{:S(2)}, u32[]{:S(2)}) collective-permute-start(bf16[208,1024]{1,0:T(8,128)(2,1)S(1)} %get-tuple-element.194), channel_id=1, source_target_pairs={{0,1},{1,0},{2,3},{3,2},{4,5},{5,4},{6,7},{7,6},{8,16},{9,17},{10,... | collective-permute-start | bytes 1277960 | tf_op jit(solution)/shard_map/ppermute | solution.py:268
  36.5 2.5 %collective-permute-start.11 = (bf16[352,512]{1,0:T(8,128)(2,1)S(1)}, bf16[352,512]{1,0:T(8,128)(2,1)S(1)}, u32[]{:S(2)}, u32[]{:S(2)}) collective-permute-start(bf16[352,512]{1,0:T(8,128)(2,1)S(1)} %get-tuple-element.178), channel_id=1, source_target_pairs={{0,1},{1,0},{2,3},{3,2},{4,5},{5,4},{6,7},{7,6},{8,9},{9,8},{10,11... | collective-permute-start | bytes 1081352 | tf_op jit(solution)/shard_map/ppermute | solution.py:268
  37.5 9.7 %collective-permute-start.16 = (bf16[320,512]{1,0:T(8,128)(2,1)S(1)}, bf16[320,512]{1,0:T(8,128)(2,1)S(1)}, u32[]{:S(2)}, u32[]{:S(2)}) collective-permute-start(bf16[320,512]{1,0:T(8,128)(2,1)S(1)} %get-tuple-element.191), channel_id=1, source_target_pairs={{0,4},{1,5},{2,6},{3,7},{4,0},{5,1},{6,2},{7,3},{8,12},{9,13},{10,... | collective-permute-start | bytes 983048 | tf_op jit(solution)/shard_map/ppermute | solution.py:268
  39.5 11.7 %collective-permute-start.15 = (bf16[352,512]{1,0:T(8,128)(2,1)S(1)}, bf16[352,512]{1,0:T(8,128)(2,1)S(1)}, u32[]{:S(2)}, u32[]{:S(2)}) collective-permute-start(bf16[352,512]{1,0:T(8,128)(2,1)S(1)} %get-tuple-element.189), channel_id=1, source_target_pairs={{0,2},{1,3},{2,0},{3,1},{4,6},{5,7},{6,4},{7,5},{8,10},{9,11},{10,... | collective-permute-start | bytes 1081352 | tf_op jit(solution)/shard_map/ppermute | solution.py:268
  42.8 17.2 %collective-permute-start.21 = (bf16[288,1024]{1,0:T(8,128)(2,1)S(1)}, bf16[288,1024]{1,0:T(8,128)(2,1)S(1)}, u32[]{:S(2)}, u32[]{:S(2)}) collective-permute-start(bf16[288,1024]{1,0:T(8,128)(2,1)S(1)} %get-tuple-element.207), channel_id=1, source_target_pairs={{0,1},{1,0},{2,3},{3,2},{4,5},{5,4},{6,7},{7,6},{8,16},{9,17},{10,... | collective-permute-start | bytes 1769480 | tf_op jit(solution)/shard_map/ppermute | solution.py:268
  43.9 9.4 %collective-permute-start.14 = (bf16[368,512]{1,0:T(8,128)(2,1)S(1)}, bf16[368,512]{1,0:T(8,128)(2,1)S(1)}, u32[]{:S(2)}, u32[]{:S(2)}) collective-permute-start(bf16[368,512]{1,0:T(8,128)(2,1)S(1)} %get-tuple-element.187), channel_id=1, source_target_pairs={{0,1},{1,0},{2,3},{3,2},{4,5},{5,4},{6,7},{7,6},{8,9},{9,8},{10,11... | collective-permute-start | bytes 1130504 | tf_op jit(solution)/shard_map/ppermute | solution.py:268
  47.6 11.0 %collective-permute-start.22 = (bf16[320,512]{1,0:T(8,128)(2,1)S(1)}, bf16[320,512]{1,0:T(8,128)(2,1)S(1)}, u32[]{:S(2)}, u32[]{:S(2)}) collective-permute-start(bf16[320,512]{1,0:T(8,128)(2,1)S(1)} %get-tuple-element.209), channel_id=1, source_target_pairs={{0,8},{1,9},{2,10},{3,11},{4,12},{5,13},{6,14},{7,15},{8,0},{9,1},... | collective-permute-start | bytes 983048 | tf_op jit(solution)/shard_map/ppermute | solution.py:268
  51.6 9.7 %collective-permute-start.20 = (bf16[352,512]{1,0:T(8,128)(2,1)S(1)}, bf16[352,512]{1,0:T(8,128)(2,1)S(1)}, u32[]{:S(2)}, u32[]{:S(2)}) collective-permute-start(bf16[352,512]{1,0:T(8,128)(2,1)S(1)} %get-tuple-element.204), channel_id=1, source_target_pairs={{0,4},{1,5},{2,6},{3,7},{4,0},{5,1},{6,2},{7,3},{8,12},{9,13},{10,... | collective-permute-start | bytes 1081352 | tf_op jit(solution)/shard_map/ppermute | solution.py:268
  53.7 10.2 %collective-permute-start.19 = (bf16[368,512]{1,0:T(8,128)(2,1)S(1)}, bf16[368,512]{1,0:T(8,128)(2,1)S(1)}, u32[]{:S(2)}, u32[]{:S(2)}) collective-permute-start(bf16[368,512]{1,0:T(8,128)(2,1)S(1)} %get-tuple-element.202), channel_id=1, source_target_pairs={{0,2},{1,3},{2,0},{3,1},{4,6},{5,7},{6,4},{7,5},{8,10},{9,11},{10,... | collective-permute-start | bytes 1130504 | tf_op jit(solution)/shard_map/ppermute | solution.py:268
  56.2 9.2 %collective-permute-start.18 = (bf16[336,512]{1,0:T(8,128)(2,1)S(1)}, bf16[336,512]{1,0:T(8,128)(2,1)S(1)}, u32[]{:S(2)}, u32[]{:S(2)}) collective-permute-start(bf16[336,512]{1,0:T(8,128)(2,1)S(1)} %get-tuple-element.200), channel_id=1, source_target_pairs={{0,1},{1,0},{2,3},{3,2},{4,5},{5,4},{6,7},{7,6},{8,9},{9,8},{10,11... | collective-permute-start | bytes 1032200 | tf_op jit(solution)/shard_map/ppermute | solution.py:268
  59.9 12.9 %collective-permute-start.26 = (bf16[320,1024]{1,0:T(8,128)(2,1)S(1)}, bf16[320,1024]{1,0:T(8,128)(2,1)S(1)}, u32[]{:S(2)}, u32[]{:S(2)}) collective-permute-start(bf16[320,1024]{1,0:T(8,128)(2,1)S(1)} %get-tuple-element.223), channel_id=1, source_target_pairs={{0,1},{1,0},{2,3},{3,2},{4,5},{5,4},{6,7},{7,6},{8,16},{9,17},{10,... | collective-permute-start | bytes 1966088 | tf_op jit(solution)/shard_map/ppermute | solution.py:268
  61.7 9.6 %collective-permute-start.27 = (bf16[352,512]{1,0:T(8,128)(2,1)S(1)}, bf16[352,512]{1,0:T(8,128)(2,1)S(1)}, u32[]{:S(2)}, u32[]{:S(2)}) collective-permute-start(bf16[352,512]{1,0:T(8,128)(2,1)S(1)} %get-tuple-element.225), channel_id=1, source_target_pairs={{0,8},{1,9},{2,10},{3,11},{4,12},{5,13},{6,14},{7,15},{8,0},{9,1},... | collective-permute-start | bytes 1081352 | tf_op jit(solution)/shard_map/ppermute | solution.py:268
  64.4 8.9 %collective-permute-start.25 = (bf16[368,512]{1,0:T(8,128)(2,1)S(1)}, bf16[368,512]{1,0:T(8,128)(2,1)S(1)}, u32[]{:S(2)}, u32[]{:S(2)}) collective-permute-start(bf16[368,512]{1,0:T(8,128)(2,1)S(1)} %get-tuple-element.220), channel_id=1, source_target_pairs={{0,4},{1,5},{2,6},{3,7},{4,0},{5,1},{6,2},{7,3},{8,12},{9,13},{10,... | collective-permute-start | bytes 1130504 | tf_op jit(solution)/shard_map/ppermute | solution.py:268
  65.9 7.9 %collective-permute-start.24 = (bf16[336,512]{1,0:T(8,128)(2,1)S(1)}, bf16[336,512]{1,0:T(8,128)(2,1)S(1)}, u32[]{:S(2)}, u32[]{:S(2)}) collective-permute-start(bf16[336,512]{1,0:T(8,128)(2,1)S(1)} %get-tuple-element.218), channel_id=1, source_target_pairs={{0,2},{1,3},{2,0},{3,1},{4,6},{5,7},{6,4},{7,5},{8,10},{9,11},{10,... | collective-permute-start | bytes 1032200 | tf_op jit(solution)/shard_map/ppermute | solution.py:268
  67.7 14.4 %collective-permute-start.23 = (bf16[176,512]{1,0:T(8,128)(2,1)S(1)}, bf16[176,512]{1,0:T(8,128)(2,1)S(1)}, u32[]{:S(2)}, u32[]{:S(2)}) collective-permute-start(bf16[176,512]{1,0:T(8,128)(2,1)S(1)} %get-tuple-element.216), channel_id=1, source_target_pairs={{0,1},{1,0},{2,3},{3,2},{4,5},{5,4},{6,7},{7,6},{8,9},{9,8},{10,11... | collective-permute-start | bytes 540680 | tf_op jit(solution)/shard_map/ppermute | solution.py:268
  72.7 16.4 %collective-permute-start.32 = (bf16[352,1024]{1,0:T(8,128)(2,1)S(1)}, bf16[352,1024]{1,0:T(8,128)(2,1)S(1)}, u32[]{:S(2)}, u32[]{:S(2)}) collective-permute-start(bf16[352,1024]{1,0:T(8,128)(2,1)S(1)} %get-tuple-element.242), channel_id=1, source_target_pairs={{0,1},{1,0},{2,3},{3,2},{4,5},{5,4},{6,7},{7,6},{8,16},{9,17},{10,... | collective-permute-start | bytes 2162696 | tf_op jit(solution)/shard_map/ppermute | solution.py:268
  74.3 14.9 %collective-permute-start.31 = (bf16[336,512]{1,0:T(8,128)(2,1)S(1)}, bf16[336,512]{1,0:T(8,128)(2,1)S(1)}, u32[]{:S(2)}, u32[]{:S(2)}) collective-permute-start(bf16[336,512]{1,0:T(8,128)(2,1)S(1)} %get-tuple-element.239), channel_id=1, source_target_pairs={{0,4},{1,5},{2,6},{3,7},{4,0},{5,1},{6,2},{7,3},{8,12},{9,13},{10,... | collective-permute-start | bytes 1032200 | tf_op jit(solution)/shard_map/ppermute | solution.py:268
  75.5 12.2 %collective-permute-start.29 = (bf16[368,512]{1,0:T(8,128)(2,1)S(1)}, bf16[368,512]{1,0:T(8,128)(2,1)S(1)}, u32[]{:S(2)}, u32[]{:S(2)}) collective-permute-start(bf16[368,512]{1,0:T(8,128)(2,1)S(1)} %get-tuple-element.233), channel_id=1, source_target_pairs={{0,8},{1,9},{2,10},{3,11},{4,12},{5,13},{6,14},{7,15},{8,0},{9,1},... | collective-permute-start | bytes 1130504 | tf_op jit(solution)/shard_map/ppermute | solution.py:268
  82.6 12.3 %collective-permute-start.30 = (bf16[2048,128]{1,0:T(8,128)(2,1)S(1)}, bf16[2048,128]{1,0:T(8,128)(2,1)S(1)}, u32[]{:S(2)}, u32[]{:S(2)}) collective-permute-start(bf16[2048,128]{1,0:T(8,128)(2,1)S(1)} %get-tuple-element.235), channel_id=1, source_target_pairs={{1,2},{2,1},{3,4},{4,3},{5,6},{6,5},{7,8},{8,7},{9,10},{10,9},{11,... | collective-permute-start | bytes 1572872 | tf_op jit(solution)/shard_map/ppermute | solution.py:268
  83.5 18.9 %collective-permute-start.28 = (bf16[176,512]{1,0:T(8,128)(2,1)S(1)}, bf16[176,512]{1,0:T(8,128)(2,1)S(1)}, u32[]{:S(2)}, u32[]{:S(2)}) collective-permute-start(bf16[176,512]{1,0:T(8,128)(2,1)S(1)} %get-tuple-element.231), channel_id=1, source_target_pairs={{0,2},{1,3},{2,0},{3,1},{4,6},{5,7},{6,4},{7,5},{8,10},{9,11},{10,... | collective-permute-start | bytes 540680 | tf_op jit(solution)/shard_map/ppermute | solution.py:268
  89.1 20.6 %collective-permute-start.34 = (bf16[368,1024]{1,0:T(8,128)(2,1)S(1)}, bf16[368,1024]{1,0:T(8,128)(2,1)S(1)}, u32[]{:S(2)}, u32[]{:S(2)}) collective-permute-start(bf16[368,1024]{1,0:T(8,128)(2,1)S(1)} %get-tuple-element.256), channel_id=1, source_target_pairs={{0,1},{1,0},{2,3},{3,2},{4,5},{5,4},{6,7},{7,6},{8,16},{9,17},{10,... | collective-permute-start | bytes 2261000 | tf_op jit(solution)/shard_map/ppermute | solution.py:268
  89.2 5.7 %copy-start.2 = (bf16[2,768,512]{2,1,0:T(8,128)(2,1)S(1)}, bf16[2,768,512]{2,1,0:T(8,128)(2,1)}, u32[]{:S(2)}) copy-start(bf16[2,768,512]{2,1,0:T(8,128)(2,1)} %near.13) | copy-start | bytes 4718596
  89.2 5.7 %copy-start.4 = (bf16[2,256,512]{2,1,0:T(8,128)(2,1)S(1)}, bf16[2,256,512]{2,1,0:T(8,128)(2,1)}, u32[]{:S(2)}) copy-start(bf16[2,256,512]{2,1,0:T(8,128)(2,1)} %out_basis.13) | copy-start | bytes 1572868
  89.7 15.7 %collective-permute-start.35 = (bf16[352,512]{1,0:T(8,128)(2,1)S(1)}, bf16[352,512]{1,0:T(8,128)(2,1)S(1)}, u32[]{:S(2)}, u32[]{:S(2)}) collective-permute-start(bf16[352,512]{1,0:T(8,128)(2,1)S(1)} %get-tuple-element.258), channel_id=1, source_target_pairs={{0,8},{1,9},{2,10},{3,11},{4,12},{5,13},{6,14},{7,15},{8,0},{9,1},... | collective-permute-start | bytes 1081352 | tf_op jit(solution)/shard_map/ppermute | solution.py:268
  102.7 6.9 %collective-permute-start.33 = (bf16[176,512]{1,0:T(8,128)(2,1)S(1)}, bf16[176,512]{1,0:T(8,128)(2,1)S(1)}, u32[]{:S(2)}, u32[]{:S(2)}) collective-permute-start(bf16[176,512]{1,0:T(8,128)(2,1)S(1)} %get-tuple-element.253), channel_id=1, source_target_pairs={{0,4},{1,5},{2,6},{3,7},{4,0},{5,1},{6,2},{7,3},{8,12},{9,13},{10,... | collective-permute-start | bytes 540680 | tf_op jit(solution)/shard_map/ppermute | solution.py:268
  106.7 16.2 %collective-permute-start.38 = (bf16[336,1024]{1,0:T(8,128)(2,1)S(1)}, bf16[336,1024]{1,0:T(8,128)(2,1)S(1)}, u32[]{:S(2)}, u32[]{:S(2)}) collective-permute-start(bf16[336,1024]{1,0:T(8,128)(2,1)S(1)} %get-tuple-element.273), channel_id=1, source_target_pairs={{0,1},{1,0},{2,3},{3,2},{4,5},{5,4},{6,7},{7,6},{8,16},{9,17},{10,... | collective-permute-start | bytes 2064392 | tf_op jit(solution)/shard_map/ppermute | solution.py:268
  110.1 11.6 %collective-permute-start.36 = (bf16[368,512]{1,0:T(8,128)(2,1)S(1)}, bf16[368,512]{1,0:T(8,128)(2,1)S(1)}, u32[]{:S(2)}, u32[]{:S(2)}) collective-permute-start(bf16[368,512]{1,0:T(8,128)(2,1)S(1)} %get-tuple-element.262), channel_id=1, source_target_pairs={{0,8},{1,9},{2,10},{3,11},{4,12},{5,13},{6,14},{7,15},{8,0},{9,1},... | collective-permute-start | bytes 1130504 | tf_op jit(solution)/shard_map/ppermute | solution.py:268
  122.7 4.6 %collective-permute-start.37 = (bf16[176,1024]{1,0:T(8,128)(2,1)S(1)}, bf16[176,1024]{1,0:T(8,128)(2,1)S(1)}, u32[]{:S(2)}, u32[]{:S(2)}) collective-permute-start(bf16[176,1024]{1,0:T(8,128)(2,1)S(1)} %get-tuple-element.269), channel_id=1, source_target_pairs={{0,1},{1,0},{2,3},{3,2},{4,5},{5,4},{6,7},{7,6},{8,16},{9,17},{10,... | collective-permute-start | bytes 1081352 | tf_op jit(solution)/shard_map/ppermute | solution.py:268
  123.2 10.9 %collective-permute-start.40 = (bf16[336,512]{1,0:T(8,128)(2,1)S(1)}, bf16[336,512]{1,0:T(8,128)(2,1)S(1)}, u32[]{:S(2)}, u32[]{:S(2)}) collective-permute-start(bf16[336,512]{1,0:T(8,128)(2,1)S(1)} %get-tuple-element.281), channel_id=1, source_target_pairs={{0,8},{1,9},{2,10},{3,11},{4,12},{5,13},{6,14},{7,15},{8,0},{9,1},... | collective-permute-start | bytes 1032200 | tf_op jit(solution)/shard_map/ppermute | solution.py:268
  127.6 10.0 %collective-permute-start.39 = (bf16[176,512]{1,0:T(8,128)(2,1)S(1)}, bf16[176,512]{1,0:T(8,128)(2,1)S(1)}, u32[]{:S(2)}, u32[]{:S(2)}) collective-permute-start(bf16[176,512]{1,0:T(8,128)(2,1)S(1)} %get-tuple-element.279), channel_id=1, source_target_pairs={{0,8},{1,9},{2,10},{3,11},{4,12},{5,13},{6,14},{7,15},{8,0},{9,1},... | collective-permute-start | bytes 540680 | tf_op jit(solution)/shard_map/ppermute | solution.py:268

commit v4 on v3

--- a/solution.py
+++ b/solution.py
@@ -9,7 +9,7 @@
 
 BF16 = jnp.bfloat16
 F32 = jnp.float32
-SHARES = (13, 18, 20, 22, 23, 21, 11)
+SHARES = (15, 21, 25, 28, 25, 14)
 
 
 def dot(a, b):
@@ -31,8 +31,6 @@
         new, old = turn - inward, turn - inward - 2
         if turn == inward:
             order.append(("take", "chip"))
-        if turn == inward:
-            order.append(("rims", "middle"))
         if new >= 0 and new != 1:
             order.append(("turn", pieces[new] if new < count else None, pieces[old] if old >= 0 else None))
         if turn > count:
@@ -45,7 +43,7 @@
             if 0 <= turn - level < count:
                 order.append(("level", pieces[turn - level], level))
         if turn == inward:
-            order += [("turn", pieces[1], None), ("relay", pieces[new])]
+            order += [("rims", "middle"), ("turn", pieces[1], None), ("relay", pieces[new])]
         if turn == inward + 1:
             order.append(("relay", pieces[new]))
         if turn < count:

time: 140 us -> 138 us (0.986)
  Pallas kernels: 39.2 us -> 36.2 us
  waiting for transfers between devices: 41 us -> 43.3 us
    pallas_call x50 -> x44, Pallas kernels: 39.2 us -> 36.2 us  [call(): pl.pallas_call(body, in_specs=in_specs, out_specs=out_specs, out_shape=ou...]
    ppermute x41 -> x36, waiting for transfers between devices: 41 us -> 43.3 us  [per_device(): send = lambda operand, pairs: lax.ppermute(operand, 'box', pairs)]
    ppermute x41 -> x36, starting transfers between devices: 58.9 us -> 57.9 us  [per_device(): send = lambda operand, pairs: lax.ppermute(operand, 'box', pairs)]
  transfers between devices with their start and end apart: 41 -> 36, of which waited for: 16 -> 14; matrix products, arithmetic and copies ran while one was open for 0% -> 0% of each run, Pallas kernels for 25% -> 23%
where the time goes in v4:
time: 138 us
  starting transfers between devices  57.9 us (42%)
  waiting for transfers between devices  43.3 us (31%)
  Pallas kernels  36.2 us (26%)
    ppermute x36, starting transfers between devices, per_device(): send = lambda operand, pairs: lax.ppermute(operand, 'box', pairs)  57.9 us
    ppermute x36, waiting for transfers between devices, per_device(): send = lambda operand, pairs: lax.ppermute(operand, 'box', pairs)  43.3 us
    pallas_call x44, Pallas kernels, call(): pl.pallas_call(body, in_specs=in_specs, out_specs=out_specs, out_shape=ou...  36.2 us
  transfers between devices with their start and end apart: 36, of which 14 were waited for; matrix products, arithmetic and copies ran while one was open for 0% of the time, Pallas kernels for 23%

profile of v4, /device:TPU:0, one launch (start us, length us, event | category | flops | bytes accessed | tf_op | source)
XLA Modules:
  0.0 138.0 jit_solution(13400917713088850700)
XLA Ops:
  0.0 2.6 %leaf.12 = (bf16[240,512]{1,0:T(8,128)(2,1)S(1)}, bf16[240,512]{1,0:T(8,128)(2,1)S(1)}, bf16[4,2,256,256]{3,2,1,0:T(8,128)(2,1)S(1)}, f32[8,128]{1,0:T(8,128)S(1)}) custom-call(f32[2048,1024]{1,0:T(8,128)} %src.29, bf16[2,512,256]{2,1,0:T(8,128)(2,1)} %leaf.23, bf16[6,2,256,256]{3,2,1,0:T(8,128)(2,1)} %refs_4_.3, bf16[6,2,256,256]{3,2,1,0:T(8,128)(2,1)} %cross.47, ...), custom_call_target="tpu_custom_call" | custom-call | flops 3000000000 | bytes 1 | tf_op jit(solution)/shard_map/leaf/pallas_call | solution.py:235
  3.2 2.7 %collective-permute-start.9 = (bf16[4,2,256,256]{3,2,1,0:T(8,128)(2,1)S(1)}, bf16[4,2,256,256]{3,2,1,0:T(8,128)(2,1)S(1)}, u32[]{:S(2)}, u32[]{:S(2)}) collective-permute-start(bf16[4,2,256,256]{3,2,1,0:T(8,128)(2,1)S(1)} %get-tuple-element.154), channel_id=1, source_target_pairs={{0,8},{1,9},{2,10},{3,11},{4,12},{5,13},{6,14},{7,15},{8,0},{9,1},... | collective-permute-start | bytes 3145736 | tf_op jit(solution)/shard_map/ppermute | solution.py:266
  6.3 1.6 %collective-permute-start.2 = (bf16[240,512]{1,0:T(8,128)(2,1)S(1)}, bf16[240,512]{1,0:T(8,128)(2,1)S(1)}, u32[]{:S(2)}, u32[]{:S(2)}) collective-permute-start(bf16[240,512]{1,0:T(8,128)(2,1)S(1)} %get-tuple-element.134), channel_id=1, source_target_pairs={{0,2},{1,3},{2,0},{3,1},{4,6},{5,7},{6,4},{7,5},{8,10},{9,11},{10,... | collective-permute-start | bytes 737288 | tf_op jit(solution)/shard_map/ppermute | solution.py:266
  7.8 1.0 leaf.14
  9.6 4.7 %collective-permute-done.2.moved = bf16[240,512]{1,0:T(8,128)(2,1)S(1)} collective-permute-done((bf16[240,512]{1,0:T(8,128)(2,1)S(1)}, bf16[240,512]{1,0:T(8,128)(2,1)S(1)}, u32[]{:S(2)}, u32[]{:S(2)}) %collective-permute-start.2) | collective-permute-done | bytes 245792 | tf_op jit(solution)/shard_map/ppermute | solution.py:266
  14.8 1.6 %collective-permute-start.4 = (bf16[240,512]{1,0:T(8,128)(2,1)S(1)}, bf16[240,512]{1,0:T(8,128)(2,1)S(1)}, u32[]{:S(2)}, u32[]{:S(2)}) collective-permute-start(bf16[240,512]{1,0:T(8,128)(2,1)S(1)} %get-tuple-element.141), channel_id=1, source_target_pairs={{0,4},{1,5},{2,6},{3,7},{4,0},{5,1},{6,2},{7,3},{8,12},{9,13},{10,... | collective-permute-start | bytes 737288 | tf_op jit(solution)/shard_map/ppermute | solution.py:266
  16.8 1.6 %collective-permute-start.3 = (bf16[336,512]{1,0:T(8,128)(2,1)S(1)}, bf16[336,512]{1,0:T(8,128)(2,1)S(1)}, u32[]{:S(2)}, u32[]{:S(2)}) collective-permute-start(bf16[336,512]{1,0:T(8,128)(2,1)S(1)} %get-tuple-element.139), channel_id=1, source_target_pairs={{0,2},{1,3},{2,0},{3,1},{4,6},{5,7},{6,4},{7,5},{8,10},{9,11},{10,... | collective-permute-start | bytes 1032200 | tf_op jit(solution)/shard_map/ppermute | solution.py:266
  18.4 1.0 leaf.16
  19.5 2.5 %collective-permute-done.4.moved = bf16[240,512]{1,0:T(8,128)(2,1)S(1)} collective-permute-done((bf16[240,512]{1,0:T(8,128)(2,1)S(1)}, bf16[240,512]{1,0:T(8,128)(2,1)S(1)}, u32[]{:S(2)}, u32[]{:S(2)}) %collective-permute-start.4) | collective-permute-done | bytes 245792 | tf_op jit(solution)/shard_map/ppermute | solution.py:266
  22.3 1.4 %collective-permute-start.10 = (bf16[240,512]{1,0:T(8,128)(2,1)S(1)}, bf16[240,512]{1,0:T(8,128)(2,1)S(1)}, u32[]{:S(2)}, u32[]{:S(2)}) collective-permute-start(bf16[240,512]{1,0:T(8,128)(2,1)S(1)} %get-tuple-element.155.own), channel_id=1, source_target_pairs={{0,8},{1,9},{2,10},{3,11},{4,12},{5,13},{6,14},{7,15},{8,0},{9,1},... | collective-permute-start | bytes 737288 | tf_op jit(solution)/shard_map/ppermute | solution.py:266
  23.7 2.2 %collective-permute-done.3.moved = bf16[336,512]{1,0:T(8,128)(2,1)S(1)} collective-permute-done((bf16[336,512]{1,0:T(8,128)(2,1)S(1)}, bf16[336,512]{1,0:T(8,128)(2,1)S(1)}, u32[]{:S(2)}, u32[]{:S(2)}) %collective-permute-start.3) | collective-permute-done | bytes 344096 | tf_op jit(solution)/shard_map/ppermute | solution.py:266
  27.4 1.6 %collective-permute-start.13 = (bf16[400,512]{1,0:T(8,128)(2,1)S(1)}, bf16[400,512]{1,0:T(8,128)(2,1)S(1)}, u32[]{:S(2)}, u32[]{:S(2)}) collective-permute-start(bf16[400,512]{1,0:T(8,128)(2,1)S(1)} %get-tuple-element.162), channel_id=1, source_target_pairs={{0,2},{1,3},{2,0},{3,1},{4,6},{5,7},{6,4},{7,5},{8,10},{9,11},{10,... | collective-permute-start | bytes 1228808 | tf_op jit(solution)/shard_map/ppermute | solution.py:266
  30.0 4.5 %collective-permute-done.6.moved = bf16[336,512]{1,0:T(8,128)(2,1)S(1)} collective-permute-done((bf16[336,512]{1,0:T(8,128)(2,1)S(1)}, bf16[336,512]{1,0:T(8,128)(2,1)S(1)}, u32[]{:S(2)}, u32[]{:S(2)}) %collective-permute-start.6) | collective-permute-done | bytes 344096 | tf_op jit(solution)/shard_map/ppermute | solution.py:266
  34.8 1.4 %collective-permute-start.8 = (bf16[336,512]{1,0:T(8,128)(2,1)S(1)}, bf16[336,512]{1,0:T(8,128)(2,1)S(1)}, u32[]{:S(2)}, u32[]{:S(2)}) collective-permute-start(bf16[336,512]{1,0:T(8,128)(2,1)S(1)} %get-tuple-element.153.own), channel_id=1, source_target_pairs={{0,8},{1,9},{2,10},{3,11},{4,12},{5,13},{6,14},{7,15},{8,0},{9,1},... | collective-permute-start | bytes 1032200 | tf_op jit(solution)/shard_map/ppermute | solution.py:266
  36.2 1.1 relay.6
  37.4 1.1 leaf.18
  39.6 0.9 collective-permute-start.16
  41.0 1.6 %collective-permute-start.15 = (bf16[448,512]{1,0:T(8,128)(2,1)S(1)}, bf16[448,512]{1,0:T(8,128)(2,1)S(1)}, u32[]{:S(2)}, u32[]{:S(2)}) collective-permute-start(bf16[448,512]{1,0:T(8,128)(2,1)S(1)} %get-tuple-element.170), channel_id=1, source_target_pairs={{0,2},{1,3},{2,0},{3,1},{4,6},{5,7},{6,4},{7,5},{8,10},{9,11},{10,... | collective-permute-start | bytes 1376264 | tf_op jit(solution)/shard_map/ppermute | solution.py:266
  42.6 1.3 relay.7
  44.1 1.0 leaf.20
  45.7 5.4 %collective-permute-done.16.refs_1_ = bf16[400,512]{1,0:T(8,128)(2,1)S(1)} collective-permute-done((bf16[400,512]{1,0:T(8,128)(2,1)S(1)}, bf16[400,512]{1,0:T(8,128)(2,1)S(1)}, u32[]{:S(2)}, u32[]{:S(2)}) %collective-permute-start.16) | collective-permute-done | bytes 409632 | tf_op jit(solution)/shard_map/ppermute | solution.py:266
  51.5 3.2 %collective-permute-start.22 = (bf16[400,512]{1,0:T(8,128)(2,1)S(1)}, bf16[400,512]{1,0:T(8,128)(2,1)S(1)}, u32[]{:S(2)}, u32[]{:S(2)}) collective-permute-start(bf16[400,512]{1,0:T(8,128)(2,1)S(1)} %get-tuple-element.190), channel_id=1, source_target_pairs={{0,8},{1,9},{2,10},{3,11},{4,12},{5,13},{6,14},{7,15},{8,0},{9,1},... | collective-permute-start | bytes 1228808 | tf_op jit(solution)/shard_map/ppermute | solution.py:266
  55.1 0.9 collective-permute-start.20
  56.6 1.6 %collective-permute-start.19 = (bf16[400,512]{1,0:T(8,128)(2,1)S(1)}, bf16[400,512]{1,0:T(8,128)(2,1)S(1)}, u32[]{:S(2)}, u32[]{:S(2)}) collective-permute-start(bf16[400,512]{1,0:T(8,128)(2,1)S(1)} %get-tuple-element.183), channel_id=1, source_target_pairs={{0,2},{1,3},{2,0},{3,1},{4,6},{5,7},{6,4},{7,5},{8,10},{9,11},{10,... | collective-permute-start | bytes 1228808 | tf_op jit(solution)/shard_map/ppermute | solution.py:266
  59.0 3.9 %collective-permute-done.22.other.back = bf16[400,512]{1,0:T(8,128)(2,1)S(1)} collective-permute-done((bf16[400,512]{1,0:T(8,128)(2,1)S(1)}, bf16[400,512]{1,0:T(8,128)(2,1)S(1)}, u32[]{:S(2)}, u32[]{:S(2)}) %collective-permute-start.22) | collective-permute-done | bytes 409632 | tf_op jit(solution)/shard_map/ppermute | solution.py:266
  62.9 1.5 %relay.8 = (bf16[400,512]{1,0:T(8,128)(2,1)S(1)}, bf16[400,512]{1,0:T(8,128)(2,1)S(1)}, bf16[400,1024]{1,0:T(8,128)(2,1)S(1)}, f32[8,128]{1,0:T(8,128)S(1)}) custom-call(bf16[400,512]{1,0:T(8,128)(2,1)S(1)} %get-tuple-element.189.own, bf16[400,512]{1,0:T(8,128)(2,1)S(1)} %collective-permute-done.22.other.back, bf16[6,2,256,256]{3,2,1,0:T(8,128)(2,1)S(1)} %copy-done.1, ...), custom_call_target="tpu_custom_call" | custom-call | flops 10000000 | bytes 1 | tf_op jit(solution)/shard_map/relay/pallas_call | solution.py:235
  64.5 2.0 %collective-permute-done.20.refs_1_ = bf16[448,512]{1,0:T(8,128)(2,1)S(1)} collective-permute-done((bf16[448,512]{1,0:T(8,128)(2,1)S(1)}, bf16[448,512]{1,0:T(8,128)(2,1)S(1)}, u32[]{:S(2)}, u32[]{:S(2)}) %collective-permute-start.20) | collective-permute-done | bytes 458784 | tf_op jit(solution)/shard_map/ppermute | solution.py:266
  67.6 1.4 collective-permute-start.26
  68.9 1.6 %collective-permute-start.24 = (bf16[448,512]{1,0:T(8,128)(2,1)S(1)}, bf16[448,512]{1,0:T(8,128)(2,1)S(1)}, u32[]{:S(2)}, u32[]{:S(2)}) collective-permute-start(bf16[448,512]{1,0:T(8,128)(2,1)S(1)} %get-tuple-element.198), channel_id=1, source_target_pairs={{0,8},{1,9},{2,10},{3,11},{4,12},{5,13},{6,14},{7,15},{8,0},{9,1},... | collective-permute-start | bytes 1376264 | tf_op jit(solution)/shard_map/ppermute | solution.py:266
  72.0 2.2 %collective-permute-start.23 = (bf16[224,512]{1,0:T(8,128)(2,1)S(1)}, bf16[224,512]{1,0:T(8,128)(2,1)S(1)}, u32[]{:S(2)}, u32[]{:S(2)}) collective-permute-start(bf16[224,512]{1,0:T(8,128)(2,1)S(1)} %get-tuple-element.196), channel_id=1, source_target_pairs={{0,2},{1,3},{2,0},{3,1},{4,6},{5,7},{6,4},{7,5},{8,10},{9,11},{10,... | collective-permute-start | bytes 688136 | tf_op jit(solution)/shard_map/ppermute | solution.py:266
  74.2 5.8 %collective-permute-done.24.other.back = bf16[448,512]{1,0:T(8,128)(2,1)S(1)} collective-permute-done((bf16[448,512]{1,0:T(8,128)(2,1)S(1)}, bf16[448,512]{1,0:T(8,128)(2,1)S(1)}, u32[]{:S(2)}, u32[]{:S(2)}) %collective-permute-start.24) | collective-permute-done | bytes 458784 | tf_op jit(solution)/shard_map/ppermute | solution.py:266
  80.0 1.6 %relay.9 = (bf16[448,512]{1,0:T(8,128)(2,1)S(1)}, bf16[448,512]{1,0:T(8,128)(2,1)S(1)}, bf16[448,1024]{1,0:T(8,128)(2,1)S(1)}, f32[8,128]{1,0:T(8,128)S(1)}) custom-call(bf16[448,512]{1,0:T(8,128)(2,1)S(1)} %get-tuple-element.207.own, bf16[448,512]{1,0:T(8,128)(2,1)S(1)} %collective-permute-done.24.other.back, bf16[6,2,256,256]{3,2,1,0:T(8,128)(2,1)S(1)} %copy-done.1, ...), custom_call_target="tpu_custom_call" | custom-call | flops 10000000 | bytes 1 | tf_op jit(solution)/shard_map/relay/pallas_call | solution.py:235
  82.2 4.3 %collective-permute-start.30 = (bf16[400,512]{1,0:T(8,128)(2,1)S(1)}, bf16[400,512]{1,0:T(8,128)(2,1)S(1)}, u32[]{:S(2)}, u32[]{:S(2)}) collective-permute-start(bf16[400,512]{1,0:T(8,128)(2,1)S(1)} %get-tuple-element.220), channel_id=1, source_target_pairs={{0,8},{1,9},{2,10},{3,11},{4,12},{5,13},{6,14},{7,15},{8,0},{9,1},... | collective-permute-start | bytes 1228808 | tf_op jit(solution)/shard_map/ppermute | solution.py:266
  86.6 1.6 %last.6 = (f32[2048,1024]{1,0:T(8,128)}, f32[8,128]{1,0:T(8,128)S(1)}) custom-call(bf16[240,512]{1,0:T(8,128)(2,1)S(1)} %get-tuple-element.201.own, bf16[400,512]{1,0:T(8,128)(2,1)S(1)} %collective-permute-done.22.other.back, bf16[2,256,512]{2,1,0:T(8,128)(2,1)S(1)} %copy-done.4, bf16[2,768,512]{2,1,0:T(8,128)(2,1)S(1)} %copy-done.2, ...), custom_call_target="tpu_custom_call" | custom-call | flops 10000000 | bytes 1 | tf_op jit(solution)/shard_map/last/pallas_call | solution.py:235
  88.2 1.9 %last.7 = (f32[2048,1024]{1,0:T(8,128)}, f32[8,128]{1,0:T(8,128)S(1)}) custom-call(bf16[336,512]{1,0:T(8,128)(2,1)S(1)} %get-tuple-element.197.own, bf16[448,512]{1,0:T(8,128)(2,1)S(1)} %collective-permute-done.24.other.back, bf16[2,256,512]{2,1,0:T(8,128)(2,1)S(1)} %copy-done.4, ...), custom_call_target="tpu_custom_call", output_to_operand_aliasing={{0}: (9, {})} | custom-call | flops 10000000 | bytes 1 | tf_op jit(solution)/shard_map/last/pallas_call | solution.py:235
  90.7 3.0 %collective-permute-start.28 = (bf16[224,512]{1,0:T(8,128)(2,1)S(1)}, bf16[224,512]{1,0:T(8,128)(2,1)S(1)}, u32[]{:S(2)}, u32[]{:S(2)}) collective-permute-start(bf16[224,512]{1,0:T(8,128)(2,1)S(1)} %get-tuple-element.215), channel_id=1, source_target_pairs={{0,4},{1,5},{2,6},{3,7},{4,0},{5,1},{6,2},{7,3},{8,12},{9,13},{10,... | collective-permute-start | bytes 688136 | tf_op jit(solution)/shard_map/ppermute | solution.py:266
  94.5 1.5 %relay.10 = (bf16[400,512]{1,0:T(8,128)(2,1)S(1)}, bf16[400,512]{1,0:T(8,128)(2,1)S(1)}, bf16[400,1024]{1,0:T(8,128)(2,1)S(1)}, f32[8,128]{1,0:T(8,128)S(1)}) custom-call(bf16[400,512]{1,0:T(8,128)(2,1)S(1)} %get-tuple-element.219.own, bf16[400,512]{1,0:T(8,128)(2,1)S(1)} %collective-permute-done.30.other.back, bf16[6,2,256,256]{3,2,1,0:T(8,128)(2,1)S(1)} %copy-done.1, ...), custom_call_target="tpu_custom_call" | custom-call | flops 10000000 | bytes 1 | tf_op jit(solution)/shard_map/relay/pallas_call | solution.py:235
  96.0 3.7 %collective-permute-done.28.refs_1_ = bf16[224,512]{1,0:T(8,128)(2,1)S(1)} collective-permute-done((bf16[224,512]{1,0:T(8,128)(2,1)S(1)}, bf16[224,512]{1,0:T(8,128)(2,1)S(1)}, u32[]{:S(2)}, u32[]{:S(2)}) %collective-permute-start.28) | collective-permute-done | bytes 229408 | tf_op jit(solution)/shard_map/ppermute | solution.py:266
  100.2 6.0 %collective-permute-start.31 = (bf16[448,512]{1,0:T(8,128)(2,1)S(1)}, bf16[448,512]{1,0:T(8,128)(2,1)S(1)}, u32[]{:S(2)}, u32[]{:S(2)}) collective-permute-start(bf16[448,512]{1,0:T(8,128)(2,1)S(1)} %get-tuple-element.224), channel_id=1, source_target_pairs={{0,8},{1,9},{2,10},{3,11},{4,12},{5,13},{6,14},{7,15},{8,0},{9,1},... | collective-permute-start | bytes 1376264 | tf_op jit(solution)/shard_map/ppermute | solution.py:266
  106.2 2.0 %last.8 = (f32[2048,1024]{1,0:T(8,128)}, f32[8,128]{1,0:T(8,128)S(1)}) custom-call(bf16[400,512]{1,0:T(8,128)(2,1)S(1)} %get-tuple-element.225.own, bf16[400,512]{1,0:T(8,128)(2,1)S(1)} %collective-permute-done.30.other.back, bf16[2,256,512]{2,1,0:T(8,128)(2,1)S(1)} %copy-done.4, ...), custom_call_target="tpu_custom_call", output_to_operand_aliasing={{0}: (9, {})} | custom-call | flops 10000000 | bytes 1 | tf_op jit(solution)/shard_map/last/pallas_call | solution.py:235
  108.2 5.2 %collective-permute-done.31.other.back = bf16[448,512]{1,0:T(8,128)(2,1)S(1)} collective-permute-done((bf16[448,512]{1,0:T(8,128)(2,1)S(1)}, bf16[448,512]{1,0:T(8,128)(2,1)S(1)}, u32[]{:S(2)}, u32[]{:S(2)}) %collective-permute-start.31) | collective-permute-done | bytes 458784 | tf_op jit(solution)/shard_map/ppermute | solution.py:266
  113.4 1.1 relay.11
  115.0 8.7 %collective-permute-start.35 = (bf16[400,512]{1,0:T(8,128)(2,1)S(1)}, bf16[400,512]{1,0:T(8,128)(2,1)S(1)}, u32[]{:S(2)}, u32[]{:S(2)}) collective-permute-start(bf16[400,512]{1,0:T(8,128)(2,1)S(1)} %get-tuple-element.243), channel_id=1, source_target_pairs={{0,8},{1,9},{2,10},{3,11},{4,12},{5,13},{6,14},{7,15},{8,0},{9,1},... | collective-permute-start | bytes 1228808 | tf_op jit(solution)/shard_map/ppermute | solution.py:266
  123.7 2.1 %last.9 = (f32[2048,1024]{1,0:T(8,128)}, f32[8,128]{1,0:T(8,128)S(1)}) custom-call(bf16[448,512]{1,0:T(8,128)(2,1)S(1)} %get-tuple-element.232.own, bf16[448,512]{1,0:T(8,128)(2,1)S(1)} %collective-permute-done.31.other.back, bf16[2,256,512]{2,1,0:T(8,128)(2,1)S(1)} %copy-done.4, ...), custom_call_target="tpu_custom_call", output_to_operand_aliasing={{0}: (9, {})} | custom-call | flops 10000000 | bytes 1 | tf_op jit(solution)/shard_map/last/pallas_call | solution.py:235
  126.1 5.5 %collective-permute-start.34 = (bf16[224,512]{1,0:T(8,128)(2,1)S(1)}, bf16[224,512]{1,0:T(8,128)(2,1)S(1)}, u32[]{:S(2)}, u32[]{:S(2)}) collective-permute-start(bf16[224,512]{1,0:T(8,128)(2,1)S(1)} %get-tuple-element.241), channel_id=1, source_target_pairs={{0,8},{1,9},{2,10},{3,11},{4,12},{5,13},{6,14},{7,15},{8,0},{9,1},... | collective-permute-start | bytes 688136 | tf_op jit(solution)/shard_map/ppermute | solution.py:266
  131.6 2.0 %last.10 = (f32[2048,1024]{1,0:T(8,128)}, f32[8,128]{1,0:T(8,128)S(1)}) custom-call(bf16[400,512]{1,0:T(8,128)(2,1)S(1)} %get-tuple-element.242.own, bf16[400,512]{1,0:T(8,128)(2,1)S(1)} %collective-permute-done.35.back, bf16[2,256,512]{2,1,0:T(8,128)(2,1)S(1)} %copy-done.4, bf16[2,768,512]{2,1,0:T(8,128)(2,1)S(1)} %copy-done.2, ...), custom_call_target="tpu_custom_call", output_to_operand_aliasing={{0}: (9, {})} | custom-call | flops 10000000 | bytes 1 | tf_op jit(solution)/shard_map/last/pallas_call | solution.py:235
  133.6 2.1 %collective-permute-done.34.back = bf16[224,512]{1,0:T(8,128)(2,1)S(1)} collective-permute-done((bf16[224,512]{1,0:T(8,128)(2,1)S(1)}, bf16[224,512]{1,0:T(8,128)(2,1)S(1)}, u32[]{:S(2)}, u32[]{:S(2)}) %collective-permute-start.34) | collective-permute-done | bytes 229408 | tf_op jit(solution)/shard_map/ppermute | solution.py:266
  135.7 2.2 %last.11 = (f32[2048,1024]{1,0:T(8,128)}, f32[8,128]{1,0:T(8,128)}) custom-call(bf16[224,512]{1,0:T(8,128)(2,1)S(1)} %get-tuple-element.240.own, bf16[224,512]{1,0:T(8,128)(2,1)S(1)} %collective-permute-done.34.back, bf16[2,256,512]{2,1,0:T(8,128)(2,1)S(1)} %copy-done.4, bf16[2,768,512]{2,1,0:T(8,128)(2,1)S(1)} %copy-done.2, ...), custom_call_target="tpu_custom_call", output_to_operand_aliasing={{0}: (9, {})} | custom-call | flops 10000000 | bytes 1 | tf_op jit(solution)/shard_map/last/pallas_call | solution.py:235
  (84 shorter events, 16.2 us)
Async XLA Ops:
  0.0 5.9 %copy-start.1 = (bf16[6,2,256,256]{3,2,1,0:T(8,128)(2,1)S(1)}, bf16[6,2,256,256]{3,2,1,0:T(8,128)(2,1)}, u32[]{:S(2)}) copy-start(bf16[6,2,256,256]{3,2,1,0:T(8,128)(2,1)} %refs_4_.3) | copy-start | bytes 4718596
  0.0 5.9 %copy-start = (bf16[6,2,256,256]{3,2,1,0:T(8,128)(2,1)S(1)}, bf16[6,2,256,256]{3,2,1,0:T(8,128)(2,1)}, u32[]{:S(2)}) copy-start(bf16[6,2,256,256]{3,2,1,0:T(8,128)(2,1)} %cross.47) | copy-start | bytes 4718596
  0.0 7.8 %slice-start = ((s8[8388608]{0:T(1024)(128)(4,1)}), s8[4194304]{0:T(1024)(128)(4,1)S(1)}, s32[]{:S(2)}) async-start(s8[8388608]{0:T(1024)(128)(4,1)} %bitcast), calls=%async_computation | async-start | bytes 8388608
  0.0 7.8 %slice-start.1 = ((s8[8388608]{0:T(1024)(128)(4,1)}), s8[4194304]{0:T(1024)(128)(4,1)S(1)}, s32[]{:S(2)}) async-start(s8[8388608]{0:T(1024)(128)(4,1)} %bitcast), calls=%async_computation.1 | async-start | bytes 8388608
  2.7 5.2 %copy-start.3 = (bf16[2,512,256]{2,1,0:T(8,128)(2,1)S(1)}, bf16[2,512,256]{2,1,0:T(8,128)(2,1)}, u32[]{:S(2)}) copy-start(bf16[2,512,256]{2,1,0:T(8,128)(2,1)} %leaf.23) | copy-start | bytes 1572868
  2.7 3.2 %collective-permute-start = (bf16[240,512]{1,0:T(8,128)(2,1)S(1)}, bf16[240,512]{1,0:T(8,128)(2,1)S(1)}, u32[]{:S(2)}, u32[]{:S(2)}) collective-permute-start(bf16[240,512]{1,0:T(8,128)(2,1)S(1)} %get-tuple-element.128), channel_id=1, source_target_pairs={{0,1},{1,0},{2,3},{3,2},{4,5},{5,4},{6,7},{7,6},{8,9},{9,8},{10,11... | collective-permute-start | bytes 737288 | tf_op jit(solution)/shard_map/ppermute | solution.py:266
  3.2 33.0 %collective-permute-start.9 = (bf16[4,2,256,256]{3,2,1,0:T(8,128)(2,1)S(1)}, bf16[4,2,256,256]{3,2,1,0:T(8,128)(2,1)S(1)}, u32[]{:S(2)}, u32[]{:S(2)}) collective-permute-start(bf16[4,2,256,256]{3,2,1,0:T(8,128)(2,1)S(1)} %get-tuple-element.154), channel_id=1, source_target_pairs={{0,8},{1,9},{2,10},{3,11},{4,12},{5,13},{6,14},{7,15},{8,0},{9,1},... | collective-permute-start | bytes 3145736 | tf_op jit(solution)/shard_map/ppermute | solution.py:266
  6.3 8.1 %collective-permute-start.2 = (bf16[240,512]{1,0:T(8,128)(2,1)S(1)}, bf16[240,512]{1,0:T(8,128)(2,1)S(1)}, u32[]{:S(2)}, u32[]{:S(2)}) collective-permute-start(bf16[240,512]{1,0:T(8,128)(2,1)S(1)} %get-tuple-element.134), channel_id=1, source_target_pairs={{0,2},{1,3},{2,0},{3,1},{4,6},{5,7},{6,4},{7,5},{8,10},{9,11},{10,... | collective-permute-start | bytes 737288 | tf_op jit(solution)/shard_map/ppermute | solution.py:266
  8.8 7.5 %collective-permute-start.1 = (bf16[336,512]{1,0:T(8,128)(2,1)S(1)}, bf16[336,512]{1,0:T(8,128)(2,1)S(1)}, u32[]{:S(2)}, u32[]{:S(2)}) collective-permute-start(bf16[336,512]{1,0:T(8,128)(2,1)S(1)} %get-tuple-element.132), channel_id=1, source_target_pairs={{0,1},{1,0},{2,3},{3,2},{4,5},{5,4},{6,7},{7,6},{8,9},{9,8},{10,11... | collective-permute-start | bytes 1032200 | tf_op jit(solution)/shard_map/ppermute | solution.py:266
  9.1 10.4 %collective-permute-start.5 = (bf16[2048,128]{1,0:T(8,128)(2,1)S(1)}, bf16[2048,128]{1,0:T(8,128)(2,1)S(1)}, u32[]{:S(2)}, u32[]{:S(2)}) collective-permute-start(bf16[2048,128]{1,0:T(8,128)(2,1)S(1)} %get-tuple-element.142), channel_id=1, source_target_pairs={{0,1},{1,0},{2,3},{3,2},{4,5},{5,4},{6,7},{7,6},{8,9},{9,8},{10,11... | collective-permute-start | bytes 1572872 | tf_op jit(solution)/shard_map/ppermute | solution.py:266
  14.8 7.3 %collective-permute-start.4 = (bf16[240,512]{1,0:T(8,128)(2,1)S(1)}, bf16[240,512]{1,0:T(8,128)(2,1)S(1)}, u32[]{:S(2)}, u32[]{:S(2)}) collective-permute-start(bf16[240,512]{1,0:T(8,128)(2,1)S(1)} %get-tuple-element.141), channel_id=1, source_target_pairs={{0,4},{1,5},{2,6},{3,7},{4,0},{5,1},{6,2},{7,3},{8,12},{9,13},{10,... | collective-permute-start | bytes 737288 | tf_op jit(solution)/shard_map/ppermute | solution.py:266
  16.8 9.1 %collective-permute-start.3 = (bf16[336,512]{1,0:T(8,128)(2,1)S(1)}, bf16[336,512]{1,0:T(8,128)(2,1)S(1)}, u32[]{:S(2)}, u32[]{:S(2)}) collective-permute-start(bf16[336,512]{1,0:T(8,128)(2,1)S(1)} %get-tuple-element.139), channel_id=1, source_target_pairs={{0,2},{1,3},{2,0},{3,1},{4,6},{5,7},{6,4},{7,5},{8,10},{9,11},{10,... | collective-permute-start | bytes 1032200 | tf_op jit(solution)/shard_map/ppermute | solution.py:266
  19.4 7.5 %collective-permute-start.7 = (bf16[400,512]{1,0:T(8,128)(2,1)S(1)}, bf16[400,512]{1,0:T(8,128)(2,1)S(1)}, u32[]{:S(2)}, u32[]{:S(2)}) collective-permute-start(bf16[400,512]{1,0:T(8,128)(2,1)S(1)} %get-tuple-element.149), channel_id=1, source_target_pairs={{0,1},{1,0},{2,3},{3,2},{4,5},{5,4},{6,7},{7,6},{8,9},{9,8},{10,11... | collective-permute-start | bytes 1228808 | tf_op jit(solution)/shard_map/ppermute | solution.py:266
  22.3 13.9 %collective-permute-start.10 = (bf16[240,512]{1,0:T(8,128)(2,1)S(1)}, bf16[240,512]{1,0:T(8,128)(2,1)S(1)}, u32[]{:S(2)}, u32[]{:S(2)}) collective-permute-start(bf16[240,512]{1,0:T(8,128)(2,1)S(1)} %get-tuple-element.155.own), channel_id=1, source_target_pairs={{0,8},{1,9},{2,10},{3,11},{4,12},{5,13},{6,14},{7,15},{8,0},{9,1},... | collective-permute-start | bytes 737288 | tf_op jit(solution)/shard_map/ppermute | solution.py:266
  26.3 8.2 %collective-permute-start.6 = (bf16[336,512]{1,0:T(8,128)(2,1)S(1)}, bf16[336,512]{1,0:T(8,128)(2,1)S(1)}, u32[]{:S(2)}, u32[]{:S(2)}) collective-permute-start(bf16[336,512]{1,0:T(8,128)(2,1)S(1)} %get-tuple-element.147), channel_id=1, source_target_pairs={{0,4},{1,5},{2,6},{3,7},{4,0},{5,1},{6,2},{7,3},{8,12},{9,13},{10,... | collective-permute-start | bytes 1032200 | tf_op jit(solution)/shard_map/ppermute | solution.py:266
  27.4 11.7 %collective-permute-start.13 = (bf16[400,512]{1,0:T(8,128)(2,1)S(1)}, bf16[400,512]{1,0:T(8,128)(2,1)S(1)}, u32[]{:S(2)}, u32[]{:S(2)}) collective-permute-start(bf16[400,512]{1,0:T(8,128)(2,1)S(1)} %get-tuple-element.162), channel_id=1, source_target_pairs={{0,2},{1,3},{2,0},{3,1},{4,6},{5,7},{6,4},{7,5},{8,10},{9,11},{10,... | collective-permute-start | bytes 1228808 | tf_op jit(solution)/shard_map/ppermute | solution.py:266
  29.1 11.4 %collective-permute-start.12 = (bf16[2048,128]{1,0:T(8,128)(2,1)S(1)}, bf16[2048,128]{1,0:T(8,128)(2,1)S(1)}, u32[]{:S(2)}, u32[]{:S(2)}) collective-permute-start(bf16[2048,128]{1,0:T(8,128)(2,1)S(1)} %get-tuple-element.160), channel_id=1, source_target_pairs={{15,16},{16,15}} | collective-permute-start | bytes 1572872 | tf_op jit(solution)/shard_map/ppermute | solution.py:266
  34.8 7.8 %collective-permute-start.8 = (bf16[336,512]{1,0:T(8,128)(2,1)S(1)}, bf16[336,512]{1,0:T(8,128)(2,1)S(1)}, u32[]{:S(2)}, u32[]{:S(2)}) collective-permute-start(bf16[336,512]{1,0:T(8,128)(2,1)S(1)} %get-tuple-element.153.own), channel_id=1, source_target_pairs={{0,8},{1,9},{2,10},{3,11},{4,12},{5,13},{6,14},{7,15},{8,0},{9,1},... | collective-permute-start | bytes 1032200 | tf_op jit(solution)/shard_map/ppermute | solution.py:266
  37.3 8.3 %collective-permute-start.17 = (bf16[240,1024]{1,0:T(8,128)(2,1)S(1)}, bf16[240,1024]{1,0:T(8,128)(2,1)S(1)}, u32[]{:S(2)}, u32[]{:S(2)}) collective-permute-start(bf16[240,1024]{1,0:T(8,128)(2,1)S(1)} %get-tuple-element.175), channel_id=1, source_target_pairs={{0,1},{1,0},{2,3},{3,2},{4,5},{5,4},{6,7},{7,6},{8,16},{9,17},{10,... | collective-permute-start | bytes 1474568 | tf_op jit(solution)/shard_map/ppermute | solution.py:266
  38.5 2.0 %collective-permute-start.11 = (bf16[448,512]{1,0:T(8,128)(2,1)S(1)}, bf16[448,512]{1,0:T(8,128)(2,1)S(1)}, u32[]{:S(2)}, u32[]{:S(2)}) collective-permute-start(bf16[448,512]{1,0:T(8,128)(2,1)S(1)} %get-tuple-element.159), channel_id=1, source_target_pairs={{0,1},{1,0},{2,3},{3,2},{4,5},{5,4},{6,7},{7,6},{8,9},{9,8},{10,11... | collective-permute-start | bytes 1376264 | tf_op jit(solution)/shard_map/ppermute | solution.py:266
  39.6 11.5 %collective-permute-start.16 = (bf16[400,512]{1,0:T(8,128)(2,1)S(1)}, bf16[400,512]{1,0:T(8,128)(2,1)S(1)}, u32[]{:S(2)}, u32[]{:S(2)}) collective-permute-start(bf16[400,512]{1,0:T(8,128)(2,1)S(1)} %get-tuple-element.172), channel_id=1, source_target_pairs={{0,4},{1,5},{2,6},{3,7},{4,0},{5,1},{6,2},{7,3},{8,12},{9,13},{10,... | collective-permute-start | bytes 1228808 | tf_op jit(solution)/shard_map/ppermute | solution.py:266
  41.0 13.6 %collective-permute-start.15 = (bf16[448,512]{1,0:T(8,128)(2,1)S(1)}, bf16[448,512]{1,0:T(8,128)(2,1)S(1)}, u32[]{:S(2)}, u32[]{:S(2)}) collective-permute-start(bf16[448,512]{1,0:T(8,128)(2,1)S(1)} %get-tuple-element.170), channel_id=1, source_target_pairs={{0,2},{1,3},{2,0},{3,1},{4,6},{5,7},{6,4},{7,5},{8,10},{9,11},{10,... | collective-permute-start | bytes 1376264 | tf_op jit(solution)/shard_map/ppermute | solution.py:266
  44.0 20.5 %collective-permute-start.21 = (bf16[336,1024]{1,0:T(8,128)(2,1)S(1)}, bf16[336,1024]{1,0:T(8,128)(2,1)S(1)}, u32[]{:S(2)}, u32[]{:S(2)}) collective-permute-start(bf16[336,1024]{1,0:T(8,128)(2,1)S(1)} %get-tuple-element.188), channel_id=1, source_target_pairs={{0,1},{1,0},{2,3},{3,2},{4,5},{5,4},{6,7},{7,6},{8,16},{9,17},{10,... | collective-permute-start | bytes 2064392 | tf_op jit(solution)/shard_map/ppermute | solution.py:266
  45.1 10.9 %collective-permute-start.14 = (bf16[400,512]{1,0:T(8,128)(2,1)S(1)}, bf16[400,512]{1,0:T(8,128)(2,1)S(1)}, u32[]{:S(2)}, u32[]{:S(2)}) collective-permute-start(bf16[400,512]{1,0:T(8,128)(2,1)S(1)} %get-tuple-element.168), channel_id=1, source_target_pairs={{0,1},{1,0},{2,3},{3,2},{4,5},{5,4},{6,7},{7,6},{8,9},{9,8},{10,11... | collective-permute-start | bytes 1228808 | tf_op jit(solution)/shard_map/ppermute | solution.py:266
  51.5 11.5 %collective-permute-start.22 = (bf16[400,512]{1,0:T(8,128)(2,1)S(1)}, bf16[400,512]{1,0:T(8,128)(2,1)S(1)}, u32[]{:S(2)}, u32[]{:S(2)}) collective-permute-start(bf16[400,512]{1,0:T(8,128)(2,1)S(1)} %get-tuple-element.190), channel_id=1, source_target_pairs={{0,8},{1,9},{2,10},{3,11},{4,12},{5,13},{6,14},{7,15},{8,0},{9,1},... | collective-permute-start | bytes 1228808 | tf_op jit(solution)/shard_map/ppermute | solution.py:266
  55.1 11.3 %collective-permute-start.20 = (bf16[448,512]{1,0:T(8,128)(2,1)S(1)}, bf16[448,512]{1,0:T(8,128)(2,1)S(1)}, u32[]{:S(2)}, u32[]{:S(2)}) collective-permute-start(bf16[448,512]{1,0:T(8,128)(2,1)S(1)} %get-tuple-element.185), channel_id=1, source_target_pairs={{0,4},{1,5},{2,6},{3,7},{4,0},{5,1},{6,2},{7,3},{8,12},{9,13},{10,... | collective-permute-start | bytes 1376264 | tf_op jit(solution)/shard_map/ppermute | solution.py:266
  56.6 10.5 %collective-permute-start.19 = (bf16[400,512]{1,0:T(8,128)(2,1)S(1)}, bf16[400,512]{1,0:T(8,128)(2,1)S(1)}, u32[]{:S(2)}, u32[]{:S(2)}) collective-permute-start(bf16[400,512]{1,0:T(8,128)(2,1)S(1)} %get-tuple-element.183), channel_id=1, source_target_pairs={{0,2},{1,3},{2,0},{3,1},{4,6},{5,7},{6,4},{7,5},{8,10},{9,11},{10,... | collective-permute-start | bytes 1228808 | tf_op jit(solution)/shard_map/ppermute | solution.py:266
  59.0 11.6 %collective-permute-start.18 = (bf16[224,512]{1,0:T(8,128)(2,1)S(1)}, bf16[224,512]{1,0:T(8,128)(2,1)S(1)}, u32[]{:S(2)}, u32[]{:S(2)}) collective-permute-start(bf16[224,512]{1,0:T(8,128)(2,1)S(1)} %get-tuple-element.181), channel_id=1, source_target_pairs={{0,1},{1,0},{2,3},{3,2},{4,5},{5,4},{6,7},{7,6},{8,9},{9,8},{10,11... | collective-permute-start | bytes 688136 | tf_op jit(solution)/shard_map/ppermute | solution.py:266
  64.4 17.3 %collective-permute-start.27 = (bf16[400,1024]{1,0:T(8,128)(2,1)S(1)}, bf16[400,1024]{1,0:T(8,128)(2,1)S(1)}, u32[]{:S(2)}, u32[]{:S(2)}) collective-permute-start(bf16[400,1024]{1,0:T(8,128)(2,1)S(1)} %get-tuple-element.206), channel_id=1, source_target_pairs={{0,1},{1,0},{2,3},{3,2},{4,5},{5,4},{6,7},{7,6},{8,16},{9,17},{10,... | collective-permute-start | bytes 2457608 | tf_op jit(solution)/shard_map/ppermute | solution.py:266
  67.6 14.1 %collective-permute-start.26 = (bf16[400,512]{1,0:T(8,128)(2,1)S(1)}, bf16[400,512]{1,0:T(8,128)(2,1)S(1)}, u32[]{:S(2)}, u32[]{:S(2)}) collective-permute-start(bf16[400,512]{1,0:T(8,128)(2,1)S(1)} %get-tuple-element.203), channel_id=1, source_target_pairs={{0,4},{1,5},{2,6},{3,7},{4,0},{5,1},{6,2},{7,3},{8,12},{9,13},{10,... | collective-permute-start | bytes 1228808 | tf_op jit(solution)/shard_map/ppermute | solution.py:266
  68.9 11.1 %collective-permute-start.24 = (bf16[448,512]{1,0:T(8,128)(2,1)S(1)}, bf16[448,512]{1,0:T(8,128)(2,1)S(1)}, u32[]{:S(2)}, u32[]{:S(2)}) collective-permute-start(bf16[448,512]{1,0:T(8,128)(2,1)S(1)} %get-tuple-element.198), channel_id=1, source_target_pairs={{0,8},{1,9},{2,10},{3,11},{4,12},{5,13},{6,14},{7,15},{8,0},{9,1},... | collective-permute-start | bytes 1376264 | tf_op jit(solution)/shard_map/ppermute | solution.py:266
  71.1 15.5 %collective-permute-start.25 = (bf16[2048,128]{1,0:T(8,128)(2,1)S(1)}, bf16[2048,128]{1,0:T(8,128)(2,1)S(1)}, u32[]{:S(2)}, u32[]{:S(2)}) collective-permute-start(bf16[2048,128]{1,0:T(8,128)(2,1)S(1)} %get-tuple-element.200), channel_id=1, source_target_pairs={{1,2},{2,1},{3,4},{4,3},{5,6},{6,5},{7,8},{8,7},{9,10},{10,9},{11,... | collective-permute-start | bytes 1572872 | tf_op jit(solution)/shard_map/ppermute | solution.py:266
  72.0 18.3 %collective-permute-start.23 = (bf16[224,512]{1,0:T(8,128)(2,1)S(1)}, bf16[224,512]{1,0:T(8,128)(2,1)S(1)}, u32[]{:S(2)}, u32[]{:S(2)}) collective-permute-start(bf16[224,512]{1,0:T(8,128)(2,1)S(1)} %get-tuple-element.196), channel_id=1, source_target_pairs={{0,2},{1,3},{2,0},{3,1},{4,6},{5,7},{6,4},{7,5},{8,10},{9,11},{10,... | collective-permute-start | bytes 688136 | tf_op jit(solution)/shard_map/ppermute | solution.py:266
  81.6 18.1 %collective-permute-start.29 = (bf16[448,1024]{1,0:T(8,128)(2,1)S(1)}, bf16[448,1024]{1,0:T(8,128)(2,1)S(1)}, u32[]{:S(2)}, u32[]{:S(2)}) collective-permute-start(bf16[448,1024]{1,0:T(8,128)(2,1)S(1)} %get-tuple-element.218), channel_id=1, source_target_pairs={{0,1},{1,0},{2,3},{3,2},{4,5},{5,4},{6,7},{7,6},{8,16},{9,17},{10,... | collective-permute-start | bytes 2752520 | tf_op jit(solution)/shard_map/ppermute | solution.py:266
  81.7 4.9 %copy-start.2 = (bf16[2,768,512]{2,1,0:T(8,128)(2,1)S(1)}, bf16[2,768,512]{2,1,0:T(8,128)(2,1)}, u32[]{:S(2)}) copy-start(bf16[2,768,512]{2,1,0:T(8,128)(2,1)} %near.11) | copy-start | bytes 4718596
  81.7 4.9 %copy-start.4 = (bf16[2,256,512]{2,1,0:T(8,128)(2,1)S(1)}, bf16[2,256,512]{2,1,0:T(8,128)(2,1)}, u32[]{:S(2)}) copy-start(bf16[2,256,512]{2,1,0:T(8,128)(2,1)} %out_basis.11) | copy-start | bytes 1572868
  82.2 12.2 %collective-permute-start.30 = (bf16[400,512]{1,0:T(8,128)(2,1)S(1)}, bf16[400,512]{1,0:T(8,128)(2,1)S(1)}, u32[]{:S(2)}, u32[]{:S(2)}) collective-permute-start(bf16[400,512]{1,0:T(8,128)(2,1)S(1)} %get-tuple-element.220), channel_id=1, source_target_pairs={{0,8},{1,9},{2,10},{3,11},{4,12},{5,13},{6,14},{7,15},{8,0},{9,1},... | collective-permute-start | bytes 1228808 | tf_op jit(solution)/shard_map/ppermute | solution.py:266
  90.7 9.0 %collective-permute-start.28 = (bf16[224,512]{1,0:T(8,128)(2,1)S(1)}, bf16[224,512]{1,0:T(8,128)(2,1)S(1)}, u32[]{:S(2)}, u32[]{:S(2)}) collective-permute-start(bf16[224,512]{1,0:T(8,128)(2,1)S(1)} %get-tuple-element.215), channel_id=1, source_target_pairs={{0,4},{1,5},{2,6},{3,7},{4,0},{5,1},{6,2},{7,3},{8,12},{9,13},{10,... | collective-permute-start | bytes 688136 | tf_op jit(solution)/shard_map/ppermute | solution.py:266
  96.0 18.6 %collective-permute-start.33 = (bf16[400,1024]{1,0:T(8,128)(2,1)S(1)}, bf16[400,1024]{1,0:T(8,128)(2,1)S(1)}, u32[]{:S(2)}, u32[]{:S(2)}) collective-permute-start(bf16[400,1024]{1,0:T(8,128)(2,1)S(1)} %get-tuple-element.235), channel_id=1, source_target_pairs={{0,1},{1,0},{2,3},{3,2},{4,5},{5,4},{6,7},{7,6},{8,16},{9,17},{10,... | collective-permute-start | bytes 2457608 | tf_op jit(solution)/shard_map/ppermute | solution.py:266
  100.2 13.2 %collective-permute-start.31 = (bf16[448,512]{1,0:T(8,128)(2,1)S(1)}, bf16[448,512]{1,0:T(8,128)(2,1)S(1)}, u32[]{:S(2)}, u32[]{:S(2)}) collective-permute-start(bf16[448,512]{1,0:T(8,128)(2,1)S(1)} %get-tuple-element.224), channel_id=1, source_target_pairs={{0,8},{1,9},{2,10},{3,11},{4,12},{5,13},{6,14},{7,15},{8,0},{9,1},... | collective-permute-start | bytes 1376264 | tf_op jit(solution)/shard_map/ppermute | solution.py:266
  114.5 11.3 %collective-permute-start.32 = (bf16[224,1024]{1,0:T(8,128)(2,1)S(1)}, bf16[224,1024]{1,0:T(8,128)(2,1)S(1)}, u32[]{:S(2)}, u32[]{:S(2)}) collective-permute-start(bf16[224,1024]{1,0:T(8,128)(2,1)S(1)} %get-tuple-element.231), channel_id=1, source_target_pairs={{0,1},{1,0},{2,3},{3,2},{4,5},{5,4},{6,7},{7,6},{8,16},{9,17},{10,... | collective-permute-start | bytes 1376264 | tf_op jit(solution)/shard_map/ppermute | solution.py:266
  115.0 16.6 %collective-permute-start.35 = (bf16[400,512]{1,0:T(8,128)(2,1)S(1)}, bf16[400,512]{1,0:T(8,128)(2,1)S(1)}, u32[]{:S(2)}, u32[]{:S(2)}) collective-permute-start(bf16[400,512]{1,0:T(8,128)(2,1)S(1)} %get-tuple-element.243), channel_id=1, source_target_pairs={{0,8},{1,9},{2,10},{3,11},{4,12},{5,13},{6,14},{7,15},{8,0},{9,1},... | collective-permute-start | bytes 1228808 | tf_op jit(solution)/shard_map/ppermute | solution.py:266
  126.1 9.6 %collective-permute-start.34 = (bf16[224,512]{1,0:T(8,128)(2,1)S(1)}, bf16[224,512]{1,0:T(8,128)(2,1)S(1)}, u32[]{:S(2)}, u32[]{:S(2)}) collective-permute-start(bf16[224,512]{1,0:T(8,128)(2,1)S(1)} %get-tuple-element.241), channel_id=1, source_target_pairs={{0,8},{1,9},{2,10},{3,11},{4,12},{5,13},{6,14},{7,15},{8,0},{9,1},... | collective-permute-start | bytes 688136 | tf_op jit(solution)/shard_map/ppermute | solution.py:266

commit v5 on v4

--- a/solution.py
+++ b/solution.py
@@ -9,7 +9,7 @@
 
 BF16 = jnp.bfloat16
 F32 = jnp.float32
-SHARES = (15, 21, 25, 28, 25, 14)
+SHARES = (15, 21, 26, 29, 25, 12)
 
 
 def dot(a, b):

time: 138 us -> 139 us (level)
  transfers between devices with their start and end apart: 36 -> 36, of which waited for: 14 -> 13; matrix products, arithmetic and copies ran while one was open for 0% -> 0% of each run, Pallas kernels for 23% -> 23%
where the time goes in v5:
time: 139 us; the launch traced here: 138 us
  starting transfers between devices  58.3 us (42%)
  waiting for transfers between devices  42.6 us (31%)
  Pallas kernels  36.3 us (26%)
    ppermute x36, starting transfers between devices, per_device(): send = lambda operand, pairs: lax.ppermute(operand, 'box', pairs)  58.3 us
    ppermute x36, waiting for transfers between devices, per_device(): send = lambda operand, pairs: lax.ppermute(operand, 'box', pairs)  42.6 us
    pallas_call x44, Pallas kernels, call(): pl.pallas_call(body, in_specs=in_specs, out_specs=out_specs, out_shape=ou...  36.3 us
  transfers between devices with their start and end apart: 36, of which 13 were waited for; matrix products, arithmetic and copies ran while one was open for 0% of the time, Pallas kernels for 23%

profile of v5, /device:TPU:0, one launch (start us, length us, event | category | flops | bytes accessed | tf_op | source)
XLA Modules:
  0.0 137.9 jit_solution(13328049905595039736)
XLA Ops:
  0.0 2.6 %leaf.12 = (bf16[240,512]{1,0:T(8,128)(2,1)S(1)}, bf16[240,512]{1,0:T(8,128)(2,1)S(1)}, bf16[4,2,256,256]{3,2,1,0:T(8,128)(2,1)S(1)}, f32[8,128]{1,0:T(8,128)S(1)}) custom-call(f32[2048,1024]{1,0:T(8,128)} %src.29, bf16[2,512,256]{2,1,0:T(8,128)(2,1)} %leaf.23, bf16[6,2,256,256]{3,2,1,0:T(8,128)(2,1)} %refs_4_.3, bf16[6,2,256,256]{3,2,1,0:T(8,128)(2,1)} %cross.47, ...), custom_call_target="tpu_custom_call" | custom-call | flops 3000000000 | bytes 1 | tf_op jit(solution)/shard_map/leaf/pallas_call | solution.py:235
  3.2 2.7 %collective-permute-start.9 = (bf16[4,2,256,256]{3,2,1,0:T(8,128)(2,1)S(1)}, bf16[4,2,256,256]{3,2,1,0:T(8,128)(2,1)S(1)}, u32[]{:S(2)}, u32[]{:S(2)}) collective-permute-start(bf16[4,2,256,256]{3,2,1,0:T(8,128)(2,1)S(1)} %get-tuple-element.154), channel_id=1, source_target_pairs={{0,8},{1,9},{2,10},{3,11},{4,12},{5,13},{6,14},{7,15},{8,0},{9,1},... | collective-permute-start | bytes 3145736 | tf_op jit(solution)/shard_map/ppermute | solution.py:266
  6.3 1.6 %collective-permute-start.2 = (bf16[240,512]{1,0:T(8,128)(2,1)S(1)}, bf16[240,512]{1,0:T(8,128)(2,1)S(1)}, u32[]{:S(2)}, u32[]{:S(2)}) collective-permute-start(bf16[240,512]{1,0:T(8,128)(2,1)S(1)} %get-tuple-element.134), channel_id=1, source_target_pairs={{0,2},{1,3},{2,0},{3,1},{4,6},{5,7},{6,4},{7,5},{8,10},{9,11},{10,... | collective-permute-start | bytes 737288 | tf_op jit(solution)/shard_map/ppermute | solution.py:266
  7.8 1.0 leaf.14
  9.6 4.7 %collective-permute-done.2.moved = bf16[240,512]{1,0:T(8,128)(2,1)S(1)} collective-permute-done((bf16[240,512]{1,0:T(8,128)(2,1)S(1)}, bf16[240,512]{1,0:T(8,128)(2,1)S(1)}, u32[]{:S(2)}, u32[]{:S(2)}) %collective-permute-start.2) | collective-permute-done | bytes 245792 | tf_op jit(solution)/shard_map/ppermute | solution.py:266
  14.8 1.6 %collective-permute-start.4 = (bf16[240,512]{1,0:T(8,128)(2,1)S(1)}, bf16[240,512]{1,0:T(8,128)(2,1)S(1)}, u32[]{:S(2)}, u32[]{:S(2)}) collective-permute-start(bf16[240,512]{1,0:T(8,128)(2,1)S(1)} %get-tuple-element.141), channel_id=1, source_target_pairs={{0,4},{1,5},{2,6},{3,7},{4,0},{5,1},{6,2},{7,3},{8,12},{9,13},{10,... | collective-permute-start | bytes 737288 | tf_op jit(solution)/shard_map/ppermute | solution.py:266
  16.8 1.6 %collective-permute-start.3 = (bf16[336,512]{1,0:T(8,128)(2,1)S(1)}, bf16[336,512]{1,0:T(8,128)(2,1)S(1)}, u32[]{:S(2)}, u32[]{:S(2)}) collective-permute-start(bf16[336,512]{1,0:T(8,128)(2,1)S(1)} %get-tuple-element.139), channel_id=1, source_target_pairs={{0,2},{1,3},{2,0},{3,1},{4,6},{5,7},{6,4},{7,5},{8,10},{9,11},{10,... | collective-permute-start | bytes 1032200 | tf_op jit(solution)/shard_map/ppermute | solution.py:266
  18.4 1.1 leaf.16
  19.5 2.5 %collective-permute-done.4.moved = bf16[240,512]{1,0:T(8,128)(2,1)S(1)} collective-permute-done((bf16[240,512]{1,0:T(8,128)(2,1)S(1)}, bf16[240,512]{1,0:T(8,128)(2,1)S(1)}, u32[]{:S(2)}, u32[]{:S(2)}) %collective-permute-start.4) | collective-permute-done | bytes 245792 | tf_op jit(solution)/shard_map/ppermute | solution.py:266
  22.3 1.4 %collective-permute-start.10 = (bf16[240,512]{1,0:T(8,128)(2,1)S(1)}, bf16[240,512]{1,0:T(8,128)(2,1)S(1)}, u32[]{:S(2)}, u32[]{:S(2)}) collective-permute-start(bf16[240,512]{1,0:T(8,128)(2,1)S(1)} %get-tuple-element.155.own), channel_id=1, source_target_pairs={{0,8},{1,9},{2,10},{3,11},{4,12},{5,13},{6,14},{7,15},{8,0},{9,1},... | collective-permute-start | bytes 737288 | tf_op jit(solution)/shard_map/ppermute | solution.py:266
  23.7 2.2 %collective-permute-done.3.moved = bf16[336,512]{1,0:T(8,128)(2,1)S(1)} collective-permute-done((bf16[336,512]{1,0:T(8,128)(2,1)S(1)}, bf16[336,512]{1,0:T(8,128)(2,1)S(1)}, u32[]{:S(2)}, u32[]{:S(2)}) %collective-permute-start.3) | collective-permute-done | bytes 344096 | tf_op jit(solution)/shard_map/ppermute | solution.py:266
  27.4 1.6 %collective-permute-start.13 = (bf16[416,512]{1,0:T(8,128)(2,1)S(1)}, bf16[416,512]{1,0:T(8,128)(2,1)S(1)}, u32[]{:S(2)}, u32[]{:S(2)}) collective-permute-start(bf16[416,512]{1,0:T(8,128)(2,1)S(1)} %get-tuple-element.162), channel_id=1, source_target_pairs={{0,2},{1,3},{2,0},{3,1},{4,6},{5,7},{6,4},{7,5},{8,10},{9,11},{10,... | collective-permute-start | bytes 1277960 | tf_op jit(solution)/shard_map/ppermute | solution.py:266
  30.0 4.5 %collective-permute-done.6.moved = bf16[336,512]{1,0:T(8,128)(2,1)S(1)} collective-permute-done((bf16[336,512]{1,0:T(8,128)(2,1)S(1)}, bf16[336,512]{1,0:T(8,128)(2,1)S(1)}, u32[]{:S(2)}, u32[]{:S(2)}) %collective-permute-start.6) | collective-permute-done | bytes 344096 | tf_op jit(solution)/shard_map/ppermute | solution.py:266
  34.8 1.4 %collective-permute-start.8 = (bf16[336,512]{1,0:T(8,128)(2,1)S(1)}, bf16[336,512]{1,0:T(8,128)(2,1)S(1)}, u32[]{:S(2)}, u32[]{:S(2)}) collective-permute-start(bf16[336,512]{1,0:T(8,128)(2,1)S(1)} %get-tuple-element.153.own), channel_id=1, source_target_pairs={{0,8},{1,9},{2,10},{3,11},{4,12},{5,13},{6,14},{7,15},{8,0},{9,1},... | collective-permute-start | bytes 1032200 | tf_op jit(solution)/shard_map/ppermute | solution.py:266
  36.2 1.1 relay.6
  37.4 1.1 leaf.18
  39.6 0.9 collective-permute-start.16
  41.1 1.6 %collective-permute-start.15 = (bf16[464,512]{1,0:T(8,128)(2,1)S(1)}, bf16[464,512]{1,0:T(8,128)(2,1)S(1)}, u32[]{:S(2)}, u32[]{:S(2)}) collective-permute-start(bf16[464,512]{1,0:T(8,128)(2,1)S(1)} %get-tuple-element.170), channel_id=1, source_target_pairs={{0,2},{1,3},{2,0},{3,1},{4,6},{5,7},{6,4},{7,5},{8,10},{9,11},{10,... | collective-permute-start | bytes 1425416 | tf_op jit(solution)/shard_map/ppermute | solution.py:266
  42.7 1.3 relay.7
  44.2 1.0 leaf.20
  45.7 5.7 %collective-permute-done.16.refs_1_ = bf16[416,512]{1,0:T(8,128)(2,1)S(1)} collective-permute-done((bf16[416,512]{1,0:T(8,128)(2,1)S(1)}, bf16[416,512]{1,0:T(8,128)(2,1)S(1)}, u32[]{:S(2)}, u32[]{:S(2)}) %collective-permute-start.16) | collective-permute-done | bytes 426016 | tf_op jit(solution)/shard_map/ppermute | solution.py:266
  51.8 3.2 %collective-permute-start.22 = (bf16[416,512]{1,0:T(8,128)(2,1)S(1)}, bf16[416,512]{1,0:T(8,128)(2,1)S(1)}, u32[]{:S(2)}, u32[]{:S(2)}) collective-permute-start(bf16[416,512]{1,0:T(8,128)(2,1)S(1)} %get-tuple-element.190), channel_id=1, source_target_pairs={{0,8},{1,9},{2,10},{3,11},{4,12},{5,13},{6,14},{7,15},{8,0},{9,1},... | collective-permute-start | bytes 1277960 | tf_op jit(solution)/shard_map/ppermute | solution.py:266
  55.5 0.9 collective-permute-start.20
  57.0 1.6 %collective-permute-start.19 = (bf16[400,512]{1,0:T(8,128)(2,1)S(1)}, bf16[400,512]{1,0:T(8,128)(2,1)S(1)}, u32[]{:S(2)}, u32[]{:S(2)}) collective-permute-start(bf16[400,512]{1,0:T(8,128)(2,1)S(1)} %get-tuple-element.183), channel_id=1, source_target_pairs={{0,2},{1,3},{2,0},{3,1},{4,6},{5,7},{6,4},{7,5},{8,10},{9,11},{10,... | collective-permute-start | bytes 1228808 | tf_op jit(solution)/shard_map/ppermute | solution.py:266
  59.4 3.9 %collective-permute-done.22.other.back = bf16[416,512]{1,0:T(8,128)(2,1)S(1)} collective-permute-done((bf16[416,512]{1,0:T(8,128)(2,1)S(1)}, bf16[416,512]{1,0:T(8,128)(2,1)S(1)}, u32[]{:S(2)}, u32[]{:S(2)}) %collective-permute-start.22) | collective-permute-done | bytes 426016 | tf_op jit(solution)/shard_map/ppermute | solution.py:266
  63.3 1.5 %relay.8 = (bf16[416,512]{1,0:T(8,128)(2,1)S(1)}, bf16[416,512]{1,0:T(8,128)(2,1)S(1)}, bf16[416,1024]{1,0:T(8,128)(2,1)S(1)}, f32[8,128]{1,0:T(8,128)S(1)}) custom-call(bf16[416,512]{1,0:T(8,128)(2,1)S(1)} %get-tuple-element.189.own, bf16[416,512]{1,0:T(8,128)(2,1)S(1)} %collective-permute-done.22.other.back, bf16[6,2,256,256]{3,2,1,0:T(8,128)(2,1)S(1)} %copy-done.1, ...), custom_call_target="tpu_custom_call" | custom-call | flops 10000000 | bytes 1 | tf_op jit(solution)/shard_map/relay/pallas_call | solution.py:235
  64.9 2.3 %collective-permute-done.20.refs_1_ = bf16[464,512]{1,0:T(8,128)(2,1)S(1)} collective-permute-done((bf16[464,512]{1,0:T(8,128)(2,1)S(1)}, bf16[464,512]{1,0:T(8,128)(2,1)S(1)}, u32[]{:S(2)}, u32[]{:S(2)}) %collective-permute-start.20) | collective-permute-done | bytes 475168 | tf_op jit(solution)/shard_map/ppermute | solution.py:266
  68.2 1.1 collective-permute-start.26
  69.3 1.3 collective-permute-start.24
  72.1 2.3 %collective-permute-start.23 = (bf16[192,512]{1,0:T(8,128)(2,1)S(1)}, bf16[192,512]{1,0:T(8,128)(2,1)S(1)}, u32[]{:S(2)}, u32[]{:S(2)}) collective-permute-start(bf16[192,512]{1,0:T(8,128)(2,1)S(1)} %get-tuple-element.196), channel_id=1, source_target_pairs={{0,2},{1,3},{2,0},{3,1},{4,6},{5,7},{6,4},{7,5},{8,10},{9,11},{10,... | collective-permute-start | bytes 589832 | tf_op jit(solution)/shard_map/ppermute | solution.py:266
  74.3 6.5 %collective-permute-done.24.other.back = bf16[464,512]{1,0:T(8,128)(2,1)S(1)} collective-permute-done((bf16[464,512]{1,0:T(8,128)(2,1)S(1)}, bf16[464,512]{1,0:T(8,128)(2,1)S(1)}, u32[]{:S(2)}, u32[]{:S(2)}) %collective-permute-start.24) | collective-permute-done | bytes 475168 | tf_op jit(solution)/shard_map/ppermute | solution.py:266
  80.8 1.6 %relay.9 = (bf16[464,512]{1,0:T(8,128)(2,1)S(1)}, bf16[464,512]{1,0:T(8,128)(2,1)S(1)}, bf16[464,1024]{1,0:T(8,128)(2,1)S(1)}, f32[8,128]{1,0:T(8,128)S(1)}) custom-call(bf16[464,512]{1,0:T(8,128)(2,1)S(1)} %get-tuple-element.207.own, bf16[464,512]{1,0:T(8,128)(2,1)S(1)} %collective-permute-done.24.other.back, bf16[6,2,256,256]{3,2,1,0:T(8,128)(2,1)S(1)} %copy-done.1, ...), custom_call_target="tpu_custom_call" | custom-call | flops 10000000 | bytes 1 | tf_op jit(solution)/shard_map/relay/pallas_call | solution.py:235
  83.1 3.8 %collective-permute-start.30 = (bf16[416,512]{1,0:T(8,128)(2,1)S(1)}, bf16[416,512]{1,0:T(8,128)(2,1)S(1)}, u32[]{:S(2)}, u32[]{:S(2)}) collective-permute-start(bf16[416,512]{1,0:T(8,128)(2,1)S(1)} %get-tuple-element.220), channel_id=1, source_target_pairs={{0,8},{1,9},{2,10},{3,11},{4,12},{5,13},{6,14},{7,15},{8,0},{9,1},... | collective-permute-start | bytes 1277960 | tf_op jit(solution)/shard_map/ppermute | solution.py:266
  86.9 1.6 %last.6 = (f32[2048,1024]{1,0:T(8,128)}, f32[8,128]{1,0:T(8,128)S(1)}) custom-call(bf16[240,512]{1,0:T(8,128)(2,1)S(1)} %get-tuple-element.201.own, bf16[416,512]{1,0:T(8,128)(2,1)S(1)} %collective-permute-done.22.other.back, bf16[2,256,512]{2,1,0:T(8,128)(2,1)S(1)} %copy-done.4, bf16[2,768,512]{2,1,0:T(8,128)(2,1)S(1)} %copy-done.2, ...), custom_call_target="tpu_custom_call" | custom-call | flops 10000000 | bytes 1 | tf_op jit(solution)/shard_map/last/pallas_call | solution.py:235
  88.4 1.9 %last.7 = (f32[2048,1024]{1,0:T(8,128)}, f32[8,128]{1,0:T(8,128)S(1)}) custom-call(bf16[336,512]{1,0:T(8,128)(2,1)S(1)} %get-tuple-element.197.own, bf16[464,512]{1,0:T(8,128)(2,1)S(1)} %collective-permute-done.24.other.back, bf16[2,256,512]{2,1,0:T(8,128)(2,1)S(1)} %copy-done.4, ...), custom_call_target="tpu_custom_call", output_to_operand_aliasing={{0}: (9, {})} | custom-call | flops 10000000 | bytes 1 | tf_op jit(solution)/shard_map/last/pallas_call | solution.py:235
  90.7 4.2 %collective-permute-start.28 = (bf16[192,512]{1,0:T(8,128)(2,1)S(1)}, bf16[192,512]{1,0:T(8,128)(2,1)S(1)}, u32[]{:S(2)}, u32[]{:S(2)}) collective-permute-start(bf16[192,512]{1,0:T(8,128)(2,1)S(1)} %get-tuple-element.215), channel_id=1, source_target_pairs={{0,4},{1,5},{2,6},{3,7},{4,0},{5,1},{6,2},{7,3},{8,12},{9,13},{10,... | collective-permute-start | bytes 589832 | tf_op jit(solution)/shard_map/ppermute | solution.py:266
  95.6 1.5 %relay.10 = (bf16[400,512]{1,0:T(8,128)(2,1)S(1)}, bf16[400,512]{1,0:T(8,128)(2,1)S(1)}, bf16[400,1024]{1,0:T(8,128)(2,1)S(1)}, f32[8,128]{1,0:T(8,128)S(1)}) custom-call(bf16[400,512]{1,0:T(8,128)(2,1)S(1)} %get-tuple-element.219.own, bf16[416,512]{1,0:T(8,128)(2,1)S(1)} %collective-permute-done.30.other.back, bf16[6,2,256,256]{3,2,1,0:T(8,128)(2,1)S(1)} %copy-done.1, ...), custom_call_target="tpu_custom_call" | custom-call | flops 10000000 | bytes 1 | tf_op jit(solution)/shard_map/relay/pallas_call | solution.py:235
  97.1 1.5 %collective-permute-done.28.refs_1_ = bf16[192,512]{1,0:T(8,128)(2,1)S(1)} collective-permute-done((bf16[192,512]{1,0:T(8,128)(2,1)S(1)}, bf16[192,512]{1,0:T(8,128)(2,1)S(1)}, u32[]{:S(2)}, u32[]{:S(2)}) %collective-permute-start.28) | collective-permute-done | bytes 196640 | tf_op jit(solution)/shard_map/ppermute | solution.py:266
  99.2 8.3 %collective-permute-start.31 = (bf16[464,512]{1,0:T(8,128)(2,1)S(1)}, bf16[464,512]{1,0:T(8,128)(2,1)S(1)}, u32[]{:S(2)}, u32[]{:S(2)}) collective-permute-start(bf16[464,512]{1,0:T(8,128)(2,1)S(1)} %get-tuple-element.224), channel_id=1, source_target_pairs={{0,8},{1,9},{2,10},{3,11},{4,12},{5,13},{6,14},{7,15},{8,0},{9,1},... | collective-permute-start | bytes 1425416 | tf_op jit(solution)/shard_map/ppermute | solution.py:266
  107.5 2.1 %last.8 = (f32[2048,1024]{1,0:T(8,128)}, f32[8,128]{1,0:T(8,128)S(1)}) custom-call(bf16[416,512]{1,0:T(8,128)(2,1)S(1)} %get-tuple-element.225.own, bf16[416,512]{1,0:T(8,128)(2,1)S(1)} %collective-permute-done.30.other.back, bf16[2,256,512]{2,1,0:T(8,128)(2,1)S(1)} %copy-done.4, ...), custom_call_target="tpu_custom_call", output_to_operand_aliasing={{0}: (9, {})} | custom-call | flops 10000000 | bytes 1 | tf_op jit(solution)/shard_map/last/pallas_call | solution.py:235
  109.5 5.8 %collective-permute-done.31.other.back = bf16[464,512]{1,0:T(8,128)(2,1)S(1)} collective-permute-done((bf16[464,512]{1,0:T(8,128)(2,1)S(1)}, bf16[464,512]{1,0:T(8,128)(2,1)S(1)}, u32[]{:S(2)}, u32[]{:S(2)}) %collective-permute-start.31) | collective-permute-done | bytes 475168 | tf_op jit(solution)/shard_map/ppermute | solution.py:266
  115.3 1.0 relay.11
  116.9 8.1 %collective-permute-start.35 = (bf16[400,512]{1,0:T(8,128)(2,1)S(1)}, bf16[400,512]{1,0:T(8,128)(2,1)S(1)}, u32[]{:S(2)}, u32[]{:S(2)}) collective-permute-start(bf16[400,512]{1,0:T(8,128)(2,1)S(1)} %get-tuple-element.243), channel_id=1, source_target_pairs={{0,8},{1,9},{2,10},{3,11},{4,12},{5,13},{6,14},{7,15},{8,0},{9,1},... | collective-permute-start | bytes 1228808 | tf_op jit(solution)/shard_map/ppermute | solution.py:266
  125.0 2.1 %last.9 = (f32[2048,1024]{1,0:T(8,128)}, f32[8,128]{1,0:T(8,128)S(1)}) custom-call(bf16[464,512]{1,0:T(8,128)(2,1)S(1)} %get-tuple-element.232.own, bf16[464,512]{1,0:T(8,128)(2,1)S(1)} %collective-permute-done.31.other.back, bf16[2,256,512]{2,1,0:T(8,128)(2,1)S(1)} %copy-done.4, ...), custom_call_target="tpu_custom_call", output_to_operand_aliasing={{0}: (9, {})} | custom-call | flops 10000000 | bytes 1 | tf_op jit(solution)/shard_map/last/pallas_call | solution.py:235
  127.4 4.2 %collective-permute-start.34 = (bf16[192,512]{1,0:T(8,128)(2,1)S(1)}, bf16[192,512]{1,0:T(8,128)(2,1)S(1)}, u32[]{:S(2)}, u32[]{:S(2)}) collective-permute-start(bf16[192,512]{1,0:T(8,128)(2,1)S(1)} %get-tuple-element.241), channel_id=1, source_target_pairs={{0,8},{1,9},{2,10},{3,11},{4,12},{5,13},{6,14},{7,15},{8,0},{9,1},... | collective-permute-start | bytes 589832 | tf_op jit(solution)/shard_map/ppermute | solution.py:266
  131.8 2.0 %last.10 = (f32[2048,1024]{1,0:T(8,128)}, f32[8,128]{1,0:T(8,128)S(1)}) custom-call(bf16[400,512]{1,0:T(8,128)(2,1)S(1)} %get-tuple-element.242.own, bf16[400,512]{1,0:T(8,128)(2,1)S(1)} %collective-permute-done.35.back, bf16[2,256,512]{2,1,0:T(8,128)(2,1)S(1)} %copy-done.4, bf16[2,768,512]{2,1,0:T(8,128)(2,1)S(1)} %copy-done.2, ...), custom_call_target="tpu_custom_call", output_to_operand_aliasing={{0}: (9, {})} | custom-call | flops 10000000 | bytes 1 | tf_op jit(solution)/shard_map/last/pallas_call | solution.py:235
  133.8 1.8 %collective-permute-done.34.back = bf16[192,512]{1,0:T(8,128)(2,1)S(1)} collective-permute-done((bf16[192,512]{1,0:T(8,128)(2,1)S(1)}, bf16[192,512]{1,0:T(8,128)(2,1)S(1)}, u32[]{:S(2)}, u32[]{:S(2)}) %collective-permute-start.34) | collective-permute-done | bytes 196640 | tf_op jit(solution)/shard_map/ppermute | solution.py:266
  135.6 2.1 %last.11 = (f32[2048,1024]{1,0:T(8,128)}, f32[8,128]{1,0:T(8,128)}) custom-call(bf16[192,512]{1,0:T(8,128)(2,1)S(1)} %get-tuple-element.240.own, bf16[192,512]{1,0:T(8,128)(2,1)S(1)} %collective-permute-done.34.back, bf16[2,256,512]{2,1,0:T(8,128)(2,1)S(1)} %copy-done.4, bf16[2,768,512]{2,1,0:T(8,128)(2,1)S(1)} %copy-done.2, ...), custom_call_target="tpu_custom_call", output_to_operand_aliasing={{0}: (9, {})} | custom-call | flops 10000000 | bytes 1 | tf_op jit(solution)/shard_map/last/pallas_call | solution.py:235
  (84 shorter events, 16.0 us)
Async XLA Ops:
  0.0 5.9 %copy-start.1 = (bf16[6,2,256,256]{3,2,1,0:T(8,128)(2,1)S(1)}, bf16[6,2,256,256]{3,2,1,0:T(8,128)(2,1)}, u32[]{:S(2)}) copy-start(bf16[6,2,256,256]{3,2,1,0:T(8,128)(2,1)} %refs_4_.3) | copy-start | bytes 4718596
  0.0 5.9 %copy-start = (bf16[6,2,256,256]{3,2,1,0:T(8,128)(2,1)S(1)}, bf16[6,2,256,256]{3,2,1,0:T(8,128)(2,1)}, u32[]{:S(2)}) copy-start(bf16[6,2,256,256]{3,2,1,0:T(8,128)(2,1)} %cross.47) | copy-start | bytes 4718596
  0.0 7.8 %slice-start = ((s8[8388608]{0:T(1024)(128)(4,1)}), s8[4194304]{0:T(1024)(128)(4,1)S(1)}, s32[]{:S(2)}) async-start(s8[8388608]{0:T(1024)(128)(4,1)} %bitcast), calls=%async_computation | async-start | bytes 8388608
  0.0 7.8 %slice-start.1 = ((s8[8388608]{0:T(1024)(128)(4,1)}), s8[4194304]{0:T(1024)(128)(4,1)S(1)}, s32[]{:S(2)}) async-start(s8[8388608]{0:T(1024)(128)(4,1)} %bitcast), calls=%async_computation.1 | async-start | bytes 8388608
  2.7 5.2 %copy-start.3 = (bf16[2,512,256]{2,1,0:T(8,128)(2,1)S(1)}, bf16[2,512,256]{2,1,0:T(8,128)(2,1)}, u32[]{:S(2)}) copy-start(bf16[2,512,256]{2,1,0:T(8,128)(2,1)} %leaf.23) | copy-start | bytes 1572868
  2.7 3.2 %collective-permute-start = (bf16[240,512]{1,0:T(8,128)(2,1)S(1)}, bf16[240,512]{1,0:T(8,128)(2,1)S(1)}, u32[]{:S(2)}, u32[]{:S(2)}) collective-permute-start(bf16[240,512]{1,0:T(8,128)(2,1)S(1)} %get-tuple-element.128), channel_id=1, source_target_pairs={{0,1},{1,0},{2,3},{3,2},{4,5},{5,4},{6,7},{7,6},{8,9},{9,8},{10,11... | collective-permute-start | bytes 737288 | tf_op jit(solution)/shard_map/ppermute | solution.py:266
  3.2 33.0 %collective-permute-start.9 = (bf16[4,2,256,256]{3,2,1,0:T(8,128)(2,1)S(1)}, bf16[4,2,256,256]{3,2,1,0:T(8,128)(2,1)S(1)}, u32[]{:S(2)}, u32[]{:S(2)}) collective-permute-start(bf16[4,2,256,256]{3,2,1,0:T(8,128)(2,1)S(1)} %get-tuple-element.154), channel_id=1, source_target_pairs={{0,8},{1,9},{2,10},{3,11},{4,12},{5,13},{6,14},{7,15},{8,0},{9,1},... | collective-permute-start | bytes 3145736 | tf_op jit(solution)/shard_map/ppermute | solution.py:266
  6.3 8.1 %collective-permute-start.2 = (bf16[240,512]{1,0:T(8,128)(2,1)S(1)}, bf16[240,512]{1,0:T(8,128)(2,1)S(1)}, u32[]{:S(2)}, u32[]{:S(2)}) collective-permute-start(bf16[240,512]{1,0:T(8,128)(2,1)S(1)} %get-tuple-element.134), channel_id=1, source_target_pairs={{0,2},{1,3},{2,0},{3,1},{4,6},{5,7},{6,4},{7,5},{8,10},{9,11},{10,... | collective-permute-start | bytes 737288 | tf_op jit(solution)/shard_map/ppermute | solution.py:266
  8.8 7.5 %collective-permute-start.1 = (bf16[336,512]{1,0:T(8,128)(2,1)S(1)}, bf16[336,512]{1,0:T(8,128)(2,1)S(1)}, u32[]{:S(2)}, u32[]{:S(2)}) collective-permute-start(bf16[336,512]{1,0:T(8,128)(2,1)S(1)} %get-tuple-element.132), channel_id=1, source_target_pairs={{0,1},{1,0},{2,3},{3,2},{4,5},{5,4},{6,7},{7,6},{8,9},{9,8},{10,11... | collective-permute-start | bytes 1032200 | tf_op jit(solution)/shard_map/ppermute | solution.py:266
  9.1 10.5 %collective-permute-start.5 = (bf16[2048,128]{1,0:T(8,128)(2,1)S(1)}, bf16[2048,128]{1,0:T(8,128)(2,1)S(1)}, u32[]{:S(2)}, u32[]{:S(2)}) collective-permute-start(bf16[2048,128]{1,0:T(8,128)(2,1)S(1)} %get-tuple-element.142), channel_id=1, source_target_pairs={{0,1},{1,0},{2,3},{3,2},{4,5},{5,4},{6,7},{7,6},{8,9},{9,8},{10,11... | collective-permute-start | bytes 1572872 | tf_op jit(solution)/shard_map/ppermute | solution.py:266
  14.8 7.3 %collective-permute-start.4 = (bf16[240,512]{1,0:T(8,128)(2,1)S(1)}, bf16[240,512]{1,0:T(8,128)(2,1)S(1)}, u32[]{:S(2)}, u32[]{:S(2)}) collective-permute-start(bf16[240,512]{1,0:T(8,128)(2,1)S(1)} %get-tuple-element.141), channel_id=1, source_target_pairs={{0,4},{1,5},{2,6},{3,7},{4,0},{5,1},{6,2},{7,3},{8,12},{9,13},{10,... | collective-permute-start | bytes 737288 | tf_op jit(solution)/shard_map/ppermute | solution.py:266
  16.8 9.1 %collective-permute-start.3 = (bf16[336,512]{1,0:T(8,128)(2,1)S(1)}, bf16[336,512]{1,0:T(8,128)(2,1)S(1)}, u32[]{:S(2)}, u32[]{:S(2)}) collective-permute-start(bf16[336,512]{1,0:T(8,128)(2,1)S(1)} %get-tuple-element.139), channel_id=1, source_target_pairs={{0,2},{1,3},{2,0},{3,1},{4,6},{5,7},{6,4},{7,5},{8,10},{9,11},{10,... | collective-permute-start | bytes 1032200 | tf_op jit(solution)/shard_map/ppermute | solution.py:266
  19.4 7.5 %collective-permute-start.7 = (bf16[416,512]{1,0:T(8,128)(2,1)S(1)}, bf16[416,512]{1,0:T(8,128)(2,1)S(1)}, u32[]{:S(2)}, u32[]{:S(2)}) collective-permute-start(bf16[416,512]{1,0:T(8,128)(2,1)S(1)} %get-tuple-element.149), channel_id=1, source_target_pairs={{0,1},{1,0},{2,3},{3,2},{4,5},{5,4},{6,7},{7,6},{8,9},{9,8},{10,11... | collective-permute-start | bytes 1277960 | tf_op jit(solution)/shard_map/ppermute | solution.py:266
  22.3 13.9 %collective-permute-start.10 = (bf16[240,512]{1,0:T(8,128)(2,1)S(1)}, bf16[240,512]{1,0:T(8,128)(2,1)S(1)}, u32[]{:S(2)}, u32[]{:S(2)}) collective-permute-start(bf16[240,512]{1,0:T(8,128)(2,1)S(1)} %get-tuple-element.155.own), channel_id=1, source_target_pairs={{0,8},{1,9},{2,10},{3,11},{4,12},{5,13},{6,14},{7,15},{8,0},{9,1},... | collective-permute-start | bytes 737288 | tf_op jit(solution)/shard_map/ppermute | solution.py:266
  26.3 8.2 %collective-permute-start.6 = (bf16[336,512]{1,0:T(8,128)(2,1)S(1)}, bf16[336,512]{1,0:T(8,128)(2,1)S(1)}, u32[]{:S(2)}, u32[]{:S(2)}) collective-permute-start(bf16[336,512]{1,0:T(8,128)(2,1)S(1)} %get-tuple-element.147), channel_id=1, source_target_pairs={{0,4},{1,5},{2,6},{3,7},{4,0},{5,1},{6,2},{7,3},{8,12},{9,13},{10,... | collective-permute-start | bytes 1032200 | tf_op jit(solution)/shard_map/ppermute | solution.py:266
  27.4 11.7 %collective-permute-start.13 = (bf16[416,512]{1,0:T(8,128)(2,1)S(1)}, bf16[416,512]{1,0:T(8,128)(2,1)S(1)}, u32[]{:S(2)}, u32[]{:S(2)}) collective-permute-start(bf16[416,512]{1,0:T(8,128)(2,1)S(1)} %get-tuple-element.162), channel_id=1, source_target_pairs={{0,2},{1,3},{2,0},{3,1},{4,6},{5,7},{6,4},{7,5},{8,10},{9,11},{10,... | collective-permute-start | bytes 1277960 | tf_op jit(solution)/shard_map/ppermute | solution.py:266
  29.1 11.4 %collective-permute-start.12 = (bf16[2048,128]{1,0:T(8,128)(2,1)S(1)}, bf16[2048,128]{1,0:T(8,128)(2,1)S(1)}, u32[]{:S(2)}, u32[]{:S(2)}) collective-permute-start(bf16[2048,128]{1,0:T(8,128)(2,1)S(1)} %get-tuple-element.160), channel_id=1, source_target_pairs={{15,16},{16,15}} | collective-permute-start | bytes 1572872 | tf_op jit(solution)/shard_map/ppermute | solution.py:266
  34.8 7.9 %collective-permute-start.8 = (bf16[336,512]{1,0:T(8,128)(2,1)S(1)}, bf16[336,512]{1,0:T(8,128)(2,1)S(1)}, u32[]{:S(2)}, u32[]{:S(2)}) collective-permute-start(bf16[336,512]{1,0:T(8,128)(2,1)S(1)} %get-tuple-element.153.own), channel_id=1, source_target_pairs={{0,8},{1,9},{2,10},{3,11},{4,12},{5,13},{6,14},{7,15},{8,0},{9,1},... | collective-permute-start | bytes 1032200 | tf_op jit(solution)/shard_map/ppermute | solution.py:266
  37.3 8.4 %collective-permute-start.17 = (bf16[240,1024]{1,0:T(8,128)(2,1)S(1)}, bf16[240,1024]{1,0:T(8,128)(2,1)S(1)}, u32[]{:S(2)}, u32[]{:S(2)}) collective-permute-start(bf16[240,1024]{1,0:T(8,128)(2,1)S(1)} %get-tuple-element.175), channel_id=1, source_target_pairs={{0,1},{1,0},{2,3},{3,2},{4,5},{5,4},{6,7},{7,6},{8,16},{9,17},{10,... | collective-permute-start | bytes 1474568 | tf_op jit(solution)/shard_map/ppermute | solution.py:266
  38.6 2.0 %collective-permute-start.11 = (bf16[464,512]{1,0:T(8,128)(2,1)S(1)}, bf16[464,512]{1,0:T(8,128)(2,1)S(1)}, u32[]{:S(2)}, u32[]{:S(2)}) collective-permute-start(bf16[464,512]{1,0:T(8,128)(2,1)S(1)} %get-tuple-element.159), channel_id=1, source_target_pairs={{0,1},{1,0},{2,3},{3,2},{4,5},{5,4},{6,7},{7,6},{8,9},{9,8},{10,11... | collective-permute-start | bytes 1425416 | tf_op jit(solution)/shard_map/ppermute | solution.py:266
  39.6 11.8 %collective-permute-start.16 = (bf16[416,512]{1,0:T(8,128)(2,1)S(1)}, bf16[416,512]{1,0:T(8,128)(2,1)S(1)}, u32[]{:S(2)}, u32[]{:S(2)}) collective-permute-start(bf16[416,512]{1,0:T(8,128)(2,1)S(1)} %get-tuple-element.172), channel_id=1, source_target_pairs={{0,4},{1,5},{2,6},{3,7},{4,0},{5,1},{6,2},{7,3},{8,12},{9,13},{10,... | collective-permute-start | bytes 1277960 | tf_op jit(solution)/shard_map/ppermute | solution.py:266
  41.1 13.9 %collective-permute-start.15 = (bf16[464,512]{1,0:T(8,128)(2,1)S(1)}, bf16[464,512]{1,0:T(8,128)(2,1)S(1)}, u32[]{:S(2)}, u32[]{:S(2)}) collective-permute-start(bf16[464,512]{1,0:T(8,128)(2,1)S(1)} %get-tuple-element.170), channel_id=1, source_target_pairs={{0,2},{1,3},{2,0},{3,1},{4,6},{5,7},{6,4},{7,5},{8,10},{9,11},{10,... | collective-permute-start | bytes 1425416 | tf_op jit(solution)/shard_map/ppermute | solution.py:266
  44.0 20.9 %collective-permute-start.21 = (bf16[336,1024]{1,0:T(8,128)(2,1)S(1)}, bf16[336,1024]{1,0:T(8,128)(2,1)S(1)}, u32[]{:S(2)}, u32[]{:S(2)}) collective-permute-start(bf16[336,1024]{1,0:T(8,128)(2,1)S(1)} %get-tuple-element.188), channel_id=1, source_target_pairs={{0,1},{1,0},{2,3},{3,2},{4,5},{5,4},{6,7},{7,6},{8,16},{9,17},{10,... | collective-permute-start | bytes 2064392 | tf_op jit(solution)/shard_map/ppermute | solution.py:266
  45.2 11.3 %collective-permute-start.14 = (bf16[400,512]{1,0:T(8,128)(2,1)S(1)}, bf16[400,512]{1,0:T(8,128)(2,1)S(1)}, u32[]{:S(2)}, u32[]{:S(2)}) collective-permute-start(bf16[400,512]{1,0:T(8,128)(2,1)S(1)} %get-tuple-element.168), channel_id=1, source_target_pairs={{0,1},{1,0},{2,3},{3,2},{4,5},{5,4},{6,7},{7,6},{8,9},{9,8},{10,11... | collective-permute-start | bytes 1228808 | tf_op jit(solution)/shard_map/ppermute | solution.py:266
  51.8 11.5 %collective-permute-start.22 = (bf16[416,512]{1,0:T(8,128)(2,1)S(1)}, bf16[416,512]{1,0:T(8,128)(2,1)S(1)}, u32[]{:S(2)}, u32[]{:S(2)}) collective-permute-start(bf16[416,512]{1,0:T(8,128)(2,1)S(1)} %get-tuple-element.190), channel_id=1, source_target_pairs={{0,8},{1,9},{2,10},{3,11},{4,12},{5,13},{6,14},{7,15},{8,0},{9,1},... | collective-permute-start | bytes 1277960 | tf_op jit(solution)/shard_map/ppermute | solution.py:266
  55.5 11.7 %collective-permute-start.20 = (bf16[464,512]{1,0:T(8,128)(2,1)S(1)}, bf16[464,512]{1,0:T(8,128)(2,1)S(1)}, u32[]{:S(2)}, u32[]{:S(2)}) collective-permute-start(bf16[464,512]{1,0:T(8,128)(2,1)S(1)} %get-tuple-element.185), channel_id=1, source_target_pairs={{0,4},{1,5},{2,6},{3,7},{4,0},{5,1},{6,2},{7,3},{8,12},{9,13},{10,... | collective-permute-start | bytes 1425416 | tf_op jit(solution)/shard_map/ppermute | solution.py:266
  57.0 10.8 %collective-permute-start.19 = (bf16[400,512]{1,0:T(8,128)(2,1)S(1)}, bf16[400,512]{1,0:T(8,128)(2,1)S(1)}, u32[]{:S(2)}, u32[]{:S(2)}) collective-permute-start(bf16[400,512]{1,0:T(8,128)(2,1)S(1)} %get-tuple-element.183), channel_id=1, source_target_pairs={{0,2},{1,3},{2,0},{3,1},{4,6},{5,7},{6,4},{7,5},{8,10},{9,11},{10,... | collective-permute-start | bytes 1228808 | tf_op jit(solution)/shard_map/ppermute | solution.py:266
  59.3 11.3 %collective-permute-start.18 = (bf16[192,512]{1,0:T(8,128)(2,1)S(1)}, bf16[192,512]{1,0:T(8,128)(2,1)S(1)}, u32[]{:S(2)}, u32[]{:S(2)}) collective-permute-start(bf16[192,512]{1,0:T(8,128)(2,1)S(1)} %get-tuple-element.181), channel_id=1, source_target_pairs={{0,1},{1,0},{2,3},{3,2},{4,5},{5,4},{6,7},{7,6},{8,9},{9,8},{10,11... | collective-permute-start | bytes 589832 | tf_op jit(solution)/shard_map/ppermute | solution.py:266
  64.8 17.7 %collective-permute-start.27 = (bf16[416,1024]{1,0:T(8,128)(2,1)S(1)}, bf16[416,1024]{1,0:T(8,128)(2,1)S(1)}, u32[]{:S(2)}, u32[]{:S(2)}) collective-permute-start(bf16[416,1024]{1,0:T(8,128)(2,1)S(1)} %get-tuple-element.206), channel_id=1, source_target_pairs={{0,1},{1,0},{2,3},{3,2},{4,5},{5,4},{6,7},{7,6},{8,16},{9,17},{10,... | collective-permute-start | bytes 2555912 | tf_op jit(solution)/shard_map/ppermute | solution.py:266
  68.2 14.3 %collective-permute-start.26 = (bf16[400,512]{1,0:T(8,128)(2,1)S(1)}, bf16[400,512]{1,0:T(8,128)(2,1)S(1)}, u32[]{:S(2)}, u32[]{:S(2)}) collective-permute-start(bf16[400,512]{1,0:T(8,128)(2,1)S(1)} %get-tuple-element.203), channel_id=1, source_target_pairs={{0,4},{1,5},{2,6},{3,7},{4,0},{5,1},{6,2},{7,3},{8,12},{9,13},{10,... | collective-permute-start | bytes 1228808 | tf_op jit(solution)/shard_map/ppermute | solution.py:266
  69.3 11.5 %collective-permute-start.24 = (bf16[464,512]{1,0:T(8,128)(2,1)S(1)}, bf16[464,512]{1,0:T(8,128)(2,1)S(1)}, u32[]{:S(2)}, u32[]{:S(2)}) collective-permute-start(bf16[464,512]{1,0:T(8,128)(2,1)S(1)} %get-tuple-element.198), channel_id=1, source_target_pairs={{0,8},{1,9},{2,10},{3,11},{4,12},{5,13},{6,14},{7,15},{8,0},{9,1},... | collective-permute-start | bytes 1425416 | tf_op jit(solution)/shard_map/ppermute | solution.py:266
  71.1 15.7 %collective-permute-start.25 = (bf16[2048,128]{1,0:T(8,128)(2,1)S(1)}, bf16[2048,128]{1,0:T(8,128)(2,1)S(1)}, u32[]{:S(2)}, u32[]{:S(2)}) collective-permute-start(bf16[2048,128]{1,0:T(8,128)(2,1)S(1)} %get-tuple-element.200), channel_id=1, source_target_pairs={{1,2},{2,1},{3,4},{4,3},{5,6},{6,5},{7,8},{8,7},{9,10},{10,9},{11,... | collective-permute-start | bytes 1572872 | tf_op jit(solution)/shard_map/ppermute | solution.py:266
  72.1 18.2 %collective-permute-start.23 = (bf16[192,512]{1,0:T(8,128)(2,1)S(1)}, bf16[192,512]{1,0:T(8,128)(2,1)S(1)}, u32[]{:S(2)}, u32[]{:S(2)}) collective-permute-start(bf16[192,512]{1,0:T(8,128)(2,1)S(1)} %get-tuple-element.196), channel_id=1, source_target_pairs={{0,2},{1,3},{2,0},{3,1},{4,6},{5,7},{6,4},{7,5},{8,10},{9,11},{10,... | collective-permute-start | bytes 589832 | tf_op jit(solution)/shard_map/ppermute | solution.py:266
  82.4 16.3 %collective-permute-start.29 = (bf16[464,1024]{1,0:T(8,128)(2,1)S(1)}, bf16[464,1024]{1,0:T(8,128)(2,1)S(1)}, u32[]{:S(2)}, u32[]{:S(2)}) collective-permute-start(bf16[464,1024]{1,0:T(8,128)(2,1)S(1)} %get-tuple-element.218), channel_id=1, source_target_pairs={{0,1},{1,0},{2,3},{3,2},{4,5},{5,4},{6,7},{7,6},{8,16},{9,17},{10,... | collective-permute-start | bytes 2850824 | tf_op jit(solution)/shard_map/ppermute | solution.py:266
  82.5 4.3 %copy-start.2 = (bf16[2,768,512]{2,1,0:T(8,128)(2,1)S(1)}, bf16[2,768,512]{2,1,0:T(8,128)(2,1)}, u32[]{:S(2)}) copy-start(bf16[2,768,512]{2,1,0:T(8,128)(2,1)} %near.11) | copy-start | bytes 4718596
  82.5 4.3 %copy-start.4 = (bf16[2,256,512]{2,1,0:T(8,128)(2,1)S(1)}, bf16[2,256,512]{2,1,0:T(8,128)(2,1)}, u32[]{:S(2)}) copy-start(bf16[2,256,512]{2,1,0:T(8,128)(2,1)} %out_basis.11) | copy-start | bytes 1572868
  83.1 12.5 %collective-permute-start.30 = (bf16[416,512]{1,0:T(8,128)(2,1)S(1)}, bf16[416,512]{1,0:T(8,128)(2,1)S(1)}, u32[]{:S(2)}, u32[]{:S(2)}) collective-permute-start(bf16[416,512]{1,0:T(8,128)(2,1)S(1)} %get-tuple-element.220), channel_id=1, source_target_pairs={{0,8},{1,9},{2,10},{3,11},{4,12},{5,13},{6,14},{7,15},{8,0},{9,1},... | collective-permute-start | bytes 1277960 | tf_op jit(solution)/shard_map/ppermute | solution.py:266
  90.7 8.0 %collective-permute-start.28 = (bf16[192,512]{1,0:T(8,128)(2,1)S(1)}, bf16[192,512]{1,0:T(8,128)(2,1)S(1)}, u32[]{:S(2)}, u32[]{:S(2)}) collective-permute-start(bf16[192,512]{1,0:T(8,128)(2,1)S(1)} %get-tuple-element.215), channel_id=1, source_target_pairs={{0,4},{1,5},{2,6},{3,7},{4,0},{5,1},{6,2},{7,3},{8,12},{9,13},{10,... | collective-permute-start | bytes 589832 | tf_op jit(solution)/shard_map/ppermute | solution.py:266
  97.1 19.4 %collective-permute-start.33 = (bf16[400,1024]{1,0:T(8,128)(2,1)S(1)}, bf16[400,1024]{1,0:T(8,128)(2,1)S(1)}, u32[]{:S(2)}, u32[]{:S(2)}) collective-permute-start(bf16[400,1024]{1,0:T(8,128)(2,1)S(1)} %get-tuple-element.235), channel_id=1, source_target_pairs={{0,1},{1,0},{2,3},{3,2},{4,5},{5,4},{6,7},{7,6},{8,16},{9,17},{10,... | collective-permute-start | bytes 2457608 | tf_op jit(solution)/shard_map/ppermute | solution.py:266
  99.2 16.2 %collective-permute-start.31 = (bf16[464,512]{1,0:T(8,128)(2,1)S(1)}, bf16[464,512]{1,0:T(8,128)(2,1)S(1)}, u32[]{:S(2)}, u32[]{:S(2)}) collective-permute-start(bf16[464,512]{1,0:T(8,128)(2,1)S(1)} %get-tuple-element.224), channel_id=1, source_target_pairs={{0,8},{1,9},{2,10},{3,11},{4,12},{5,13},{6,14},{7,15},{8,0},{9,1},... | collective-permute-start | bytes 1425416 | tf_op jit(solution)/shard_map/ppermute | solution.py:266
  116.4 10.7 %collective-permute-start.32 = (bf16[192,1024]{1,0:T(8,128)(2,1)S(1)}, bf16[192,1024]{1,0:T(8,128)(2,1)S(1)}, u32[]{:S(2)}, u32[]{:S(2)}) collective-permute-start(bf16[192,1024]{1,0:T(8,128)(2,1)S(1)} %get-tuple-element.231), channel_id=1, source_target_pairs={{0,1},{1,0},{2,3},{3,2},{4,5},{5,4},{6,7},{7,6},{8,16},{9,17},{10,... | collective-permute-start | bytes 1179656 | tf_op jit(solution)/shard_map/ppermute | solution.py:266
  116.9 15.0 %collective-permute-start.35 = (bf16[400,512]{1,0:T(8,128)(2,1)S(1)}, bf16[400,512]{1,0:T(8,128)(2,1)S(1)}, u32[]{:S(2)}, u32[]{:S(2)}) collective-permute-start(bf16[400,512]{1,0:T(8,128)(2,1)S(1)} %get-tuple-element.243), channel_id=1, source_target_pairs={{0,8},{1,9},{2,10},{3,11},{4,12},{5,13},{6,14},{7,15},{8,0},{9,1},... | collective-permute-start | bytes 1228808 | tf_op jit(solution)/shard_map/ppermute | solution.py:266
  127.4 8.2 %collective-permute-start.34 = (bf16[192,512]{1,0:T(8,128)(2,1)S(1)}, bf16[192,512]{1,0:T(8,128)(2,1)S(1)}, u32[]{:S(2)}, u32[]{:S(2)}) collective-permute-start(bf16[192,512]{1,0:T(8,128)(2,1)S(1)} %get-tuple-element.241), channel_id=1, source_target_pairs={{0,8},{1,9},{2,10},{3,11},{4,12},{5,13},{6,14},{7,15},{8,0},{9,1},... | collective-permute-start | bytes 589832 | tf_op jit(solution)/shard_map/ppermute | solution.py:266
